TPU v7x, 32 devices: a whole 2x2x4 slice. The times are simulated.
32 devices in a mesh: lat: 8 (over z, core), lon: 4 (over y, x).
Axes of the slice: x: 2, y: 2, z: 4, core: 2. Of those that a mesh axis runs over, the one named last changes fastest.
Arguments:
- winds: float32 [2, 16, 720, 2880], P(None, None, 'lat', 'lon'), may hold values from -6 to 6
- theta: float32 [16, 720, 2880], P(None, 'lat', 'lon'), may hold values from -6 to 6
- thick: float32 [16, 720, 2880], P(None, 'lat', 'lon'), may hold values from 0.5 to 1.5
- polar_rows: int32 [240], replicated, may hold values from 0 to 719, as said below
- cutoffs: int32 [240], replicated, may hold values from 1 to 719, as said below
Outputs:
- new_winds: float32 [2, 16, 720, 2880], P(None, None, 'lat', 'lon')
- new_theta: float32 [16, 720, 2880], P(None, 'lat', 'lon')
- new_thick: float32 [16, 720, 2880], P(None, 'lat', 'lon')
Inputs may be any that keep to these rules, and one draw needn't show every extreme that they name: `polar_rows`: each row is listed once, in an order drawn from the seed. The listed rows are a run of rows from row 0 up together with a run of rows ending at row 719; each run has between 90 and 150 rows, so no row of the middle half of the latitudes is listed. `cutoffs`: rows 0 and 719 have cutoff 1, and the listed row of each run that lies farthest from its pole has cutoff 720 - 1. Any other listed row that lies d rows from its nearest pole (d = 0 at the pole) has a cutoff between min(d + 1, 719) and min(2 (d + 1), 719).
All inputs are finite; a program needn't handle non-finite values.
Results may differ from a plain program's by a relative error of at most 0.000071.
Values sent between devices are 32-bit elements; how exact they have to be, the bound alone decides.
No kernel may reach another device: no remote copies, remote signals or barrier semaphores. Data moves between devices by JAX's collectives and lax.ppermute only.
A program may use at most 192 MiB of HBM per device.

v0:
```python
import functools

import jax
import jax.numpy as jnp
import ml_dtypes
import numpy as np
from jax import lax
from jax.experimental import pallas as pl
from jax.experimental.pallas import tpu as pltpu
from jax.sharding import PartitionSpec as P

FIELDS = 4
LANES = 128
PIECE = 3
VMEM = 60 * 1024 * 1024


def round_up(value, step):
    return -(-value // step) * step


class Group:
    def __init__(self, first, stop, near, far, blocks, levels, quarters):
        self.first, self.stop, self.blocks, self.levels = first, stop, blocks, levels
        self.near, self.far = int(near), int(far)
        self.own = stop - first
        self.farthest = self.own == 0
        self.slots = 1 if self.farthest else self.own + self.near + self.far
        self.height = self.slots * levels
        self.quarters = list(quarters)
        assert sum(self.quarters) == self.slots
        one, two, three, four = self.quarters
        self.beside = max(one, three) if one and three else 0
        self.half = -(-two // 2)
        self.packed = self.beside > 0 or two > 1
        self.pieces = []
        if self.packed:
            if not self.beside:
                for start, count in ((0, one), (one + two, three)):
                    if count:
                        self.pieces.append((0, start, count))
            if four:
                self.pieces.append((0, one + two + three, four))
        self.whole_rows = sum(piece[2] for piece in self.pieces)
        self.full = self.height * (blocks - 1 if self.packed else blocks)
        self.packed_rows = (self.whole_rows + self.beside + self.half) * levels if self.packed else 0
        self.total = self.full + self.packed_rows
        parts = max(1, round(self.slots / 16))
        self.chunk = -(-self.slots // parts)
        self.parts = -(-self.slots // self.chunk)

    def start(self, hemi, rows):
        return jnp.where(hemi == 1, rows - self.stop + 1 - self.far, self.first + 1 - self.near)

    def chunk_at(self, part):
        return jnp.minimum(part * self.chunk, self.slots - self.chunk)

    def slot(self, hemi, first, count):
        first = min(first, self.slots - count)
        return jnp.where(hemi == 1, self.slots - count - first, first)

    def pairs(self):
        one, two, three, _ = self.quarters
        result = []
        if self.beside:
            result.append((one + two, 0, self.beside, 96))
        if two:
            result.append((one, one + two - self.half, self.half, 64))
        return result

    def pack(self, hemi, last, to):
        row = 0
        for _, first, count in self.pieces:
            to(row, count, last(self.slot(hemi, first, count), count))
            row += count
        for left, right, count, lanes in self.pairs():
            lane = lax.broadcasted_iota(jnp.int32, (count * self.levels, LANES), 1)
            beside = pltpu.roll(last(self.slot(hemi, right, count), count), lanes, 1)
            to(row, count, jnp.where(lane < lanes, last(self.slot(hemi, left, count), count), beside))
            row += count

    def unpack(self, hemi, packed, to):
        row = self.whole_rows
        for left, right, count, lanes in self.pairs():
            value = packed(row, count)
            to(self.slot(hemi, left, count), count, value)
            to(self.slot(hemi, right, count), count, pltpu.roll(value, LANES - lanes, 1))
            row += count
        row = 0
        for _, first, count in self.pieces:
            to(self.slot(hemi, first, count), count, packed(row, count))
            row += count


class Plan:
    def __init__(self, lat, lon, levels, rows, width, listed):
        self.lat, self.lon, self.levels, self.rows, self.width = lat, lon, levels, rows, width
        self.total_rows, self.length = lat * rows, lon * width
        self.parts = lon // FIELDS
        self.wide = round_up(width + 2, LANES)
        pole = listed // 2
        self.low, self.high = pole - pole // 4, pole + pole // 4
        top = self.length // 4 - 1

        def blocks_of(depth):
            return -(-(2 * min(2 * (depth + 1), top) + 1) // LANES)

        self.roles = []
        last = self.high - 2
        for role in range(lat // 2):
            start = role * rows
            if start > last:
                break
            need = {}
            for depth in range(start, min(start + rows - 1, last) + 1):
                need.setdefault(blocks_of(depth), []).append(depth - start)
            spans = [[need[k][0], need[k][-1] + 1, False, False, k] for k in sorted(need)]
            if role > 0:
                spans[0][2], spans[0][4] = True, max(spans[0][4], blocks_of(start - 1))
            if start + rows <= last:
                spans[-1][3], spans[-1][4] = True, max(spans[-1][4], blocks_of(start + rows))
            groups = []
            for first, stop, near, far, blocks in spans:
                depths = range(start + first - int(near), start + stop + int(far))
                quarters = [0] * 4
                for depth in depths:
                    lanes = 2 * min(2 * (depth + 1), top) + 1 - (blocks - 1) * LANES
                    quarters[max(0, -(-lanes // (LANES // 4)) - 1)] += 1
                groups.append(Group(first, stop, near, far, blocks, levels, quarters))
            groups.append(Group(0, 0, False, False, -(-(2 * top + 1) // LANES), levels, (0, 0, 0, 1)))
            self.roles.append(groups)
        self.slots = max(sum(group.slots for group in groups) for groups in self.roles)
        self.table = LANES * max(group.blocks for groups in self.roles for group in groups)
        count = len(self.roles)
        self.lent = {}
        if self.parts == 1 and 2 * count <= lat // 2:
            self.lent = {count - 1: len(self.roles[-1]) - 2}

    def blocks(self, role):
        return (role, self.lat - 1 - role)

    def parcels(self, at):
        indices = range(len(self.roles[at]))
        away = self.lent.get(at)
        home = [g for g in indices if g != away]
        return [home] if away is None else [home, [away]]

    def arrays(self):
        calls = [[], []]
        for at in range(len(self.roles)):
            if at in self.lent:
                calls[0] += [(at, 1, 0), (at, 1, 1)]
                calls[1] += [(at, 0, 0), (at, 0, 1)]
            else:
                calls[0].append((at, 0, 0))
                calls[1].append((at, 0, 1))
        return calls

    def places(self):
        result, number = {}, 0
        for at in range(len(self.roles)):
            for parcel in self.parcels(at):
                offset = 0
                for g in parcel:
                    result[at, g] = (number, offset)
                    offset += self.roles[at][g].total
                number += 1
        return result

    def height_of(self, at, parcel):
        return sum(self.roles[at][g].total for g in self.parcels(at)[parcel])

    def heights(self):
        return [
            self.height_of(at, parcel) for at in range(len(self.roles)) for parcel in range(len(self.parcels(at)))
        ]

    def slot_rows(self):
        table = np.full((len(self.roles), 2, self.slots), -1, np.int32)
        for at, groups in enumerate(self.roles):
            for hemi in range(2):
                rows = []
                for group in groups:
                    first = group.first + 1 - group.near if hemi == 0 else self.rows - group.stop + 1 - group.far
                    rows += [-2] if group.farthest else [first + k for k in range(group.slots)]
                table[at, hemi, : len(rows)] = rows
        return table


def split_table(table):
    high = table.astype(ml_dtypes.bfloat16)
    low = (table - high.astype(np.float64)).astype(ml_dtypes.bfloat16)
    return high, low


@functools.lru_cache(maxsize=None)
def tables(sizes):
    plan = Plan(*sizes)
    index = np.arange(plan.table)
    wave, odd = (index + 1) // 2, (index % 2 == 0) & (index > 0)
    used = wave < plan.length // 4
    points = np.zeros(plan.wide, np.int64)
    points[: plan.width + 1] = np.arange(plan.width + 1)
    points[-1] = -1
    shown = np.zeros(plan.wide, bool)
    shown[: plan.width + 1] = True
    shown[-1] = True

    def trig(at):
        angle = (wave[:, None] * at[None, :]) % plan.length * (2.0 * np.pi / plan.length)
        return np.where(odd[:, None], np.sin(angle), np.cos(angle)) * used[:, None]

    weight = np.where(wave == 0, 1.0, 2.0) / plan.length
    forward, inverse = [], []
    for place in range(plan.lon):
        forward.append(trig(place * plan.width + np.arange(plan.width)).T)
        inverse.append(trig(place * plan.width + points) * weight[:, None] * shown[None, :])
    shape = (plan.lon, plan.width, plan.table // LANES, LANES)
    forward = np.stack(forward).reshape(shape).transpose(0, 2, 1, 3)
    inverse = np.stack(inverse).reshape(plan.lon, plan.table // LANES, LANES, plan.wide)
    return split_table(forward), split_table(inverse)


def fetch_table(place, tabs, held, sems, blocks):
    return [
        pltpu.make_async_copy(tab.at[place, b], held.at[b, k], sems.at[b, k])
        for b in blocks
        for k, tab in enumerate(tabs)
    ]


def split(value):
    high = value.astype(jnp.bfloat16)
    low = (value - high.astype(jnp.float32)).astype(jnp.bfloat16)
    return high, low


def dot(left, right):
    return jnp.dot(left, right, preferred_element_type=jnp.float32)


def three_pass_out(left, right):
    columns = right[0].shape[1]
    both = dot(left[0], jnp.concatenate(right, axis=1))
    return both[:, :columns] + (both[:, columns:] + dot(left[1], right[0]))


def three_pass_in(value, table):
    terms = []
    for at in range(0, value.shape[1], LANES):
        high, low = split(value[:, at : at + LANES])
        terms += [high, low, high]
    return dot(jnp.concatenate(terms, axis=1), table)


def forward_kernel(plan, call, scal, winds, theta, thick, top, bottom, t_high, t_low, *refs):
    places, sets, arrays = plan.places(), field_sets(plan), plan.arrays()[call]
    outs, (points, spectra, held, in_sems, out_sems, t_sems) = refs[: len(arrays)], refs[len(arrays) :]
    levels, width = plan.levels, plan.width
    hemi = scal[3]
    for at, groups in enumerate(plan.roles):

        @pl.when(scal[2] == at)
        def _(at=at, groups=groups):
            mine = [(number, array[1:]) for number, array in enumerate(arrays) if array[0] == at]
            order = [g for g in range(len(groups)) if any(g in plan.parcels(at)[a[0]] for _, a in mine)]
            targets = {}
            for g in order:
                targets[g] = [
                    (number, i, u)
                    for number, (parcel, which) in mine
                    if g in plan.parcels(at)[parcel]
                    for i, u in enumerate(sets[which][at])
                ]
            some_fields = {g: [u ^ scal[0] for _, _, u in targets[g]] for g in order}
            turn_of = {g: n % 2 for n, g in enumerate(order)}
            ready = 0

            def first_row(group):
                if group.farthest:
                    return jnp.clip(scal[4] - 1, 0, plan.rows - 1), 0, 1
                first = jnp.where(hemi == 1, plan.rows - group.stop, group.first)
                return first, jnp.where(hemi == 1, group.far, group.near), group.own

            def fetch(g):
                first, slot, count = first_row(groups[g])
                for i, field in enumerate(some_fields[g]):

                    def pieces(source, i=i):
                        for k in range(0, count, PIECE):
                            size = min(PIECE, count - k)
                            pltpu.make_async_copy(
                                source.at[pl.ds(first + k, size)],
                                points.at[turn_of[g], i, pl.ds(slot + k, size)],
                                in_sems.at[turn_of[g], i],
                            ).start()

                    pl.when(field < 2)(lambda: pieces(winds.at[jnp.minimum(field, 1)]))
                    pl.when(field == 2)(lambda: pieces(theta))
                    pl.when(field == 3)(lambda: pieces(thick))

            def arrive(g):
                first, slot, count = first_row(groups[g])
                for i in range(len(targets[g])):
                    pltpu.make_async_copy(
                        theta.at[pl.ds(first, count)],
                        points.at[turn_of[g], i, pl.ds(slot, count)],
                        in_sems.at[turn_of[g], i],
                    ).wait()

            def leave(g, parts):
                group, turn, copies = groups[g], turn_of[g], []
                _, offset = places[at, g]
                size = group.full // parts
                for i, (number, place, _) in enumerate(targets[g]):
                    for k in range(parts if group.full else 0):
                        copies.append(
                            pltpu.make_async_copy(
                                spectra.at[turn, i, pl.ds(k * size, size)],
                                outs[number].at[place, pl.ds(offset + k * size, size)],
                                out_sems.at[turn, i, 0],
                            )
                        )
                    if group.packed:
                        copies.append(
                            pltpu.make_async_copy(
                                spectra.at[turn, i, pl.ds(group.blocks * group.height, group.packed_rows)],
                                outs[number].at[place, pl.ds(offset + group.full, group.packed_rows)],
                                out_sems.at[turn, i, 1],
                            )
                        )
                return copies

            def pack(g, i):
                group, turn = groups[g], turn_of[g]

                def last(slot, count):
                    at_row = pl.multiple_of((group.blocks - 1) * group.height + slot * levels, 8)
                    return spectra[turn, i, pl.ds(at_row, count * levels), :]

                def to(row, count, value):
                    at_row = group.blocks * group.height + row * levels
                    spectra[turn, i, at_row : at_row + count * levels, :] = value

                group.pack(hemi, last, to)

            def halo(g, slot, line, wanted):
                @pl.when(wanted)
                def _():
                    for i, field in enumerate(some_fields[g]):
                        points[turn_of[g], i, slot] = line[field]

            fetch(order[0])
            needed = range(max(groups[g].blocks for g in order))
            for copy in fetch_table(scal[1], (t_high, t_low), held, t_sems, needed):
                copy.start()
            for n, g in enumerate(order):
                group = groups[g]
                if n + 1 < len(order):
                    fetch(order[n + 1])
                arrive(g)
                for copy in fetch_table(scal[1], (t_high, t_low), held, t_sems, range(ready, group.blocks)):
                    copy.wait()
                ready = max(ready, group.blocks)
                if group.farthest:
                    halo(g, 0, top, scal[4] == 0)
                    halo(g, 0, bottom, scal[4] == plan.rows + 1)
                if group.near:
                    halo(g, 0, top, hemi == 0)
                    halo(g, group.slots - 1, bottom, hemi == 1)
                if group.far:
                    halo(g, group.slots - 1, bottom, hemi == 0)
                    halo(g, 0, top, hemi == 1)
                if n >= 2:
                    for copy in leave(order[n - 2], 1):
                        copy.wait()

                def transform(value, group=group):
                    return three_pass_out(
                        split(value),
                        [
                            jnp.concatenate([held[b, half] for b in range(group.blocks)], axis=1)
                            for half in range(2)
                        ],
                    )

                if group.farthest:
                    spec = transform(points[turn_of[g], : len(targets[g]), 0].reshape(len(targets[g]) * levels, width))
                    for i in range(len(targets[g])):
                        for b in range(group.blocks):
                            spectra[turn_of[g], i, b * levels : (b + 1) * levels, :] = spec[
                                i * levels : (i + 1) * levels, b * LANES : (b + 1) * LANES
                            ]
                else:

                    def part(n, _, g=g, group=group, transform=transform):
                        i, slot = n // group.parts, group.chunk_at(lax.rem(n, group.parts))
                        size = group.chunk * levels
                        spec = transform(points[turn_of[g], i, pl.ds(slot, group.chunk)].reshape(size, width))
                        for b in range(group.blocks):
                            target = pl.multiple_of(b * group.height + slot * levels, 8)
                            spectra[turn_of[g], i, pl.ds(target, size), :] = spec[:, b * LANES : (b + 1) * LANES]
                        return 0

                    lax.fori_loop(0, len(targets[g]) * group.parts, part, 0)
                if group.packed:
                    lax.fori_loop(0, len(targets[g]), lambda i, _, g=g: (pack(g, i), 0)[1], 0)
                for copy in leave(g, max(1, group.full // group.height)):
                    copy.start()
            for g in order[-2:]:
                for copy in leave(g, 1):
                    copy.wait()


def forward(plan, call, scal, winds, theta, thick, top, bottom, tabs):
    arrays = plan.arrays()[call]
    count = FIELDS if plan.lent else FIELDS // 2
    shapes = [(FIELDS // 2, plan.height_of(at, parcel), LANES) for at, parcel, _ in arrays]
    anywhere = pl.BlockSpec(memory_space=pl.ANY)
    halo = pl.BlockSpec((FIELDS, plan.levels, plan.width), lambda i, s: (0, 0, 0))
    slots = max(group.slots for groups in plan.roles for group in groups)
    total = max(group.height * group.blocks + group.packed_rows for groups in plan.roles for group in groups)
    outs = pl.pallas_call(
        functools.partial(forward_kernel, plan, call),
        grid_spec=pltpu.PrefetchScalarGridSpec(
            num_scalar_prefetch=1,
            grid=(1,),
            in_specs=[anywhere] * 3 + [halo, halo, anywhere, anywhere],
            out_specs=[anywhere] * len(arrays),
            scratch_shapes=[
                pltpu.VMEM((2, count, slots, plan.levels, plan.width), jnp.float32),
                pltpu.VMEM((2, count, total, LANES), jnp.float32),
                pltpu.VMEM((plan.table // LANES, 2, plan.width, LANES), jnp.bfloat16),
                pltpu.SemaphoreType.DMA((2, count)),
                pltpu.SemaphoreType.DMA((2, count, 2)),
                pltpu.SemaphoreType.DMA((plan.table // LANES, 2)),
            ],
        ),
        out_shape=[jax.ShapeDtypeStruct(shape, jnp.float32) for shape in shapes],
        compiler_params=pltpu.CompilerParams(vmem_limit_bytes=VMEM),
        cost_estimate=pl.CostEstimate(
            flops=6 * max(shape[1] for shape in shapes) * count * LANES * plan.width, bytes_accessed=15_000_000, transcendentals=0
        ),
        name="partial_spectra",
    )(scal, winds, theta, thick, top, bottom, *tabs)
    return dict(zip(arrays, outs))


def edge_kernel(plan, count, _, *refs):
    ins, outs = refs[:-2], refs[-2:]
    lane = lax.broadcasted_iota(jnp.int32, (plan.levels, LANES), 1)
    some = plan.rows // count
    for side, column in enumerate((0, (plan.width - 1) % LANES)):
        kept = (jnp.zeros((plan.levels, LANES), jnp.float32),) * FIELDS
        for piece in range(count):
            at = (side * count + piece) * FIELDS
            fields = ins[at : at + FIELDS]

            def pick(row, kept, fields=fields, piece=piece, column=column):
                values = (fields[0][0, row], fields[1][0, row], fields[2][row], fields[3][row])
                return tuple(
                    jnp.where(lane == row + piece * some, value[:, column : column + 1], old)
                    for value, old in zip(values, kept)
                )

            kept = lax.fori_loop(0, some, pick, kept, unroll=max(k for k in range(1, 11) if some % k == 0))
        for field in range(FIELDS):
            outs[side][field] = kept[field]


def edges(plan, after, winds, theta, thick):
    count = 3 if plan.rows % 3 == 0 else 1
    some = plan.rows // count
    specs = []
    for at in (0, (plan.width - 1) // LANES):
        for piece in range(count):
            for wind in range(2):
                specs.append(
                    pl.BlockSpec(
                        (1, some, plan.levels, LANES), lambda i, w=wind, p=piece, at=at: (w, p, 0, at)
                    )
                )
            specs += [pl.BlockSpec((some, plan.levels, LANES), lambda i, p=piece, at=at: (p, 0, at))] * 2
    shape = (FIELDS, plan.levels, LANES)
    return pl.pallas_call(
        functools.partial(edge_kernel, plan, count),
        grid=(1,),
        in_specs=[pl.BlockSpec(memory_space=pl.ANY)] + specs,
        out_specs=[pl.BlockSpec(shape, lambda i: (0, 0, 0))] * 2,
        out_shape=[jax.ShapeDtypeStruct(shape, jnp.float32)] * 2,
        compiler_params=pltpu.CompilerParams(vmem_limit_bytes=VMEM),
        cost_estimate=pl.CostEstimate(flops=0, bytes_accessed=6_000_000, transcendentals=0),
        name="edge_columns",
    )(after, *[winds, winds, theta, thick] * (2 * count))


def step_kernel(plan, step_rows, scal, coef, west, east, top, bottom, cuts, i_high, i_low, *refs):
    places, heights = plan.places(), plan.heights()
    halves = plan.levels // 8
    raw, refs = refs[: FIELDS * halves], refs[FIELDS * halves :]
    spectra = refs[: FIELDS * len(heights)]
    new_wind, new_theta, new_thick, held, sums, unpacked, table, ready, sems, t_sems, out_sems = refs[FIELDS * len(heights) :]
    step = pl.program_id(0)
    rows, width, wide, levels = plan.rows, plan.width, plan.wide, plan.levels
    last_step = rows // step_rows

    def inverse(at, groups):
        slot_at = np.cumsum([0] + [group.slots for group in groups])
        row_at = np.cumsum([0] + [group.total for group in groups])

        def copies(g):
            number, offset = places[at, g]
            return [
                pltpu.make_async_copy(
                    spectra[number * FIELDS + u].at[pl.ds(offset, groups[g].total)],
                    sums.at[u, pl.ds(int(row_at[g]), groups[g].total)],
                    sems.at[g, u],
                )
                for u in range(FIELDS)
            ]

        have = 0
        for g, group in enumerate(groups):
            for copy in copies(g):
                copy.start()
            for copy in fetch_table(scal[1], (i_high, i_high, i_low), table, t_sems, range(have, group.blocks)):
                copy.start()
            have = max(have, group.blocks)
        have = 0
        for g, group in enumerate(groups):
            for copy in copies(g):
                copy.wait()
            for copy in fetch_table(scal[1], (i_high, i_high, i_low), table, t_sems, range(have, group.blocks)):
                copy.wait()
            have = max(have, group.blocks)
            lanes = group.blocks * LANES
            first_slot, first_sum = int(slot_at[g]), int(row_at[g])

            def back_of(spec, size, lanes=lanes, group=group):
                back = three_pass_in(spec, table[: group.blocks].reshape(3 * lanes, wide))
                return back.reshape(size, levels, wide)

            def masked(u, slot, size, group=group, first_slot=first_slot, first_sum=first_sum):
                rows_at = pl.ds(pl.multiple_of((first_slot + slot) * levels, 8), size)
                cut = cuts[rows_at, :]
                lane = lax.broadcasted_iota(jnp.int32, (size, LANES), 1)
                pieces = []
                for b in range(group.blocks):
                    keep = lax.shift_right_logical(lane + (b * LANES + 1), 1) <= cut
                    if group.packed and b == group.blocks - 1:
                        value = unpacked[u, pl.ds(pl.multiple_of(slot * levels, 8), size), :]
                    else:
                        source = pl.multiple_of(first_sum + b * group.height + slot * levels, 8)
                        value = sums[u, pl.ds(source, size), :]
                    pieces.append(jnp.where(keep, value, 0.0))
                return jnp.concatenate(pieces, axis=1)

            def unpack(u, _, group=group, first_sum=first_sum):
                def packed(row, count):
                    at_row = first_sum + group.full + row * levels
                    return sums[u, at_row : at_row + count * levels, :]

                def to(slot, count, value):
                    at_row = pl.multiple_of(slot * levels, 8)
                    unpacked[u, pl.ds(at_row, count * levels), :] = value

                group.unpack(scal[3], packed, to)
                return 0

            if group.packed:
                lax.fori_loop(0, FIELDS, unpack, 0)
            if group.farthest:
                spec = jnp.concatenate([masked(u, 0, levels) for u in range(FIELDS)], axis=0)
                back = back_of(spec, FIELDS)

                @pl.when(scal[4] >= 0)
                def _(back=back):
                    for u in range(FIELDS):
                        held[u ^ scal[0], scal[4]] = back[u]
            else:
                start = group.start(scal[3], rows)

                def part(n, _, group=group, start=start, masked=masked, back_of=back_of):
                    u, slot = n // group.parts, group.chunk_at(lax.rem(n, group.parts))
                    back = back_of(masked(u, slot, group.chunk * levels), group.chunk)
                    held[u ^ scal[0], pl.ds(start + slot, group.chunk)] = back
                    return 0

                lax.fori_loop(0, FIELDS * group.parts, part, 0)

    @pl.when(step == 0)
    def _():
        for at, groups in enumerate(plan.roles):
            pl.when(scal[2] == at)(functools.partial(inverse, at, groups))
        for side, line in enumerate((top, bottom)):

            @pl.when(scal[5 + side] == 0)
            def _(side=side, line=line):
                for field in range(FIELDS):
                    held[field, side * (rows + 1), :, :width] = line[field]

    base = step * step_rows
    tail = width % LANES

    @pl.when(step < last_step)
    def _():
        lane = lax.broadcasted_iota(jnp.int32, (levels, LANES), 1)

        def load(n, _):
            at = n
            row = base + n
            is_raw = (row >= scal[7]) & (row < scal[8])
            for field in range(FIELDS):
                for half in range(halves):
                    piece = raw[field * halves + half]
                    some = slice(half * 8, half * 8 + 8)
                    value = piece[0, at] if field < 2 else piece[at]
                    held[field, row + 1, some, :width] = jnp.where(
                        is_raw, value, held[field, row + 1, some, :width]
                    )
                beyond = jnp.where(
                    lane == tail,
                    pltpu.roll(east[field], (tail + LANES - row) & (LANES - 1), 1),
                    pltpu.roll(west[field], (2 * LANES - 1 - row) & (LANES - 1), 1),
                )
                held[field, row + 1, :, width:] = jnp.where(
                    is_raw, beyond[:, tail:], held[field, row + 1, :, width:]
                )
            return 0

        @pl.when((base < scal[8]) & (base + step_rows > scal[7]))
        def _():
            lax.fori_loop(0, step_rows, load, 0, unroll=3 if step_rows % 3 == 0 else 1)

    slot = step % 2
    count = wide // LANES
    lane = lax.broadcasted_iota(jnp.int32, (8, LANES), 1)
    is_first, is_last = lane == 0, lane == LANES - 1

    def stencil(row, _):
        at = base - step_rows + row
        along, across, push, turn, cos_north, cos_south = [coef[k * rows + at] for k in range(6)]
        across_north, across_south = across * cos_north, across * cos_south
        for part in range(levels // 8):
            some = pl.ds(part * 8, 8)

            def load(field, shift, k):
                return held[field, at + shift, some, k * LANES : (k + 1) * LANES]

            here = [
                functools.lru_cache(maxsize=None)(lambda k, field=field: load(field, 1, k))
                for field in range(FIELDS)
            ]
            up = [functools.lru_cache(maxsize=None)(lambda k, f=f: pltpu.roll(f(k), LANES - 1, 1)) for f in here]
            down = [functools.lru_cache(maxsize=None)(lambda k, f=f: pltpu.roll(f(k), 1, 1)) for f in here]

            def shifted(which, k):
                return (
                    jnp.where(is_last, up[which]((k + 1) % count), up[which](k)),
                    jnp.where(is_first, down[which]((k - 1) % count), down[which](k)),
                )

            for k in range(count):
                stop = min(width, (k + 1) * LANES)

                def put(field, piece, k=k, stop=stop):
                    ready[slot, field, row, some, k * LANES : stop] = piece[:, : stop - k * LANES]

                u, v, t, h = [here[field](k) for field in range(FIELDS)]
                advect, carry = along * u, 0.1 * v
                (u_e, u_w), (v_e, v_w), (t_e, t_w), (h_e, h_w) = [shifted(field, k) for field in range(FIELDS)]
                v_n, v_s, h_n, h_s = load(1, 0, k), load(1, 2, k), load(3, 0, k), load(3, 2, k)
                put(
                    3,
                    h
                    - along * (u_e * h_e - u_w * h_w)
                    - (across_south * (v_s * h_s) - across_north * (v_n * h_n)),
                )
                put(
                    1,
                    v
                    - advect * (v_e - v_w)
                    - carry * (v_s - v_n)
                    - 0.15 * (h_s - h_n)
                    - turn * u,
                )
                put(
                    0,
                    u
                    - advect * (u_e - u_w)
                    - carry * (load(0, 2, k) - load(0, 0, k))
                    - push * (h_e - h_w)
                    + turn * v,
                )
                put(2, t - advect * (t_e - t_w) - carry * (load(2, 2, k) - load(2, 0, k)))
        return 0

    outs = (new_wind.at[0], new_wind.at[1], new_theta, new_thick)

    def leave(at_step, size, act):
        for field, out in enumerate(outs):
            for k in range(0, step_rows, size):
                act(
                    pltpu.make_async_copy(
                        ready.at[at_step % 2, field, pl.ds(k, size)],
                        out.at[pl.ds((at_step - 1) * step_rows + k, size)],
                        out_sems.at[at_step % 2, field],
                    )
                )

    @pl.when(step > 2)
    def _():
        leave(step - 2, step_rows, lambda copy: copy.wait())

    @pl.when(step > 0)
    def _():
        lax.fori_loop(0, step_rows, stencil, 0)
        leave(step, PIECE if step_rows % PIECE == 0 else step_rows, lambda copy: copy.start())

    @pl.when(step == last_step)
    def _():
        if last_step > 1:
            leave(step - 1, step_rows, lambda copy: copy.wait())
        leave(step, step_rows, lambda copy: copy.wait())


def substep(plan, step_rows, scal, coef, winds, theta, thick, west, east, top, bottom, cuts, tabs, spectra):
    rows, width, levels = plan.rows, plan.width, plan.levels
    once = pl.Buffered(1)
    steps = rows // step_rows

    def block(i, s):
        return jnp.clip(i, s[9], s[10])

    def whole(shape):
        return pl.BlockSpec(shape, lambda i, s: (0,) * len(shape), pipeline_mode=once)

    anywhere = pl.BlockSpec(memory_space=pl.ANY)
    halves = range(levels // 8)
    raw_specs = [
        pl.BlockSpec((1, step_rows, 8, width), lambda i, s, w=wind, h=half: (w, block(i, s), h, 0))
        for wind in range(2)
        for half in halves
    ] + [
        pl.BlockSpec((step_rows, 8, width), lambda i, s, h=half: (block(i, s), h, 0))
        for _ in range(2)
        for half in halves
    ]
    raw = [array for array in (winds, winds, theta, thick) for _ in halves]
    edge, halo = (FIELDS, levels, LANES), (FIELDS, levels, width)
    in_specs = [
        pl.BlockSpec(memory_space=pltpu.SMEM),
        whole(edge),
        whole(edge),
        whole(halo),
        whole(halo),
        whole((plan.slots * levels, LANES)),
        anywhere,
        anywhere,
    ] + raw_specs + [anywhere] * len(spectra)
    shapes = [(2, rows, levels, width)] + [(rows, levels, width)] * 2
    most = max(sum(group.total for group in groups) for groups in plan.roles)
    return pl.pallas_call(
        functools.partial(step_kernel, plan, step_rows),
        grid_spec=pltpu.PrefetchScalarGridSpec(
            num_scalar_prefetch=1,
            grid=(steps + 1,),
            in_specs=in_specs,
            out_specs=[anywhere] * 3,
            scratch_shapes=[
                pltpu.VMEM((FIELDS, rows + 2, levels, plan.wide), jnp.float32),
                pltpu.VMEM((FIELDS, most, LANES), jnp.float32),
                pltpu.VMEM((FIELDS, max(group.height for groups in plan.roles for group in groups), LANES), jnp.float32),
                pltpu.VMEM((plan.table // LANES, 3, LANES, plan.wide), jnp.bfloat16),
                pltpu.VMEM((2, FIELDS, step_rows, levels, width), jnp.float32),
                pltpu.SemaphoreType.DMA((max(len(groups) for groups in plan.roles), FIELDS)),
                pltpu.SemaphoreType.DMA((plan.table // LANES, 3)),
                pltpu.SemaphoreType.DMA((2, FIELDS)),
            ],
        ),
        out_shape=[jax.ShapeDtypeStruct(shape, jnp.float32) for shape in shapes],
        compiler_params=pltpu.CompilerParams(vmem_limit_bytes=VMEM),
        cost_estimate=pl.CostEstimate(
            flops=6 * most * FIELDS * LANES * plan.wide, bytes_accessed=40_000_000, transcendentals=0
        ),
        name="inverse_and_substep",
    )(scal, coef, west, east, top, bottom, cuts, *tabs, *raw, *spectra)


def lon_swap(plan, value, blocks, bit):
    pairs = [
        (block * plan.lon + place, block * plan.lon + (place ^ (1 << bit)))
        for block in blocks
        for place in range(plan.lon)
    ]
    return lax.ppermute(value, ("lat", "lon"), pairs)


def lat_move(plan, value, sources, targets):
    pairs = [
        (source * plan.lon + place, target * plan.lon + place)
        for source, target in zip(sources, targets)
        for place in range(plan.lon)
    ]
    return lax.ppermute(value, ("lat", "lon"), pairs)


def spread(plan, blocks, slots, order):
    for bit in reversed(order):
        for s in sorted(slots):
            slots[s | (1 << bit)] = lon_swap(plan, slots[s], blocks, bit)
    return slots


def gather_sums(plan, blocks, slots, order):
    slots = dict(slots)
    for bit in order:
        sent = [s for s in slots if s >> bit & 1]
        for s in sorted(sent, key=lambda s: -bin(s).count("1")):
            slots[s ^ (1 << bit)] = slots[s ^ (1 << bit)] + lon_swap(plan, slots.pop(s), blocks, bit)
    return spread(plan, blocks, slots, order)


def field_sets(plan):
    sent, kept = [], []
    for at in range(len(plan.roles)):
        bit = at % 2
        sent.append([u for u in range(FIELDS) if u >> bit & 1])
        kept.append([u for u in range(FIELDS) if not u >> bit & 1])
    return sent, kept


def parcel_sums(plan, place, at, blocks, sent, kept):
    first, second = field_sets(plan)
    parts, own = plan.parts, place % plan.parts
    if parts == 1:
        near, far = at % 2, 1 - at % 2
        moved = lon_swap(plan, sent, blocks, near)
        send = kept[1] + moved[1]
        slots = {0: (kept[0] + moved[0]) + lon_swap(plan, send, blocks, far)}
        slots = spread(plan, blocks, slots, [near, far])
        return [slots[u] for u in range(FIELDS)]
    bits = plan.lon.bit_length() - 1
    slots = {}
    for us, array in ((first[at], sent), (second[at], kept)):
        for i, u in enumerate(us):
            pieces = array[i].reshape(parts, -1, LANES)
            for k in range(parts):
                slots[u * parts + k] = pieces[k ^ own]
    order = list(range(bits)) if at % 2 == 0 else list(reversed(range(bits)))
    slots = gather_sums(plan, blocks, slots, order)
    result = []
    for u in range(FIELDS):
        pieces = jnp.stack([slots[u * parts + k] for k in range(parts)])
        result.append(pieces[jnp.arange(parts) ^ own].reshape(-1, LANES))
    return result


def all_sums(plan, place, arrays):
    result = []
    for at in range(len(plan.roles)):
        home = plan.blocks(at)
        for parcel in range(len(plan.parcels(at))):
            first, second = arrays[at, parcel, 0], arrays[at, parcel, 1]
            if parcel == 0:
                result += parcel_sums(plan, place, at, home, first, second)
                continue
            helpers = plan.blocks(at + len(plan.roles))
            first, second = [lat_move(plan, array, home, helpers) for array in (first, second)]
            sums = parcel_sums(plan, place, at, helpers, first, second)
            result += [lat_move(plan, array, helpers, home) for array in sums]
    return result


def body(winds, theta, thick, polar_rows, cutoffs):
    lat, lon = lax.axis_size("lat"), lax.axis_size("lon")
    levels, rows, width = theta.shape
    sizes = (lat, lon, levels, rows, width, polar_rows.shape[0])
    plan = Plan(*sizes)
    t_tabs, i_tabs = [tuple(jnp.asarray(part) for part in pair) for pair in tables(sizes)]
    block, place = lax.axis_index("lat"), lax.axis_index("lon")
    winds = winds.transpose(0, 2, 1, 3)
    theta = theta.transpose(1, 0, 2)
    thick = thick.transpose(1, 0, 2)
    hemi = (block >= lat // 2).astype(jnp.int32)
    role = jnp.where(hemi == 1, lat - 1 - block, block)

    def line(row):
        return jnp.stack([winds[0, row], winds[1, row], theta[row], thick[row]])

    south_pairs = [(b * lon + p, (b + 1) * lon + p) for b in range(lat - 1) for p in range(lon)]
    north_pairs = [(to, at) for at, to in south_pairs]
    top = lax.ppermute(line(rows - 1), ("lat", "lon"), south_pairs)
    bottom = lax.ppermute(line(0), ("lat", "lon"), north_pairs)

    step_rows = max(k for k in range(1, 16) if rows % k == 0)
    listed = polar_rows.shape[0]
    north_run = jnp.sum((polar_rows < plan.total_rows // 2).astype(jnp.int32))
    south_first = plan.total_rows - listed + north_run
    far_row = jnp.where(hemi == 1, south_first, north_run - 1)
    far_at = far_row - block * rows + 1
    far_at = jnp.where((far_at >= 0) & (far_at <= rows + 1), far_at, -1)
    raw_from = jnp.clip(north_run - block * rows, 0, rows)
    raw_to = jnp.clip(south_first - block * rows, 0, rows)
    block_from = jnp.minimum(raw_from, rows - 1) // step_rows
    block_to = jnp.maximum(block_from, jnp.maximum(raw_to - 1, 0) // step_rows)
    above, below = block * rows - 1, (block + 1) * rows

    def is_listed(row):
        return (row >= 0) & (row < plan.total_rows) & ((row < north_run) | (row >= south_first))

    facts = [
        place // plan.parts, place, role, hemi, far_at, is_listed(above), is_listed(below),
        raw_from, raw_to, block_from, block_to,
    ]
    scal = jnp.stack([jnp.asarray(fact).astype(jnp.int32) for fact in facts])

    arrays = forward(plan, 0, scal, winds, theta, thick, top, bottom, t_tabs)
    scal, arrays = lax.optimization_barrier((scal, arrays))
    later = forward(plan, 1, scal, winds, theta, thick, top, bottom, t_tabs)

    first_edge, last_edge = edges(plan, later[plan.arrays()[1][0]], winds, theta, thick)
    some = [b for b in range(lat) if (min(b, lat - 1 - b) + 1) * rows > plan.low]
    east_pairs = [(b * lon + i, b * lon + (i + 1) % lon) for b in some for i in range(lon)]
    west = lax.ppermute(last_edge, ("lat", "lon"), east_pairs)
    east = lax.ppermute(first_edge, ("lat", "lon"), [(to, at) for at, to in east_pairs])
    added = {key: array for key, array in later.items() if key[2] == 1}
    added, west, east = lax.optimization_barrier((added, west, east))
    arrays = {**arrays, **later, **added}
    sums = all_sums(plan, place, arrays)

    slot_rows = jnp.asarray(plan.slot_rows())[jnp.minimum(role, len(plan.roles) - 1), hemi]
    slot_rows = jnp.where(slot_rows == -2, far_at, slot_rows)
    hits = (polar_rows[None, :] == (slot_rows - 1 + block * rows)[:, None]) & (slot_rows >= 0)[:, None]
    cut = jnp.sum(jnp.where(hits, cutoffs[None, :] + 1, 0), axis=1) - 1
    cuts = jnp.broadcast_to(cut.astype(jnp.int32)[:, None, None], (plan.slots, levels, LANES))
    cuts = cuts.reshape(plan.slots * levels, LANES)

    ring = block * rows - 1 + jnp.arange(rows + 2, dtype=jnp.int32)
    centre = (ring.astype(jnp.float32) + 0.5) * (jnp.pi / plan.total_rows)
    cos, sin = jnp.sin(centre), -jnp.cos(centre)
    mid = cos[1:-1]
    coef = jnp.concatenate([0.025 / mid, 0.1 / mid, 0.05 / mid, 0.3 * sin[1:-1], cos[:-2], cos[2:]])

    out = substep(
        plan, step_rows, scal, coef, winds, theta, thick, west, east, top, bottom, cuts, i_tabs, sums
    )
    return (out[0].transpose(0, 2, 1, 3), out[1].transpose(1, 0, 2), out[2].transpose(1, 0, 2))


def solution(mesh):
    in_specs = (P(None, None, "lat", "lon"), P(None, "lat", "lon"), P(None, "lat", "lon"), P(), P())
    out_specs = (P(None, None, "lat", "lon"), P(None, "lat", "lon"), P(None, "lat", "lon"))
    return jax.shard_map(body, mesh=mesh, in_specs=in_specs, out_specs=out_specs, check_vma=False)
```

profile of v0, /device:TPU:26, one launch (start us, length us, event | category | flops | bytes accessed | tf_op | source)
XLA Modules:
  0.0 222.4 jit_solution(15859649439265539334)
XLA Ops:
  2.4 1.9 collective-permute-start
  4.4 3.6 %collective-permute-start.1 = (f32[4,16,720]{2,1,0:T(8,128)S(1)}, f32[4,16,720]{2,1,0:T(8,128)S(1)}, u32[]{:S(2)}, u32[]{:S(2)}) collective-permute-start(f32[4,16,720]{2,1,0:T(8,128)S(1)} %pad_maximum_fusion.1), channel_id=1, source_target_pairs={{4,0},{5,1},{6,2},{7,3},{8,4},{9,5},{10,6},{11,7},{12,8},{13,9},{1... | collective-permute-start | bytes 552968 | tf_op jit(solution)/shard_map/ppermute | solution.py:894
  8.1 1.3 fusion.9
  14.7 12.5 %partial_spectra.2 = (f32[2,2496,128]{2,1,0:T(8,128)}, f32[2,1600,128]{2,1,0:T(8,128)}, f32[2,1600,128]{2,1,0:T(8,128)}) custom-call(s32[11]{0:T(128)} %stack.58.scal, f32[2,90,16,720]{3,2,1,0:T(8,128)} %bitcast.49, f32[90,16,720]{2,1,0:T(8,128)} %bitcast.68, f32[90,16,720]{2,1,0:T(8,128)} %bitcast.79, f32[4,16,720]{2,1,0:T(8,128)} %copy-done.6, ...), custom_call_target="tpu_custom_call" | custom-call | flops 5520752640 | bytes 15000000 | tf_op jit(solution)/shard_map/partial_spectra/pallas_call | solution.py:423
  27.3 16.3 %partial_spectra.3 = (f32[2,2496,128]{2,1,0:T(8,128)}, f32[2,2336,128]{2,1,0:T(8,128)}, f32[2,2336,128]{2,1,0:T(8,128)}) custom-call(s32[11]{0:T(128)} %stack.58.scal, f32[2,90,16,720]{3,2,1,0:T(8,128)} %bitcast.50, f32[90,16,720]{2,1,0:T(8,128)} %bitcast.69, f32[90,16,720]{2,1,0:T(8,128)} %bitcast.80, f32[4,16,720]{2,1,0:T(8,128)} %copy-done.6, ...), custom_call_target="tpu_custom_call" | custom-call | flops 5520752640 | bytes 15000000 | tf_op jit(solution)/shard_map/partial_spectra/pallas_call | solution.py:423
  43.6 3.1 %collective-permute-start.9 = (f32[2,2336,128]{2,1,0:T(8,128)}, f32[2,2336,128]{2,1,0:T(8,128)}, u32[]{:S(2)}, u32[]{:S(2)}) collective-permute-start(f32[2,2336,128]{2,1,0:T(8,128)} %get-tuple-element.35), channel_id=1, source_target_pairs={{4,6},{5,7},{6,4},{7,5},{24,26},{25,27},{26,24},{27,25}} | collective-permute-start | bytes 7176200 | tf_op jit(solution)/shard_map/ppermute | solution.py:796
  47.5 2.5 %collective-permute-start.15 = (f32[2,1600,128]{2,1,0:T(8,128)}, f32[2,1600,128]{2,1,0:T(8,128)}, u32[]{:S(2)}, u32[]{:S(2)}) collective-permute-start(f32[2,1600,128]{2,1,0:T(8,128)} %get-tuple-element.37), channel_id=1, source_target_pairs={{4,12},{5,13},{6,14},{7,15},{24,16},{25,17},{26,18},{27,19}} | collective-permute-start | bytes 4915208 | tf_op jit(solution)/shard_map/ppermute | solution.py:805
  50.1 6.2 %edge_columns.1 = (f32[4,16,128]{2,1,0:T(8,128)}, f32[4,16,128]{2,1,0:T(8,128)}) custom-call(f32[2,2496,128]{2,1,0:T(8,128)} %get-tuple-element.32._, f32[2,90,16,720]{3,2,1,0:T(8,128)} %bitcast.51, f32[2,90,16,720]{3,2,1,0:T(8,128)} %bitcast.52, f32[90,16,720]{2,1,0:T(8,128)} %bitcast.70, f32[90,16,720]{2,1,0:T(8,128)} %bitcast.81, ...), custom_call_target="tpu_custom_call" | custom-call | bytes 6000000 | tf_op jit(solution)/shard_map/edge_columns/pallas_call | solution.py:485
  56.3 2.7 %collective-permute-start.2 = (f32[4,16,128]{2,1,0:T(8,128)}, f32[4,16,128]{2,1,0:T(8,128)S(1)}, u32[]{:S(2)}, u32[]{:S(2)}) collective-permute-start(f32[4,16,128]{2,1,0:T(8,128)} %get-tuple-element.28), channel_id=1, source_target_pairs={{4,5},{5,6},{6,7},{7,4},{8,9},{9,10},{10,11},{11,8},{12,13},{13,14... | collective-permute-start | bytes 98312 | tf_op jit(solution)/shard_map/ppermute | solution.py:925
  59.0 1.4 collective-permute-start.14
  60.4 7.3 %collective-permute-done.15 = f32[2,1600,128]{2,1,0:T(8,128)} collective-permute-done((f32[2,1600,128]{2,1,0:T(8,128)}, f32[2,1600,128]{2,1,0:T(8,128)}, u32[]{:S(2)}, u32[]{:S(2)}) %collective-permute-start.15) | collective-permute-done | bytes 1638432 | tf_op jit(solution)/shard_map/ppermute | solution.py:805
  68.5 2.3 %collective-permute-start.3 = (f32[4,16,128]{2,1,0:T(8,128)}, f32[4,16,128]{2,1,0:T(8,128)S(1)}, u32[]{:S(2)}, u32[]{:S(2)}) collective-permute-start(f32[4,16,128]{2,1,0:T(8,128)} %get-tuple-element.29), channel_id=1, source_target_pairs={{5,4},{6,5},{7,6},{4,7},{9,8},{10,9},{11,10},{8,11},{13,12},{14,13... | collective-permute-start | bytes 98312 | tf_op jit(solution)/shard_map/ppermute | solution.py:926
  70.8 5.0 %collective-permute-done.3.east = f32[4,16,128]{2,1,0:T(8,128)S(1)} collective-permute-done((f32[4,16,128]{2,1,0:T(8,128)}, f32[4,16,128]{2,1,0:T(8,128)S(1)}, u32[]{:S(2)}, u32[]{:S(2)}) %collective-permute-start.3) | collective-permute-done | bytes 32800 | tf_op jit(solution)/shard_map/ppermute | solution.py:926
  75.9 1.9 fusion.3
  77.8 2.0 collective-permute-start.10
  82.2 3.1 %collective-permute-done.14 = f32[2,1600,128]{2,1,0:T(8,128)S(1)} collective-permute-done((f32[2,1600,128]{2,1,0:T(8,128)}, f32[2,1600,128]{2,1,0:T(8,128)S(1)}, u32[]{:S(2)}, u32[]{:S(2)}) %collective-permute-start.14) | collective-permute-done | bytes 1638432 | tf_op jit(solution)/shard_map/ppermute | solution.py:805
  86.4 9.6 %collective-permute-done.10 = f32[2336,128]{1,0:T(8,128)S(1)} collective-permute-done((f32[2336,128]{1,0:T(8,128)S(1)}, f32[2336,128]{1,0:T(8,128)S(1)}, u32[]{:S(2)}, u32[]{:S(2)}) %collective-permute-start.10) | collective-permute-done | bytes 1196064 | tf_op jit(solution)/shard_map/ppermute | solution.py:796
  96.1 1.5 fusion.5.refs_12_
  97.6 2.7 %collective-permute-start.12 = (f32[2336,128]{1,0:T(8,128)S(1)}, f32[2336,128]{1,0:T(8,128)S(1)}, u32[]{:S(2)}, u32[]{:S(2)}) collective-permute-start(f32[2336,128]{1,0:T(8,128)S(1)} %fusion.5.refs_12_), channel_id=1, source_target_pairs={{4,6},{5,7},{6,4},{7,5},{24,26},{25,27},{26,24},{27,25}} | collective-permute-start | bytes 3588104 | tf_op jit(solution)/shard_map/ppermute | solution.py:796
  100.3 2.2 collective-permute-start.11
  103.8 1.6 collective-permute-start.19
  105.4 1.7 collective-permute-start.6
  107.1 19.8 %collective-permute-done.12.refs_14_ = f32[2336,128]{1,0:T(8,128)S(1)} collective-permute-done((f32[2336,128]{1,0:T(8,128)S(1)}, f32[2336,128]{1,0:T(8,128)S(1)}, u32[]{:S(2)}, u32[]{:S(2)}) %collective-permute-start.12) | collective-permute-done | bytes 1196064 | tf_op jit(solution)/shard_map/ppermute | solution.py:796
  127.0 1.6 collective-permute-start.21
  128.5 2.8 %collective-permute-done.11.refs_13_ = f32[2336,128]{1,0:T(8,128)S(1)} collective-permute-done((f32[2336,128]{1,0:T(8,128)S(1)}, f32[2336,128]{1,0:T(8,128)S(1)}, u32[]{:S(2)}, u32[]{:S(2)}) %collective-permute-start.11) | collective-permute-done | bytes 1196064 | tf_op jit(solution)/shard_map/ppermute | solution.py:796
  132.7 1.6 collective-permute-start.23
  134.3 1.8 collective-permute-start.8
  136.0 3.2 %collective-permute-start.13 = (f32[2336,128]{1,0:T(8,128)}, f32[2336,128]{1,0:T(8,128)}, u32[]{:S(2)}, u32[]{:S(2)}) collective-permute-start(f32[2336,128]{1,0:T(8,128)} %copy-done.10), channel_id=1, source_target_pairs={{4,6},{5,7},{6,4},{7,5},{24,26},{25,27},{26,24},{27,25}} | collective-permute-start | bytes 3588104 | tf_op jit(solution)/shard_map/ppermute | solution.py:796
  139.3 6.4 %collective-permute-done.18.refs_16_ = f32[1600,128]{1,0:T(8,128)} collective-permute-done((f32[1600,128]{1,0:T(8,128)S(1)}, f32[1600,128]{1,0:T(8,128)}, u32[]{:S(2)}, u32[]{:S(2)}) %collective-permute-start.18) | collective-permute-done | bytes 819232 | tf_op jit(solution)/shard_map/ppermute | solution.py:805
  150.9 18.0 %collective-permute-done.22.refs_18_ = f32[1600,128]{1,0:T(8,128)S(1)} collective-permute-done((f32[1600,128]{1,0:T(8,128)}, f32[1600,128]{1,0:T(8,128)S(1)}, u32[]{:S(2)}, u32[]{:S(2)}) %collective-permute-start.22) | collective-permute-done | bytes 819232 | tf_op jit(solution)/shard_map/ppermute | solution.py:805
  168.9 8.9 %collective-permute-done.24.refs_19_ = f32[1600,128]{1,0:T(8,128)} collective-permute-done((f32[1600,128]{1,0:T(8,128)}, f32[1600,128]{1,0:T(8,128)}, u32[]{:S(2)}, u32[]{:S(2)}) %collective-permute-start.24) | collective-permute-done | bytes 819232 | tf_op jit(solution)/shard_map/ppermute | solution.py:805
  178.9 43.3 %inverse_and_substep.1 = (f32[2,90,16,720]{3,2,1,0:T(8,128)}, f32[90,16,720]{2,1,0:T(8,128)}, f32[90,16,720]{2,1,0:T(8,128)}) custom-call(s32[11]{0:T(128)} %stack.58.scal, f32[540]{0:T(1024)} %concatenate.3.coef, f32[4,16,128]{2,1,0:T(8,128)} %copy-done.13, f32[4,16,128]{2,1,0:T(8,128)} %copy-done.14, f32[4,16,720]{2,1,0:T(8,128)} %copy-done.6, ...), custom_call_target="tpu_custom_call" | custom-call | flops 9286189056 | bytes 40000000 | tf_op jit(solution)/shard_map/inverse_and_substep/pallas_call | solution.py:763
  (82 shorter events, 17.7 us)
Async XLA Ops:
  2.4 10.9 %collective-permute-start = (f32[4,16,720]{2,1,0:T(8,128)S(1)}, f32[4,16,720]{2,1,0:T(8,128)S(1)}, u32[]{:S(2)}, u32[]{:S(2)}) collective-permute-start(f32[4,16,720]{2,1,0:T(8,128)S(1)} %pad_maximum_fusion), channel_id=1, source_target_pairs={{0,4},{1,5},{2,6},{3,7},{4,8},{5,9},{6,10},{7,11},{8,12},{9,13},{1... | collective-permute-start | bytes 552968 | tf_op jit(solution)/shard_map/ppermute | solution.py:893
  4.4 9.0 %collective-permute-start.1 = (f32[4,16,720]{2,1,0:T(8,128)S(1)}, f32[4,16,720]{2,1,0:T(8,128)S(1)}, u32[]{:S(2)}, u32[]{:S(2)}) collective-permute-start(f32[4,16,720]{2,1,0:T(8,128)S(1)} %pad_maximum_fusion.1), channel_id=1, source_target_pairs={{4,0},{5,1},{6,2},{7,3},{8,4},{9,5},{10,6},{11,7},{12,8},{13,9},{1... | collective-permute-start | bytes 552968 | tf_op jit(solution)/shard_map/ppermute | solution.py:894
  43.6 32.3 %collective-permute-start.9 = (f32[2,2336,128]{2,1,0:T(8,128)}, f32[2,2336,128]{2,1,0:T(8,128)}, u32[]{:S(2)}, u32[]{:S(2)}) collective-permute-start(f32[2,2336,128]{2,1,0:T(8,128)} %get-tuple-element.35), channel_id=1, source_target_pairs={{4,6},{5,7},{6,4},{7,5},{24,26},{25,27},{26,24},{27,25}} | collective-permute-start | bytes 7176200 | tf_op jit(solution)/shard_map/ppermute | solution.py:796
  46.7 33.1 %collective-permute-start.4 = (f32[2,2496,128]{2,1,0:T(8,128)}, f32[2,2496,128]{2,1,0:T(8,128)S(1)}, u32[]{:S(2)}, u32[]{:S(2)}) collective-permute-start(f32[2,2496,128]{2,1,0:T(8,128)} %get-tuple-element.33), channel_id=1, source_target_pairs={{0,1},{1,0},{2,3},{3,2},{28,29},{29,28},{30,31},{31,30}} | collective-permute-start | bytes 7667720 | tf_op jit(solution)/shard_map/ppermute | solution.py:796
  47.5 20.2 %collective-permute-start.15 = (f32[2,1600,128]{2,1,0:T(8,128)}, f32[2,1600,128]{2,1,0:T(8,128)}, u32[]{:S(2)}, u32[]{:S(2)}) collective-permute-start(f32[2,1600,128]{2,1,0:T(8,128)} %get-tuple-element.37), channel_id=1, source_target_pairs={{4,12},{5,13},{6,14},{7,15},{24,16},{25,17},{26,18},{27,19}} | collective-permute-start | bytes 4915208 | tf_op jit(solution)/shard_map/ppermute | solution.py:805
  56.3 12.2 %collective-permute-start.2 = (f32[4,16,128]{2,1,0:T(8,128)}, f32[4,16,128]{2,1,0:T(8,128)S(1)}, u32[]{:S(2)}, u32[]{:S(2)}) collective-permute-start(f32[4,16,128]{2,1,0:T(8,128)} %get-tuple-element.28), channel_id=1, source_target_pairs={{4,5},{5,6},{6,7},{7,4},{8,9},{9,10},{10,11},{11,8},{12,13},{13,14... | collective-permute-start | bytes 98312 | tf_op jit(solution)/shard_map/ppermute | solution.py:925
  59.0 26.3 %collective-permute-start.14 = (f32[2,1600,128]{2,1,0:T(8,128)}, f32[2,1600,128]{2,1,0:T(8,128)S(1)}, u32[]{:S(2)}, u32[]{:S(2)}) collective-permute-start(f32[2,1600,128]{2,1,0:T(8,128)} %get-tuple-element.36), channel_id=1, source_target_pairs={{4,12},{5,13},{6,14},{7,15},{24,16},{25,17},{26,18},{27,19}} | collective-permute-start | bytes 4915208 | tf_op jit(solution)/shard_map/ppermute | solution.py:805
  67.7 17.6 %collective-permute-start.16 = (f32[2,1600,128]{2,1,0:T(8,128)}, f32[2,1600,128]{2,1,0:T(8,128)S(1)}, u32[]{:S(2)}, u32[]{:S(2)}) collective-permute-start(f32[2,1600,128]{2,1,0:T(8,128)} %collective-permute-done.15), channel_id=1, source_target_pairs={{12,14},{13,15},{14,12},{15,13},{16,18},{17,19},{18,16},{19,17}} | collective-permute-start | bytes 4915208 | tf_op jit(solution)/shard_map/ppermute | solution.py:796
  68.5 7.3 %collective-permute-start.3 = (f32[4,16,128]{2,1,0:T(8,128)}, f32[4,16,128]{2,1,0:T(8,128)S(1)}, u32[]{:S(2)}, u32[]{:S(2)}) collective-permute-start(f32[4,16,128]{2,1,0:T(8,128)} %get-tuple-element.29), channel_id=1, source_target_pairs={{5,4},{6,5},{7,6},{4,7},{9,8},{10,9},{11,10},{8,11},{13,12},{14,13... | collective-permute-start | bytes 98312 | tf_op jit(solution)/shard_map/ppermute | solution.py:926
  77.8 18.3 %collective-permute-start.10 = (f32[2336,128]{1,0:T(8,128)S(1)}, f32[2336,128]{1,0:T(8,128)S(1)}, u32[]{:S(2)}, u32[]{:S(2)}) collective-permute-start(f32[2336,128]{1,0:T(8,128)S(1)} %fusion.3), channel_id=1, source_target_pairs={{4,5},{5,4},{6,7},{7,6},{24,25},{25,24},{26,27},{27,26}} | collective-permute-start | bytes 3588104 | tf_op jit(solution)/shard_map/ppermute | solution.py:796
  81.3 14.8 %copy-start.5 = (f32[2,2336,128]{2,1,0:T(8,128)S(1)}, f32[2,2336,128]{2,1,0:T(8,128)}, u32[]{:S(2)}) copy-start(f32[2,2336,128]{2,1,0:T(8,128)} %get-tuple-element.34) | copy-start | bytes 7176196
  81.3 21.2 %collective-permute-start.5 = (f32[2496,128]{1,0:T(8,128)S(1)}, f32[2496,128]{1,0:T(8,128)S(1)}, u32[]{:S(2)}, u32[]{:S(2)}) collective-permute-start(f32[2496,128]{1,0:T(8,128)S(1)} %fusion), channel_id=1, source_target_pairs={{0,2},{1,3},{2,0},{3,1},{28,30},{29,31},{30,28},{31,29}} | collective-permute-start | bytes 3833864 | tf_op jit(solution)/shard_map/ppermute | solution.py:796
  85.4 17.1 %copy-start.4 = (f32[2,2496,128]{2,1,0:T(8,128)S(1)}, f32[2,2496,128]{2,1,0:T(8,128)}, u32[]{:S(2)}) copy-start(f32[2,2496,128]{2,1,0:T(8,128)} %copy-done.3) | copy-start | bytes 7667716
  85.4 18.3 %collective-permute-start.17 = (f32[1600,128]{1,0:T(8,128)S(1)}, f32[1600,128]{1,0:T(8,128)S(1)}, u32[]{:S(2)}, u32[]{:S(2)}) collective-permute-start(f32[1600,128]{1,0:T(8,128)S(1)} %fusion.6), channel_id=1, source_target_pairs={{12,13},{13,12},{14,15},{15,14},{16,17},{17,16},{18,19},{19,18}} | collective-permute-start | bytes 2457608 | tf_op jit(solution)/shard_map/ppermute | solution.py:796
  97.6 29.4 %collective-permute-start.12 = (f32[2336,128]{1,0:T(8,128)S(1)}, f32[2336,128]{1,0:T(8,128)S(1)}, u32[]{:S(2)}, u32[]{:S(2)}) collective-permute-start(f32[2336,128]{1,0:T(8,128)S(1)} %fusion.5.refs_12_), channel_id=1, source_target_pairs={{4,6},{5,7},{6,4},{7,5},{24,26},{25,27},{26,24},{27,25}} | collective-permute-start | bytes 3588104 | tf_op jit(solution)/shard_map/ppermute | solution.py:796
  100.3 31.0 %collective-permute-start.11 = (f32[2336,128]{1,0:T(8,128)S(1)}, f32[2336,128]{1,0:T(8,128)S(1)}, u32[]{:S(2)}, u32[]{:S(2)}) collective-permute-start(f32[2336,128]{1,0:T(8,128)S(1)} %fusion.5.refs_12_), channel_id=1, source_target_pairs={{4,5},{5,4},{6,7},{7,6},{24,25},{25,24},{26,27},{27,26}} | collective-permute-start | bytes 3588104 | tf_op jit(solution)/shard_map/ppermute | solution.py:796
  102.7 31.5 %copy-start.1 = (f32[2496,128]{1,0:T(8,128)}, f32[2496,128]{1,0:T(8,128)S(1)}, u32[]{:S(2)}) copy-start(f32[2496,128]{1,0:T(8,128)S(1)} %fusion.2.refs_8_) | copy-start | bytes 3833860
  102.8 33.3 %copy-start.17 = (s32[2,2,92]{2,1,0:T(2,128)S(1)}, s32[2,2,92]{2,1,0:T(2,128)}, u32[]{:S(2)}) copy-start(s32[2,2,92]{2,1,0:T(2,128)} %constant.88.clone) | copy-start | bytes 4420
  102.8 36.5 %copy-start.16 = (s32[240]{0:T(256)S(1)}, s32[240]{0:T(256)}, u32[]{:S(2)}) copy-start(s32[240]{0:T(256)} %param.14) | copy-start | bytes 2884
  102.8 46.8 %copy-start.15 = (s32[240]{0:T(256)S(1)}, s32[240]{0:T(256)}, u32[]{:S(2)}) copy-start(s32[240]{0:T(256)} %param.13) | copy-start | bytes 2884
  102.8 31.5 %collective-permute-start.7 = (f32[2496,128]{1,0:T(8,128)S(1)}, f32[2496,128]{1,0:T(8,128)S(1)}, u32[]{:S(2)}, u32[]{:S(2)}) collective-permute-start(f32[2496,128]{1,0:T(8,128)S(1)} %fusion.2.refs_8_), channel_id=1, source_target_pairs={{0,2},{1,3},{2,0},{3,1},{28,30},{29,31},{30,28},{31,29}} | collective-permute-start | bytes 3833864 | tf_op jit(solution)/shard_map/ppermute | solution.py:796
  103.8 28.9 %collective-permute-start.19 = (f32[1600,128]{1,0:T(8,128)S(1)}, f32[1600,128]{1,0:T(8,128)}, u32[]{:S(2)}, u32[]{:S(2)}) collective-permute-start(f32[1600,128]{1,0:T(8,128)S(1)} %fusion.8), channel_id=1, source_target_pairs={{12,13},{13,12},{14,15},{15,14},{16,17},{17,16},{18,19},{19,18}} | collective-permute-start | bytes 2457608 | tf_op jit(solution)/shard_map/ppermute | solution.py:796
  105.4 41.6 %collective-permute-start.6 = (f32[2496,128]{1,0:T(8,128)S(1)}, f32[2496,128]{1,0:T(8,128)}, u32[]{:S(2)}, u32[]{:S(2)}) collective-permute-start(f32[2496,128]{1,0:T(8,128)S(1)} %fusion.2.refs_8_), channel_id=1, source_target_pairs={{0,1},{1,0},{2,3},{3,2},{28,29},{29,28},{30,31},{31,30}} | collective-permute-start | bytes 3833864 | tf_op jit(solution)/shard_map/ppermute | solution.py:796
  127.0 9.1 %collective-permute-start.21 = (f32[1600,128]{1,0:T(8,128)S(1)}, f32[1600,128]{1,0:T(8,128)}, u32[]{:S(2)}, u32[]{:S(2)}) collective-permute-start(f32[1600,128]{1,0:T(8,128)S(1)} %fusion.8), channel_id=1, source_target_pairs={{12,14},{13,15},{14,12},{15,13},{16,18},{17,19},{18,16},{19,17}} | collective-permute-start | bytes 2457608 | tf_op jit(solution)/shard_map/ppermute | solution.py:796
  131.4 14.3 %collective-permute-start.18 = (f32[1600,128]{1,0:T(8,128)S(1)}, f32[1600,128]{1,0:T(8,128)}, u32[]{:S(2)}, u32[]{:S(2)}) collective-permute-start(f32[1600,128]{1,0:T(8,128)S(1)} %fusion.8), channel_id=1, source_target_pairs={{12,4},{13,5},{14,6},{15,7},{16,24},{17,25},{18,26},{19,27}} | collective-permute-start | bytes 2457608 | tf_op jit(solution)/shard_map/ppermute | solution.py:805
  132.7 15.6 %collective-permute-start.23 = (f32[1600,128]{1,0:T(8,128)}, f32[1600,128]{1,0:T(8,128)}, u32[]{:S(2)}, u32[]{:S(2)}) collective-permute-start(f32[1600,128]{1,0:T(8,128)} %collective-permute-done.19), channel_id=1, source_target_pairs={{12,14},{13,15},{14,12},{15,13},{16,18},{17,19},{18,16},{19,17}} | collective-permute-start | bytes 2457608 | tf_op jit(solution)/shard_map/ppermute | solution.py:796
  134.3 44.7 %copy-start.8 = (f32[2496,128]{1,0:T(8,128)}, f32[2496,128]{1,0:T(8,128)S(1)}, u32[]{:S(2)}) copy-start(f32[2496,128]{1,0:T(8,128)S(1)} %collective-permute-done.7.refs_10_) | copy-start | bytes 3833860
  134.3 34.7 %collective-permute-start.8 = (f32[2496,128]{1,0:T(8,128)S(1)}, f32[2496,128]{1,0:T(8,128)}, u32[]{:S(2)}, u32[]{:S(2)}) collective-permute-start(f32[2496,128]{1,0:T(8,128)S(1)} %collective-permute-done.7.refs_10_), channel_id=1, source_target_pairs={{0,1},{1,0},{2,3},{3,2},{28,29},{29,28},{30,31},{31,30}} | collective-permute-start | bytes 3833864 | tf_op jit(solution)/shard_map/ppermute | solution.py:796
  136.0 32.9 %collective-permute-start.13 = (f32[2336,128]{1,0:T(8,128)}, f32[2336,128]{1,0:T(8,128)}, u32[]{:S(2)}, u32[]{:S(2)}) collective-permute-start(f32[2336,128]{1,0:T(8,128)} %copy-done.10), channel_id=1, source_target_pairs={{4,6},{5,7},{6,4},{7,5},{24,26},{25,27},{26,24},{27,25}} | collective-permute-start | bytes 3588104 | tf_op jit(solution)/shard_map/ppermute | solution.py:796
  145.7 23.2 %collective-permute-start.20 = (f32[1600,128]{1,0:T(8,128)}, f32[1600,128]{1,0:T(8,128)S(1)}, u32[]{:S(2)}, u32[]{:S(2)}) collective-permute-start(f32[1600,128]{1,0:T(8,128)} %collective-permute-done.19), channel_id=1, source_target_pairs={{12,4},{13,5},{14,6},{15,7},{16,24},{17,25},{18,26},{19,27}} | collective-permute-start | bytes 2457608 | tf_op jit(solution)/shard_map/ppermute | solution.py:805
  147.0 21.9 %collective-permute-start.22 = (f32[1600,128]{1,0:T(8,128)}, f32[1600,128]{1,0:T(8,128)S(1)}, u32[]{:S(2)}, u32[]{:S(2)}) collective-permute-start(f32[1600,128]{1,0:T(8,128)} %collective-permute-done.21), channel_id=1, source_target_pairs={{12,4},{13,5},{14,6},{15,7},{16,24},{17,25},{18,26},{19,27}} | collective-permute-start | bytes 2457608 | tf_op jit(solution)/shard_map/ppermute | solution.py:805
  148.3 29.5 %collective-permute-start.24 = (f32[1600,128]{1,0:T(8,128)}, f32[1600,128]{1,0:T(8,128)}, u32[]{:S(2)}, u32[]{:S(2)}) collective-permute-start(f32[1600,128]{1,0:T(8,128)} %collective-permute-done.23), channel_id=1, source_target_pairs={{12,4},{13,5},{14,6},{15,7},{16,24},{17,25},{18,26},{19,27}} | collective-permute-start | bytes 2457608 | tf_op jit(solution)/shard_map/ppermute | solution.py:805
  (11 other events, 48.9 us)
where the time goes:
time: 223 us; the launch traced here: 222 us
  waiting for transfers between devices  81.1 us (36%)
  Pallas kernels  78.3 us (35%)
  starting transfers between devices  45.4 us (20%)
  local copies, waits for them, and re-layouts  7.16 us (3%)
  other arithmetic  5.75 us (3%)
  between operations  4.6 us (2%)
    ppermute x6, waiting for transfers between devices, lat_move(): return lax.ppermute(value, ('lat', 'lon'), pairs)  43.8 us
    pallas_call x1, Pallas kernels, substep(): pl.pallas_call(functools.partial(step_kernel, plan, step_rows), grid_spec...  43.3 us
    ppermute x15, waiting for transfers between devices, lon_swap(): return lax.ppermute(value, ('lat', 'lon'), pairs)  32.3 us
    pallas_call x2, Pallas kernels, forward(): pl.pallas_call(functools.partial(forward_kernel, plan, call), grid_spec=p...  28.8 us
    ppermute x15, starting transfers between devices, lon_swap(): return lax.ppermute(value, ('lat', 'lon'), pairs)  25.8 us
    ppermute x6, starting transfers between devices, lat_move(): return lax.ppermute(value, ('lat', 'lon'), pairs)  9.09 us
    pallas_call x1, Pallas kernels, edges(): pl.pallas_call(functools.partial(edge_kernel, plan, count), grid=(1,), in...  6.24 us
    ppermute x1, waiting for transfers between devices, body(): lax.ppermute(first_edge, ('lat', 'lon'), [(to, at) for at, to in east_pai...  5.01 us
  transfers between devices with their start and end apart: 25, of which 9 were waited for; matrix products, arithmetic and copies ran while one was open for 3% of the time, Pallas kernels for 3%

commit v1 on v0

--- a/solution.py
+++ b/solution.py
@@ -13,6 +13,7 @@
 LANES = 128
 PIECE = 3
 VMEM = 60 * 1024 * 1024
+FORWARD_COST, EDGE_COST = 5_000_000_000, 5_000_000_000
 
 
 def round_up(value, step):
@@ -146,15 +147,8 @@
         return [home] if away is None else [home, [away]]
 
     def arrays(self):
-        calls = [[], []]
-        for at in range(len(self.roles)):
-            if at in self.lent:
-                calls[0] += [(at, 1, 0), (at, 1, 1)]
-                calls[1] += [(at, 0, 0), (at, 0, 1)]
-            else:
-                calls[0].append((at, 0, 0))
-                calls[1].append((at, 0, 1))
-        return calls
+        held = [(at, parcel) for at in range(len(self.roles)) for parcel in range(len(self.parcels(at)))]
+        return [[key + (which,) for key in held] for which in range(2)]
 
     def places(self):
         result, number = {}, 0
@@ -414,7 +408,7 @@
 
 def forward(plan, call, scal, winds, theta, thick, top, bottom, tabs):
     arrays = plan.arrays()[call]
-    count = FIELDS if plan.lent else FIELDS // 2
+    count = FIELDS // 2
     shapes = [(FIELDS // 2, plan.height_of(at, parcel), LANES) for at, parcel, _ in arrays]
     anywhere = pl.BlockSpec(memory_space=pl.ANY)
     halo = pl.BlockSpec((FIELDS, plan.levels, plan.width), lambda i, s: (0, 0, 0))
@@ -438,9 +432,7 @@
         ),
         out_shape=[jax.ShapeDtypeStruct(shape, jnp.float32) for shape in shapes],
         compiler_params=pltpu.CompilerParams(vmem_limit_bytes=VMEM),
-        cost_estimate=pl.CostEstimate(
-            flops=6 * max(shape[1] for shape in shapes) * count * LANES * plan.width, bytes_accessed=15_000_000, transcendentals=0
-        ),
+        cost_estimate=pl.CostEstimate(flops=FORWARD_COST, bytes_accessed=0, transcendentals=0),
         name="partial_spectra",
     )(scal, winds, theta, thick, top, bottom, *tabs)
     return dict(zip(arrays, outs))
@@ -489,7 +481,7 @@
         out_specs=[pl.BlockSpec(shape, lambda i: (0, 0, 0))] * 2,
         out_shape=[jax.ShapeDtypeStruct(shape, jnp.float32)] * 2,
         compiler_params=pltpu.CompilerParams(vmem_limit_bytes=VMEM),
-        cost_estimate=pl.CostEstimate(flops=0, bytes_accessed=6_000_000, transcendentals=0),
+        cost_estimate=pl.CostEstimate(flops=EDGE_COST, bytes_accessed=0, transcendentals=0),
         name="edge_columns",
     )(after, *[winds, winds, theta, thick] * (2 * count))
 
@@ -714,7 +706,7 @@
 
     @pl.when(step > 0)
     def _():
-        lax.fori_loop(0, step_rows, stencil, 0)
+        lax.fori_loop(0, step_rows, stencil, 0, unroll=3 if step_rows % 3 == 0 else 1)
         leave(step, PIECE if step_rows % PIECE == 0 else step_rows, lambda copy: copy.start())
 
     @pl.when(step == last_step)
@@ -915,16 +907,17 @@
     ]
     scal = jnp.stack([jnp.asarray(fact).astype(jnp.int32) for fact in facts])
 
-    arrays = forward(plan, 0, scal, winds, theta, thick, top, bottom, t_tabs)
-    scal, arrays = lax.optimization_barrier((scal, arrays))
-    later = forward(plan, 1, scal, winds, theta, thick, top, bottom, t_tabs)
-
-    first_edge, last_edge = edges(plan, later[plan.arrays()[1][0]], winds, theta, thick)
+    first_edge, last_edge = edges(plan, scal, winds, theta, thick)
     some = [b for b in range(lat) if (min(b, lat - 1 - b) + 1) * rows > plan.low]
     east_pairs = [(b * lon + i, b * lon + (i + 1) % lon) for b in some for i in range(lon)]
     west = lax.ppermute(last_edge, ("lat", "lon"), east_pairs)
     east = lax.ppermute(first_edge, ("lat", "lon"), [(to, at) for at, to in east_pairs])
-    added = {key: array for key, array in later.items() if key[2] == 1}
+
+    scal, _ = lax.optimization_barrier((scal, first_edge))
+    arrays = forward(plan, 0, scal, winds, theta, thick, top, bottom, t_tabs)
+    scal, _ = lax.optimization_barrier((scal, arrays[plan.arrays()[0][0]]))
+    later = forward(plan, 1, scal, winds, theta, thick, top, bottom, t_tabs)
+    added = {key: array for key, array in later.items() if key[1] == 0}
     added, west, east = lax.optimization_barrier((added, west, east))
     arrays = {**arrays, **later, **added}
     sums = all_sums(plan, place, arrays)

time: 223 us -> 211 us (0.946)
  waiting for transfers between devices: 81.1 us -> 72.1 us
  Pallas kernels: 78.3 us -> 72.4 us
    ppermute x6, waiting for transfers between devices: 43.8 us -> 37.5 us  [lat_move(): return lax.ppermute(value, ('lat', 'lon'), pairs)]
    pallas_call x1, Pallas kernels: 43.3 us -> 39.1 us  [substep(): pl.pallas_call(functools.partial(step_kernel, plan, step_rows), grid_spec...]
  transfers between devices with their start and end apart: 25 -> 25, of which waited for: 9 -> 8; matrix products, arithmetic and copies ran while one was open for 3% -> 3% of each run, Pallas kernels for 3% -> 10%
where the time goes in v1:
time: 211 us; the launch traced here: 209 us
  Pallas kernels  72.4 us (34%)
  waiting for transfers between devices  72.1 us (34%)
  starting transfers between devices  47.5 us (23%)
  local copies, waits for them, and re-layouts  7.04 us (3%)
  other arithmetic  5.75 us (3%)
  between operations  4.66 us (2%)
    pallas_call x1, Pallas kernels, substep(): pl.pallas_call(functools.partial(step_kernel, plan, step_rows), grid_spec...  39.1 us
    ppermute x6, waiting for transfers between devices, lat_move(): return lax.ppermute(value, ('lat', 'lon'), pairs)  37.5 us
    ppermute x15, waiting for transfers between devices, lon_swap(): return lax.ppermute(value, ('lat', 'lon'), pairs)  30.8 us
    pallas_call x2, Pallas kernels, forward(): pl.pallas_call(functools.partial(forward_kernel, plan, call), grid_spec=p...  27.1 us
    ppermute x15, starting transfers between devices, lon_swap(): return lax.ppermute(value, ('lat', 'lon'), pairs)  26.9 us
    ppermute x6, starting transfers between devices, lat_move(): return lax.ppermute(value, ('lat', 'lon'), pairs)  9.03 us
    pallas_call x1, Pallas kernels, edges(): pl.pallas_call(functools.partial(edge_kernel, plan, count), grid=(1,), in...  6.26 us
  transfers between devices with their start and end apart: 25, of which 8 were waited for; matrix products, arithmetic and copies ran while one was open for 3% of the time, Pallas kernels for 10%

profile of v1, /device:TPU:26, one launch (start us, length us, event | category | flops | bytes accessed | tf_op | source)
XLA Modules:
  0.0 209.4 jit_solution(16484415841438009369)
XLA Ops:
  2.4 1.9 collective-permute-start
  4.4 3.6 %collective-permute-start.1 = (f32[4,16,720]{2,1,0:T(8,128)S(1)}, f32[4,16,720]{2,1,0:T(8,128)S(1)}, u32[]{:S(2)}, u32[]{:S(2)}) collective-permute-start(f32[4,16,720]{2,1,0:T(8,128)S(1)} %pad_maximum_fusion.1), channel_id=1, source_target_pairs={{4,0},{5,1},{6,2},{7,3},{8,4},{9,5},{10,6},{11,7},{12,8},{13,9},{1... | collective-permute-start | bytes 552968 | tf_op jit(solution)/shard_map/ppermute | solution.py:886
  8.1 1.3 fusion.9
  13.3 6.3 %edge_columns.1 = (f32[4,16,128]{2,1,0:T(8,128)}, f32[4,16,128]{2,1,0:T(8,128)}) custom-call(s32[11]{0:T(128)} %stack.58._.scal, f32[2,90,16,720]{3,2,1,0:T(8,128)} %bitcast.49, f32[2,90,16,720]{3,2,1,0:T(8,128)} %bitcast.50, f32[90,16,720]{2,1,0:T(8,128)} %bitcast.68, f32[90,16,720]{2,1,0:T(8,128)} %bitcast.79, f32[2,90,16,720]{3,2,1,0:T(8,128)} %bitcast.51, ...), custom_call_target="tpu_custom_call" | custom-call | flops 5000000000 | tf_op jit(solution)/shard_map/edge_columns/pallas_call | solution.py:477
  20.9 13.3 %partial_spectra.2 = (f32[2,2496,128]{2,1,0:T(8,128)}, f32[2,2336,128]{2,1,0:T(8,128)}, f32[2,1600,128]{2,1,0:T(8,128)}) custom-call(s32[11]{0:T(128)} %stack.58._.scal, f32[2,90,16,720]{3,2,1,0:T(8,128)} %bitcast.61, f32[90,16,720]{2,1,0:T(8,128)} %bitcast.74, f32[90,16,720]{2,1,0:T(8,128)} %bitcast.85, f32[4,16,720]{2,1,0:T(8,128)} %copy-done.6, ...), custom_call_target="tpu_custom_call" | custom-call | flops 5000000000 | tf_op jit(solution)/shard_map/partial_spectra/pallas_call | solution.py:417
  34.2 3.8 %collective-permute-start.9 = (f32[2,2336,128]{2,1,0:T(8,128)}, f32[2,2336,128]{2,1,0:T(8,128)}, u32[]{:S(2)}, u32[]{:S(2)}) collective-permute-start(f32[2,2336,128]{2,1,0:T(8,128)} %get-tuple-element.31), channel_id=1, source_target_pairs={{4,6},{5,7},{6,4},{7,5},{24,26},{25,27},{26,24},{27,25}} | collective-permute-start | bytes 7176200 | tf_op jit(solution)/shard_map/ppermute | solution.py:788
  38.8 2.5 %collective-permute-start.15 = (f32[2,1600,128]{2,1,0:T(8,128)}, f32[2,1600,128]{2,1,0:T(8,128)}, u32[]{:S(2)}, u32[]{:S(2)}) collective-permute-start(f32[2,1600,128]{2,1,0:T(8,128)} %get-tuple-element.33), channel_id=1, source_target_pairs={{4,12},{5,13},{6,14},{7,15},{24,16},{25,17},{26,18},{27,19}} | collective-permute-start | bytes 4915208 | tf_op jit(solution)/shard_map/ppermute | solution.py:797
  41.3 2.6 %collective-permute-start.2 = (f32[4,16,128]{2,1,0:T(8,128)S(1)}, f32[4,16,128]{2,1,0:T(8,128)S(1)}, u32[]{:S(2)}, u32[]{:S(2)}) collective-permute-start(f32[4,16,128]{2,1,0:T(8,128)S(1)} %copy-done.19), channel_id=1, source_target_pairs={{4,5},{5,6},{6,7},{7,4},{8,9},{9,10},{10,11},{11,8},{12,13},{13,14... | collective-permute-start | bytes 98312 | tf_op jit(solution)/shard_map/ppermute | solution.py:913
  43.9 13.8 %partial_spectra.3 = (f32[2,2496,128]{2,1,0:T(8,128)}, f32[2,2336,128]{2,1,0:T(8,128)}, f32[2,1600,128]{2,1,0:T(8,128)}) custom-call(s32[11]{0:T(128)} %stack.58._.scal, f32[2,90,16,720]{3,2,1,0:T(8,128)} %bitcast.62, f32[90,16,720]{2,1,0:T(8,128)} %bitcast.75, f32[90,16,720]{2,1,0:T(8,128)} %bitcast.86, f32[4,16,720]{2,1,0:T(8,128)} %copy-done.6, ...), custom_call_target="tpu_custom_call" | custom-call | flops 5000000000 | tf_op jit(solution)/shard_map/partial_spectra/pallas_call | solution.py:417
  57.7 1.4 collective-permute-start.14
  59.9 3.4 %collective-permute-start.3 = (f32[4,16,128]{2,1,0:T(8,128)S(1)}, f32[4,16,128]{2,1,0:T(8,128)S(1)}, u32[]{:S(2)}, u32[]{:S(2)}) collective-permute-start(f32[4,16,128]{2,1,0:T(8,128)S(1)} %copy-done.18), channel_id=1, source_target_pairs={{5,4},{6,5},{7,6},{4,7},{9,8},{10,9},{11,10},{8,11},{13,12},{14,13... | collective-permute-start | bytes 98312 | tf_op jit(solution)/shard_map/ppermute | solution.py:914
  63.3 3.7 %collective-permute-done.3.east = f32[4,16,128]{2,1,0:T(8,128)S(1)} collective-permute-done((f32[4,16,128]{2,1,0:T(8,128)S(1)}, f32[4,16,128]{2,1,0:T(8,128)S(1)}, u32[]{:S(2)}, u32[]{:S(2)}) %collective-permute-start.3) | collective-permute-done | bytes 32800 | tf_op jit(solution)/shard_map/ppermute | solution.py:914
  67.0 1.9 fusion.3
  68.9 2.5 %collective-permute-start.10 = (f32[2336,128]{1,0:T(8,128)S(1)}, f32[2336,128]{1,0:T(8,128)S(1)}, u32[]{:S(2)}, u32[]{:S(2)}) collective-permute-start(f32[2336,128]{1,0:T(8,128)S(1)} %fusion.3), channel_id=1, source_target_pairs={{4,5},{5,4},{6,7},{7,6},{24,25},{25,24},{26,27},{27,26}} | collective-permute-start | bytes 3588104 | tf_op jit(solution)/shard_map/ppermute | solution.py:788
  73.8 4.1 %collective-permute-done.14 = f32[2,1600,128]{2,1,0:T(8,128)S(1)} collective-permute-done((f32[2,1600,128]{2,1,0:T(8,128)}, f32[2,1600,128]{2,1,0:T(8,128)S(1)}, u32[]{:S(2)}, u32[]{:S(2)}) %collective-permute-start.14) | collective-permute-done | bytes 1638432 | tf_op jit(solution)/shard_map/ppermute | solution.py:797
  78.9 8.4 %collective-permute-done.10 = f32[2336,128]{1,0:T(8,128)S(1)} collective-permute-done((f32[2336,128]{1,0:T(8,128)S(1)}, f32[2336,128]{1,0:T(8,128)S(1)}, u32[]{:S(2)}, u32[]{:S(2)}) %collective-permute-start.10) | collective-permute-done | bytes 1196064 | tf_op jit(solution)/shard_map/ppermute | solution.py:788
  87.2 1.5 fusion.5.refs_12_
  88.7 3.0 %collective-permute-start.12 = (f32[2336,128]{1,0:T(8,128)S(1)}, f32[2336,128]{1,0:T(8,128)S(1)}, u32[]{:S(2)}, u32[]{:S(2)}) collective-permute-start(f32[2336,128]{1,0:T(8,128)S(1)} %fusion.5.refs_12_), channel_id=1, source_target_pairs={{4,6},{5,7},{6,4},{7,5},{24,26},{25,27},{26,24},{27,25}} | collective-permute-start | bytes 3588104 | tf_op jit(solution)/shard_map/ppermute | solution.py:788
  91.7 2.2 %collective-permute-start.11 = (f32[2336,128]{1,0:T(8,128)S(1)}, f32[2336,128]{1,0:T(8,128)S(1)}, u32[]{:S(2)}, u32[]{:S(2)}) collective-permute-start(f32[2336,128]{1,0:T(8,128)S(1)} %fusion.5.refs_12_), channel_id=1, source_target_pairs={{4,5},{5,4},{6,7},{7,6},{24,25},{25,24},{26,27},{27,26}} | collective-permute-start | bytes 3588104 | tf_op jit(solution)/shard_map/ppermute | solution.py:788
  95.2 1.6 collective-permute-start.19
  96.8 1.7 collective-permute-start.6
  98.5 20.3 %collective-permute-done.12.refs_14_ = f32[2336,128]{1,0:T(8,128)S(1)} collective-permute-done((f32[2336,128]{1,0:T(8,128)S(1)}, f32[2336,128]{1,0:T(8,128)S(1)}, u32[]{:S(2)}, u32[]{:S(2)}) %collective-permute-start.12) | collective-permute-done | bytes 1196064 | tf_op jit(solution)/shard_map/ppermute | solution.py:788
  118.9 1.6 collective-permute-start.21
  120.5 2.1 collective-permute-done.11.refs_13_
  123.8 1.6 collective-permute-start.23
  125.4 1.7 collective-permute-start.8
  127.2 3.1 %collective-permute-start.13 = (f32[2336,128]{1,0:T(8,128)}, f32[2336,128]{1,0:T(8,128)}, u32[]{:S(2)}, u32[]{:S(2)}) collective-permute-start(f32[2336,128]{1,0:T(8,128)} %copy-done.10), channel_id=1, source_target_pairs={{4,6},{5,7},{6,4},{7,5},{24,26},{25,27},{26,24},{27,25}} | collective-permute-start | bytes 3588104 | tf_op jit(solution)/shard_map/ppermute | solution.py:788
  130.3 6.5 %collective-permute-done.18.refs_16_ = f32[1600,128]{1,0:T(8,128)} collective-permute-done((f32[1600,128]{1,0:T(8,128)S(1)}, f32[1600,128]{1,0:T(8,128)}, u32[]{:S(2)}, u32[]{:S(2)}) %collective-permute-start.18) | collective-permute-done | bytes 819232 | tf_op jit(solution)/shard_map/ppermute | solution.py:797
  138.2 1.3 collective-permute-start.22
  142.0 18.1 %collective-permute-done.22.refs_18_ = f32[1600,128]{1,0:T(8,128)S(1)} collective-permute-done((f32[1600,128]{1,0:T(8,128)}, f32[1600,128]{1,0:T(8,128)S(1)}, u32[]{:S(2)}, u32[]{:S(2)}) %collective-permute-start.22) | collective-permute-done | bytes 819232 | tf_op jit(solution)/shard_map/ppermute | solution.py:797
  160.1 8.9 %collective-permute-done.24.refs_19_ = f32[1600,128]{1,0:T(8,128)} collective-permute-done((f32[1600,128]{1,0:T(8,128)}, f32[1600,128]{1,0:T(8,128)}, u32[]{:S(2)}, u32[]{:S(2)}) %collective-permute-start.24) | collective-permute-done | bytes 819232 | tf_op jit(solution)/shard_map/ppermute | solution.py:797
  170.1 39.1 %inverse_and_substep.1 = (f32[2,90,16,720]{3,2,1,0:T(8,128)}, f32[90,16,720]{2,1,0:T(8,128)}, f32[90,16,720]{2,1,0:T(8,128)}) custom-call(s32[11]{0:T(128)} %stack.58._.scal, f32[540]{0:T(1024)} %concatenate.3.coef, f32[4,16,128]{2,1,0:T(8,128)} %copy-done.13, f32[4,16,128]{2,1,0:T(8,128)} %copy-done.14, f32[4,16,720]{2,1,0:T(8,128)} %copy-done.6, ...), custom_call_target="tpu_custom_call" | custom-call | flops 9286189056 | bytes 40000000 | tf_op jit(solution)/shard_map/inverse_and_substep/pallas_call | solution.py:755
  (86 shorter events, 16.1 us)
Async XLA Ops:
  2.4 17.1 %collective-permute-start = (f32[4,16,720]{2,1,0:T(8,128)S(1)}, f32[4,16,720]{2,1,0:T(8,128)S(1)}, u32[]{:S(2)}, u32[]{:S(2)}) collective-permute-start(f32[4,16,720]{2,1,0:T(8,128)S(1)} %pad_maximum_fusion), channel_id=1, source_target_pairs={{0,4},{1,5},{2,6},{3,7},{4,8},{5,9},{6,10},{7,11},{8,12},{9,13},{1... | collective-permute-start | bytes 552968 | tf_op jit(solution)/shard_map/ppermute | solution.py:885
  4.4 15.2 %collective-permute-start.1 = (f32[4,16,720]{2,1,0:T(8,128)S(1)}, f32[4,16,720]{2,1,0:T(8,128)S(1)}, u32[]{:S(2)}, u32[]{:S(2)}) collective-permute-start(f32[4,16,720]{2,1,0:T(8,128)S(1)} %pad_maximum_fusion.1), channel_id=1, source_target_pairs={{4,0},{5,1},{6,2},{7,3},{8,4},{9,5},{10,6},{11,7},{12,8},{13,9},{1... | collective-permute-start | bytes 552968 | tf_op jit(solution)/shard_map/ppermute | solution.py:886
  19.5 21.8 %copy-start.19 = (f32[4,16,128]{2,1,0:T(8,128)S(1)}, f32[4,16,128]{2,1,0:T(8,128)}, u32[]{:S(2)}) copy-start(f32[4,16,128]{2,1,0:T(8,128)} %get-tuple-element.26) | copy-start | bytes 98308
  34.2 32.8 %collective-permute-start.9 = (f32[2,2336,128]{2,1,0:T(8,128)}, f32[2,2336,128]{2,1,0:T(8,128)}, u32[]{:S(2)}, u32[]{:S(2)}) collective-permute-start(f32[2,2336,128]{2,1,0:T(8,128)} %get-tuple-element.31), channel_id=1, source_target_pairs={{4,6},{5,7},{6,4},{7,5},{24,26},{25,27},{26,24},{27,25}} | collective-permute-start | bytes 7176200 | tf_op jit(solution)/shard_map/ppermute | solution.py:788
  38.0 33.5 %collective-permute-start.4 = (f32[2,2496,128]{2,1,0:T(8,128)}, f32[2,2496,128]{2,1,0:T(8,128)S(1)}, u32[]{:S(2)}, u32[]{:S(2)}) collective-permute-start(f32[2,2496,128]{2,1,0:T(8,128)} %get-tuple-element.22), channel_id=1, source_target_pairs={{0,1},{1,0},{2,3},{3,2},{28,29},{29,28},{30,31},{31,30}} | collective-permute-start | bytes 7667720 | tf_op jit(solution)/shard_map/ppermute | solution.py:788
  38.8 20.2 %collective-permute-start.15 = (f32[2,1600,128]{2,1,0:T(8,128)}, f32[2,1600,128]{2,1,0:T(8,128)}, u32[]{:S(2)}, u32[]{:S(2)}) collective-permute-start(f32[2,1600,128]{2,1,0:T(8,128)} %get-tuple-element.33), channel_id=1, source_target_pairs={{4,12},{5,13},{6,14},{7,15},{24,16},{25,17},{26,18},{27,19}} | collective-permute-start | bytes 4915208 | tf_op jit(solution)/shard_map/ppermute | solution.py:797
  41.3 18.5 %copy-start.18 = (f32[4,16,128]{2,1,0:T(8,128)S(1)}, f32[4,16,128]{2,1,0:T(8,128)}, u32[]{:S(2)}) copy-start(f32[4,16,128]{2,1,0:T(8,128)} %get-tuple-element.20) | copy-start | bytes 98308
  41.3 18.5 %collective-permute-start.2 = (f32[4,16,128]{2,1,0:T(8,128)S(1)}, f32[4,16,128]{2,1,0:T(8,128)S(1)}, u32[]{:S(2)}, u32[]{:S(2)}) collective-permute-start(f32[4,16,128]{2,1,0:T(8,128)S(1)} %copy-done.19), channel_id=1, source_target_pairs={{4,5},{5,6},{6,7},{7,4},{8,9},{9,10},{10,11},{11,8},{12,13},{13,14... | collective-permute-start | bytes 98312 | tf_op jit(solution)/shard_map/ppermute | solution.py:913
  57.7 20.2 %collective-permute-start.14 = (f32[2,1600,128]{2,1,0:T(8,128)}, f32[2,1600,128]{2,1,0:T(8,128)S(1)}, u32[]{:S(2)}, u32[]{:S(2)}) collective-permute-start(f32[2,1600,128]{2,1,0:T(8,128)} %get-tuple-element.32), channel_id=1, source_target_pairs={{4,12},{5,13},{6,14},{7,15},{24,16},{25,17},{26,18},{27,19}} | collective-permute-start | bytes 4915208 | tf_op jit(solution)/shard_map/ppermute | solution.py:797
  59.1 18.8 %collective-permute-start.16 = (f32[2,1600,128]{2,1,0:T(8,128)}, f32[2,1600,128]{2,1,0:T(8,128)S(1)}, u32[]{:S(2)}, u32[]{:S(2)}) collective-permute-start(f32[2,1600,128]{2,1,0:T(8,128)} %collective-permute-done.15), channel_id=1, source_target_pairs={{12,14},{13,15},{14,12},{15,13},{16,18},{17,19},{18,16},{19,17}} | collective-permute-start | bytes 4915208 | tf_op jit(solution)/shard_map/ppermute | solution.py:788
  59.9 7.1 %collective-permute-start.3 = (f32[4,16,128]{2,1,0:T(8,128)S(1)}, f32[4,16,128]{2,1,0:T(8,128)S(1)}, u32[]{:S(2)}, u32[]{:S(2)}) collective-permute-start(f32[4,16,128]{2,1,0:T(8,128)S(1)} %copy-done.18), channel_id=1, source_target_pairs={{5,4},{6,5},{7,6},{4,7},{9,8},{10,9},{11,10},{8,11},{13,12},{14,13... | collective-permute-start | bytes 98312 | tf_op jit(solution)/shard_map/ppermute | solution.py:914
  68.9 18.3 %collective-permute-start.10 = (f32[2336,128]{1,0:T(8,128)S(1)}, f32[2336,128]{1,0:T(8,128)S(1)}, u32[]{:S(2)}, u32[]{:S(2)}) collective-permute-start(f32[2336,128]{1,0:T(8,128)S(1)} %fusion.3), channel_id=1, source_target_pairs={{4,5},{5,4},{6,7},{7,6},{24,25},{25,24},{26,27},{27,26}} | collective-permute-start | bytes 3588104 | tf_op jit(solution)/shard_map/ppermute | solution.py:788
  72.9 21.0 %collective-permute-start.5 = (f32[2496,128]{1,0:T(8,128)S(1)}, f32[2496,128]{1,0:T(8,128)S(1)}, u32[]{:S(2)}, u32[]{:S(2)}) collective-permute-start(f32[2496,128]{1,0:T(8,128)S(1)} %fusion), channel_id=1, source_target_pairs={{0,2},{1,3},{2,0},{3,1},{28,30},{29,31},{30,28},{31,29}} | collective-permute-start | bytes 3833864 | tf_op jit(solution)/shard_map/ppermute | solution.py:788
  78.0 17.1 %collective-permute-start.17 = (f32[1600,128]{1,0:T(8,128)S(1)}, f32[1600,128]{1,0:T(8,128)S(1)}, u32[]{:S(2)}, u32[]{:S(2)}) collective-permute-start(f32[1600,128]{1,0:T(8,128)S(1)} %fusion.6), channel_id=1, source_target_pairs={{12,13},{13,12},{14,15},{15,14},{16,17},{17,16},{18,19},{19,18}} | collective-permute-start | bytes 2457608 | tf_op jit(solution)/shard_map/ppermute | solution.py:788
  88.7 30.1 %collective-permute-start.12 = (f32[2336,128]{1,0:T(8,128)S(1)}, f32[2336,128]{1,0:T(8,128)S(1)}, u32[]{:S(2)}, u32[]{:S(2)}) collective-permute-start(f32[2336,128]{1,0:T(8,128)S(1)} %fusion.5.refs_12_), channel_id=1, source_target_pairs={{4,6},{5,7},{6,4},{7,5},{24,26},{25,27},{26,24},{27,25}} | collective-permute-start | bytes 3588104 | tf_op jit(solution)/shard_map/ppermute | solution.py:788
  91.7 30.8 %collective-permute-start.11 = (f32[2336,128]{1,0:T(8,128)S(1)}, f32[2336,128]{1,0:T(8,128)S(1)}, u32[]{:S(2)}, u32[]{:S(2)}) collective-permute-start(f32[2336,128]{1,0:T(8,128)S(1)} %fusion.5.refs_12_), channel_id=1, source_target_pairs={{4,5},{5,4},{6,7},{7,6},{24,25},{25,24},{26,27},{27,26}} | collective-permute-start | bytes 3588104 | tf_op jit(solution)/shard_map/ppermute | solution.py:788
  94.1 31.3 %copy-start = (f32[2496,128]{1,0:T(8,128)}, f32[2496,128]{1,0:T(8,128)S(1)}, u32[]{:S(2)}) copy-start(f32[2496,128]{1,0:T(8,128)S(1)} %fusion.2.refs_8_) | copy-start | bytes 3833860
  94.2 33.0 %copy-start.17 = (s32[2,2,92]{2,1,0:T(2,128)S(1)}, s32[2,2,92]{2,1,0:T(2,128)}, u32[]{:S(2)}) copy-start(s32[2,2,92]{2,1,0:T(2,128)} %constant.88.clone) | copy-start | bytes 4420
  94.2 36.1 %copy-start.16 = (s32[240]{0:T(256)S(1)}, s32[240]{0:T(256)}, u32[]{:S(2)}) copy-start(s32[240]{0:T(256)} %param.14) | copy-start | bytes 2884
  94.2 46.6 %copy-start.15 = (s32[240]{0:T(256)S(1)}, s32[240]{0:T(256)}, u32[]{:S(2)}) copy-start(s32[240]{0:T(256)} %param.13) | copy-start | bytes 2884
  94.2 31.2 %collective-permute-start.7 = (f32[2496,128]{1,0:T(8,128)S(1)}, f32[2496,128]{1,0:T(8,128)S(1)}, u32[]{:S(2)}, u32[]{:S(2)}) collective-permute-start(f32[2496,128]{1,0:T(8,128)S(1)} %fusion.2.refs_8_), channel_id=1, source_target_pairs={{0,2},{1,3},{2,0},{3,1},{28,30},{29,31},{30,28},{31,29}} | collective-permute-start | bytes 3833864 | tf_op jit(solution)/shard_map/ppermute | solution.py:788
  95.2 28.6 %collective-permute-start.19 = (f32[1600,128]{1,0:T(8,128)S(1)}, f32[1600,128]{1,0:T(8,128)}, u32[]{:S(2)}, u32[]{:S(2)}) collective-permute-start(f32[1600,128]{1,0:T(8,128)S(1)} %fusion.8), channel_id=1, source_target_pairs={{12,13},{13,12},{14,15},{15,14},{16,17},{17,16},{18,19},{19,18}} | collective-permute-start | bytes 2457608 | tf_op jit(solution)/shard_map/ppermute | solution.py:788
  96.8 41.3 %collective-permute-start.6 = (f32[2496,128]{1,0:T(8,128)S(1)}, f32[2496,128]{1,0:T(8,128)}, u32[]{:S(2)}, u32[]{:S(2)}) collective-permute-start(f32[2496,128]{1,0:T(8,128)S(1)} %fusion.2.refs_8_), channel_id=1, source_target_pairs={{0,1},{1,0},{2,3},{3,2},{28,29},{29,28},{30,31},{31,30}} | collective-permute-start | bytes 3833864 | tf_op jit(solution)/shard_map/ppermute | solution.py:788
  118.9 8.3 %collective-permute-start.21 = (f32[1600,128]{1,0:T(8,128)S(1)}, f32[1600,128]{1,0:T(8,128)}, u32[]{:S(2)}, u32[]{:S(2)}) collective-permute-start(f32[1600,128]{1,0:T(8,128)S(1)} %fusion.8), channel_id=1, source_target_pairs={{12,14},{13,15},{14,12},{15,13},{16,18},{17,19},{18,16},{19,17}} | collective-permute-start | bytes 2457608 | tf_op jit(solution)/shard_map/ppermute | solution.py:788
  122.5 14.3 %collective-permute-start.18 = (f32[1600,128]{1,0:T(8,128)S(1)}, f32[1600,128]{1,0:T(8,128)}, u32[]{:S(2)}, u32[]{:S(2)}) collective-permute-start(f32[1600,128]{1,0:T(8,128)S(1)} %fusion.8), channel_id=1, source_target_pairs={{12,4},{13,5},{14,6},{15,7},{16,24},{17,25},{18,26},{19,27}} | collective-permute-start | bytes 2457608 | tf_op jit(solution)/shard_map/ppermute | solution.py:797
  123.8 15.6 %collective-permute-start.23 = (f32[1600,128]{1,0:T(8,128)}, f32[1600,128]{1,0:T(8,128)}, u32[]{:S(2)}, u32[]{:S(2)}) collective-permute-start(f32[1600,128]{1,0:T(8,128)} %collective-permute-done.19), channel_id=1, source_target_pairs={{12,14},{13,15},{14,12},{15,13},{16,18},{17,19},{18,16},{19,17}} | collective-permute-start | bytes 2457608 | tf_op jit(solution)/shard_map/ppermute | solution.py:788
  125.4 44.7 %copy-start.8 = (f32[2496,128]{1,0:T(8,128)}, f32[2496,128]{1,0:T(8,128)S(1)}, u32[]{:S(2)}) copy-start(f32[2496,128]{1,0:T(8,128)S(1)} %collective-permute-done.7.refs_10_) | copy-start | bytes 3833860
  125.4 34.7 %collective-permute-start.8 = (f32[2496,128]{1,0:T(8,128)S(1)}, f32[2496,128]{1,0:T(8,128)}, u32[]{:S(2)}, u32[]{:S(2)}) collective-permute-start(f32[2496,128]{1,0:T(8,128)S(1)} %collective-permute-done.7.refs_10_), channel_id=1, source_target_pairs={{0,1},{1,0},{2,3},{3,2},{28,29},{29,28},{30,31},{31,30}} | collective-permute-start | bytes 3833864 | tf_op jit(solution)/shard_map/ppermute | solution.py:788
  127.2 32.9 %collective-permute-start.13 = (f32[2336,128]{1,0:T(8,128)}, f32[2336,128]{1,0:T(8,128)}, u32[]{:S(2)}, u32[]{:S(2)}) collective-permute-start(f32[2336,128]{1,0:T(8,128)} %copy-done.10), channel_id=1, source_target_pairs={{4,6},{5,7},{6,4},{7,5},{24,26},{25,27},{26,24},{27,25}} | collective-permute-start | bytes 3588104 | tf_op jit(solution)/shard_map/ppermute | solution.py:788
  136.9 23.2 %collective-permute-start.20 = (f32[1600,128]{1,0:T(8,128)}, f32[1600,128]{1,0:T(8,128)S(1)}, u32[]{:S(2)}, u32[]{:S(2)}) collective-permute-start(f32[1600,128]{1,0:T(8,128)} %collective-permute-done.19), channel_id=1, source_target_pairs={{12,4},{13,5},{14,6},{15,7},{16,24},{17,25},{18,26},{19,27}} | collective-permute-start | bytes 2457608 | tf_op jit(solution)/shard_map/ppermute | solution.py:797
  138.2 21.9 %collective-permute-start.22 = (f32[1600,128]{1,0:T(8,128)}, f32[1600,128]{1,0:T(8,128)S(1)}, u32[]{:S(2)}, u32[]{:S(2)}) collective-permute-start(f32[1600,128]{1,0:T(8,128)} %collective-permute-done.21), channel_id=1, source_target_pairs={{12,4},{13,5},{14,6},{15,7},{16,24},{17,25},{18,26},{19,27}} | collective-permute-start | bytes 2457608 | tf_op jit(solution)/shard_map/ppermute | solution.py:797
  139.5 29.5 %collective-permute-start.24 = (f32[1600,128]{1,0:T(8,128)}, f32[1600,128]{1,0:T(8,128)}, u32[]{:S(2)}, u32[]{:S(2)}) collective-permute-start(f32[1600,128]{1,0:T(8,128)} %collective-permute-done.23), channel_id=1, source_target_pairs={{12,4},{13,5},{14,6},{15,7},{16,24},{17,25},{18,26},{19,27}} | collective-permute-start | bytes 2457608 | tf_op jit(solution)/shard_map/ppermute | solution.py:797
  (13 other events, 78.9 us)

commit v2 on v1

--- a/solution.py
+++ b/solution.py
@@ -146,28 +146,37 @@
         home = [g for g in indices if g != away]
         return [home] if away is None else [home, [away]]
 
+    def stores(self):
+        result = []
+        for at in range(len(self.roles)):
+            size = self.height_of(at, 0)
+            for store in result:
+                sizes = [self.height_of(*member) for member in store]
+                if self.parts == 1 and max(sizes + [size]) <= 1.1 * min(sizes + [size]):
+                    store.append((at, 0))
+                    break
+            else:
+                result.append([(at, 0)])
+        return result + [[(at, 1)] for at in self.lent]
+
     def arrays(self):
-        held = [(at, parcel) for at in range(len(self.roles)) for parcel in range(len(self.parcels(at)))]
-        return [[key + (which,) for key in held] for which in range(2)]
+        return [[(store, which) for store in range(len(self.stores()))] for which in range(2)]
 
     def places(self):
-        result, number = {}, 0
-        for at in range(len(self.roles)):
-            for parcel in self.parcels(at):
+        result = {}
+        for number, store in enumerate(self.stores()):
+            for at, parcel in store:
                 offset = 0
-                for g in parcel:
+                for g in self.parcels(at)[parcel]:
                     result[at, g] = (number, offset)
                     offset += self.roles[at][g].total
-                number += 1
         return result
 
     def height_of(self, at, parcel):
         return sum(self.roles[at][g].total for g in self.parcels(at)[parcel])
 
     def heights(self):
-        return [
-            self.height_of(at, parcel) for at in range(len(self.roles)) for parcel in range(len(self.parcels(at)))
-        ]
+        return [max(self.height_of(*member) for member in store) for store in self.stores()]
 
     def slot_rows(self):
         table = np.full((len(self.roles), 2, self.slots), -1, np.int32)
@@ -256,16 +265,13 @@
 
         @pl.when(scal[2] == at)
         def _(at=at, groups=groups):
-            mine = [(number, array[1:]) for number, array in enumerate(arrays) if array[0] == at]
-            order = [g for g in range(len(groups)) if any(g in plan.parcels(at)[a[0]] for _, a in mine)]
             targets = {}
-            for g in order:
-                targets[g] = [
-                    (number, i, u)
-                    for number, (parcel, which) in mine
-                    if g in plan.parcels(at)[parcel]
-                    for i, u in enumerate(sets[which][at])
-                ]
+            for g in range(len(groups)):
+                number, which = next(
+                    (n, array[1]) for n, array in enumerate(arrays) if array[0] == places[at, g][0]
+                )
+                targets[g] = [(number, i, u) for i, u in enumerate(sets[which][at])]
+            order = list(range(len(groups)))
             some_fields = {g: [u ^ scal[0] for _, _, u in targets[g]] for g in order}
             turn_of = {g: n % 2 for n, g in enumerate(order)}
             ready = 0
@@ -409,7 +415,7 @@
 def forward(plan, call, scal, winds, theta, thick, top, bottom, tabs):
     arrays = plan.arrays()[call]
     count = FIELDS // 2
-    shapes = [(FIELDS // 2, plan.height_of(at, parcel), LANES) for at, parcel, _ in arrays]
+    shapes = [(FIELDS // 2, plan.heights()[store], LANES) for store, _ in arrays]
     anywhere = pl.BlockSpec(memory_space=pl.ANY)
     halo = pl.BlockSpec((FIELDS, plan.levels, plan.width), lambda i, s: (0, 0, 0))
     slots = max(group.slots for groups in plan.roles for group in groups)
@@ -497,6 +503,7 @@
     last_step = rows // step_rows
 
     def inverse(at, groups):
+        source = [0, 1, 2, 3] if plan.parts > 1 or at % 2 == 0 else [0, 2, 1, 3]
         slot_at = np.cumsum([0] + [group.slots for group in groups])
         row_at = np.cumsum([0] + [group.total for group in groups])
 
@@ -504,7 +511,7 @@
             number, offset = places[at, g]
             return [
                 pltpu.make_async_copy(
-                    spectra[number * FIELDS + u].at[pl.ds(offset, groups[g].total)],
+                    spectra[number * FIELDS + source[u]].at[pl.ds(offset, groups[g].total)],
                     sums.at[u, pl.ds(int(row_at[g]), groups[g].total)],
                     sems.at[g, u],
                 )
@@ -706,7 +713,7 @@
 
     @pl.when(step > 0)
     def _():
-        lax.fori_loop(0, step_rows, stencil, 0, unroll=3 if step_rows % 3 == 0 else 1)
+        lax.fori_loop(0, step_rows, stencil, 0, unroll=5 if step_rows % 5 == 0 else 1)
         leave(step, PIECE if step_rows % PIECE == 0 else step_rows, lambda copy: copy.start())
 
     @pl.when(step == last_step)
@@ -779,9 +786,10 @@
     )(scal, coef, west, east, top, bottom, cuts, *tabs, *raw, *spectra)
 
 
-def lon_swap(plan, value, blocks, bit):
+def lon_swap(plan, value, moves):
     pairs = [
         (block * plan.lon + place, block * plan.lon + (place ^ (1 << bit)))
+        for blocks, bit in moves
         for block in blocks
         for place in range(plan.lon)
     ]
@@ -797,20 +805,17 @@
     return lax.ppermute(value, ("lat", "lon"), pairs)
 
 
-def spread(plan, blocks, slots, order):
-    for bit in reversed(order):
-        for s in sorted(slots):
-            slots[s | (1 << bit)] = lon_swap(plan, slots[s], blocks, bit)
-    return slots
-
-
 def gather_sums(plan, blocks, slots, order):
     slots = dict(slots)
     for bit in order:
         sent = [s for s in slots if s >> bit & 1]
         for s in sorted(sent, key=lambda s: -bin(s).count("1")):
-            slots[s ^ (1 << bit)] = slots[s ^ (1 << bit)] + lon_swap(plan, slots.pop(s), blocks, bit)
-    return spread(plan, blocks, slots, order)
+            moved = lon_swap(plan, slots.pop(s), [(blocks, bit)])
+            slots[s ^ (1 << bit)] = slots[s ^ (1 << bit)] + moved
+    for bit in reversed(order):
+        for s in sorted(slots):
+            slots[s | (1 << bit)] = lon_swap(plan, slots[s], [(blocks, bit)])
+    return slots
 
 
 def field_sets(plan):
@@ -822,16 +827,19 @@
     return sent, kept
 
 
-def parcel_sums(plan, place, at, blocks, sent, kept):
+def store_sums(plan, members, sent, kept):
+    near = [(blocks, bit) for blocks, bit in members]
+    far = [(blocks, 1 - bit) for blocks, bit in members]
+    moved = lon_swap(plan, sent, near)
+    own = (kept[0] + moved[0]) + lon_swap(plan, kept[1] + moved[1], far)
+    across = lon_swap(plan, own, far)
+    beside = lon_swap(plan, own, near)
+    return own, beside, across, lon_swap(plan, across, near)
+
+
+def split_sums(plan, place, at, sent, kept):
     first, second = field_sets(plan)
     parts, own = plan.parts, place % plan.parts
-    if parts == 1:
-        near, far = at % 2, 1 - at % 2
-        moved = lon_swap(plan, sent, blocks, near)
-        send = kept[1] + moved[1]
-        slots = {0: (kept[0] + moved[0]) + lon_swap(plan, send, blocks, far)}
-        slots = spread(plan, blocks, slots, [near, far])
-        return [slots[u] for u in range(FIELDS)]
     bits = plan.lon.bit_length() - 1
     slots = {}
     for us, array in ((first[at], sent), (second[at], kept)):
@@ -840,7 +848,7 @@
             for k in range(parts):
                 slots[u * parts + k] = pieces[k ^ own]
     order = list(range(bits)) if at % 2 == 0 else list(reversed(range(bits)))
-    slots = gather_sums(plan, blocks, slots, order)
+    slots = gather_sums(plan, plan.blocks(at), slots, order)
     result = []
     for u in range(FIELDS):
         pieces = jnp.stack([slots[u * parts + k] for k in range(parts)])
@@ -850,17 +858,19 @@
 
 def all_sums(plan, place, arrays):
     result = []
-    for at in range(len(plan.roles)):
-        home = plan.blocks(at)
-        for parcel in range(len(plan.parcels(at))):
-            first, second = arrays[at, parcel, 0], arrays[at, parcel, 1]
-            if parcel == 0:
-                result += parcel_sums(plan, place, at, home, first, second)
-                continue
-            helpers = plan.blocks(at + len(plan.roles))
+    for number, store in enumerate(plan.stores()):
+        first, second = arrays[number, 0], arrays[number, 1]
+        if plan.parts > 1:
+            result += split_sums(plan, place, store[0][0], first, second)
+        elif store[0][1] == 0:
+            result += store_sums(plan, [(plan.blocks(at), at % 2) for at, _ in store], first, second)
+        else:
+            at = store[0][0]
+            home, helpers = plan.blocks(at), plan.blocks(at + len(plan.roles))
             first, second = [lat_move(plan, array, home, helpers) for array in (first, second)]
-            sums = parcel_sums(plan, place, at, helpers, first, second)
-            result += [lat_move(plan, array, helpers, home) for array in sums]
+            own, near, far, both = store_sums(plan, [(helpers, at % 2)], first, second)
+            own, far = lax.optimization_barrier((own, far))
+            result += [lat_move(plan, array, helpers, home) for array in (own, near, far, both)]
     return result
 
 
@@ -917,7 +927,7 @@
     arrays = forward(plan, 0, scal, winds, theta, thick, top, bottom, t_tabs)
     scal, _ = lax.optimization_barrier((scal, arrays[plan.arrays()[0][0]]))
     later = forward(plan, 1, scal, winds, theta, thick, top, bottom, t_tabs)
-    added = {key: array for key, array in later.items() if key[1] == 0}
+    added = {key: array for key, array in later.items() if plan.stores()[key[0]][0][1] == 0}
     added, west, east = lax.optimization_barrier((added, west, east))
     arrays = {**arrays, **later, **added}
     sums = all_sums(plan, place, arrays)

time: 211 us -> 209 us (level)
  waiting for transfers between devices: 72.1 us -> 77.7 us
  starting transfers between devices: 47.5 us -> 42.7 us
  Pallas kernels: 72.4 us -> 70.1 us
    ppermute x15 -> x10, starting transfers between devices: 26.9 us -> 22.1 us  [lon_swap(): return lax.ppermute(value, ('lat', 'lon'), pairs)]
    ppermute x15 -> x10, waiting for transfers between devices: 30.8 us -> 34.9 us  [lon_swap(): return lax.ppermute(value, ('lat', 'lon'), pairs)]
    pallas_call x1, Pallas kernels: 39.1 us -> 36.9 us  [substep(): pl.pallas_call(functools.partial(step_kernel, plan, step_rows), grid_spec...]
  transfers between devices with their start and end apart: 25 -> 20, of which waited for: 8 -> 8; matrix products, arithmetic and copies ran while one was open for 3% -> 4% of each run, Pallas kernels for 10% -> 10%
where the time goes in v2:
time: 209 us; the launch traced here: 207 us
  waiting for transfers between devices  77.7 us (37%)
  Pallas kernels  70.1 us (34%)
  starting transfers between devices  42.7 us (20%)
  other arithmetic  5.95 us (3%)
  local copies, waits for them, and re-layouts  5.82 us (3%)
  between operations  4.54 us (2%)
    ppermute x6, waiting for transfers between devices, lat_move(): return lax.ppermute(value, ('lat', 'lon'), pairs)  39.5 us
    pallas_call x1, Pallas kernels, substep(): pl.pallas_call(functools.partial(step_kernel, plan, step_rows), grid_spec...  36.9 us
    ppermute x10, waiting for transfers between devices, lon_swap(): return lax.ppermute(value, ('lat', 'lon'), pairs)  34.9 us
    pallas_call x2, Pallas kernels, forward(): pl.pallas_call(functools.partial(forward_kernel, plan, call), grid_spec=p...  26.9 us
    ppermute x10, starting transfers between devices, lon_swap(): return lax.ppermute(value, ('lat', 'lon'), pairs)  22.1 us
    ppermute x6, starting transfers between devices, lat_move(): return lax.ppermute(value, ('lat', 'lon'), pairs)  9.2 us
    pallas_call x1, Pallas kernels, edges(): pl.pallas_call(functools.partial(edge_kernel, plan, count), grid=(1,), in...  6.25 us
    add x4, other arithmetic, store_sums(): own = kept[0] + moved[0] + lon_swap(plan, kept[1] + moved[1], far)  4.18 us
  transfers between devices with their start and end apart: 20, of which 8 were waited for; matrix products, arithmetic and copies ran while one was open for 4% of the time, Pallas kernels for 10%

profile of v2, /device:TPU:26, one launch (start us, length us, event | category | flops | bytes accessed | tf_op | source)
XLA Modules:
  0.0 206.9 jit_solution(3557240822971617755)
XLA Ops:
  2.4 1.9 collective-permute-start
  4.4 3.6 %collective-permute-start.1 = (f32[4,16,720]{2,1,0:T(8,128)S(1)}, f32[4,16,720]{2,1,0:T(8,128)S(1)}, u32[]{:S(2)}, u32[]{:S(2)}) collective-permute-start(f32[4,16,720]{2,1,0:T(8,128)S(1)} %pad_maximum_fusion.1), channel_id=1, source_target_pairs={{4,0},{5,1},{6,2},{7,3},{8,4},{9,5},{10,6},{11,7},{12,8},{13,9},{1... | collective-permute-start | bytes 552968 | tf_op jit(solution)/shard_map/ppermute | solution.py:896
  8.1 1.3 fusion.6
  13.3 6.2 %edge_columns.1 = (f32[4,16,128]{2,1,0:T(8,128)}, f32[4,16,128]{2,1,0:T(8,128)}) custom-call(s32[11]{0:T(128)} %stack.58._.scal, f32[2,90,16,720]{3,2,1,0:T(8,128)} %bitcast.43, f32[2,90,16,720]{3,2,1,0:T(8,128)} %bitcast.44, f32[90,16,720]{2,1,0:T(8,128)} %bitcast.62, f32[90,16,720]{2,1,0:T(8,128)} %bitcast.73, f32[2,90,16,720]{3,2,1,0:T(8,128)} %bitcast.45, ...), custom_call_target="tpu_custom_call" | custom-call | flops 5000000000 | tf_op jit(solution)/shard_map/edge_columns/pallas_call | solution.py:483
  20.9 13.3 %partial_spectra.2 = (f32[2,2496,128]{2,1,0:T(8,128)}, f32[2,1600,128]{2,1,0:T(8,128)}) custom-call(s32[11]{0:T(128)} %stack.58._.scal, f32[2,90,16,720]{3,2,1,0:T(8,128)} %bitcast.55, f32[90,16,720]{2,1,0:T(8,128)} %bitcast.68, f32[90,16,720]{2,1,0:T(8,128)} %bitcast.79, f32[4,16,720]{2,1,0:T(8,128)} %copy-done.3, f32[4,16,720]{2,1,0:T(8,128)} %copy-done.4, ...), custom_call_target="tpu_custom_call" | custom-call | flops 5000000000 | tf_op jit(solution)/shard_map/partial_spectra/pallas_call | solution.py:423
  34.2 3.8 %collective-permute-start.4 = (f32[2,2496,128]{2,1,0:T(8,128)}, f32[2,2496,128]{2,1,0:T(8,128)S(1)}, u32[]{:S(2)}, u32[]{:S(2)}) collective-permute-start(f32[2,2496,128]{2,1,0:T(8,128)} %get-tuple-element.21), channel_id=1, source_target_pairs={{0,1},{1,0},{2,3},{3,2},{28,29},{29,28},{30,31},{31,30},{4,6},{5,7... | collective-permute-start | bytes 7667720 | tf_op jit(solution)/shard_map/ppermute | solution.py:796
  38.0 2.6 %collective-permute-start.10 = (f32[2,1600,128]{2,1,0:T(8,128)}, f32[2,1600,128]{2,1,0:T(8,128)}, u32[]{:S(2)}, u32[]{:S(2)}) collective-permute-start(f32[2,1600,128]{2,1,0:T(8,128)} %get-tuple-element.29), channel_id=1, source_target_pairs={{4,12},{5,13},{6,14},{7,15},{24,16},{25,17},{26,18},{27,19}} | collective-permute-start | bytes 4915208 | tf_op jit(solution)/shard_map/ppermute | solution.py:805
  40.7 13.6 %partial_spectra.3 = (f32[2,2496,128]{2,1,0:T(8,128)}, f32[2,1600,128]{2,1,0:T(8,128)}) custom-call(s32[11]{0:T(128)} %stack.58._.scal, f32[2,90,16,720]{3,2,1,0:T(8,128)} %bitcast.56, f32[90,16,720]{2,1,0:T(8,128)} %bitcast.69, f32[90,16,720]{2,1,0:T(8,128)} %bitcast.80, f32[4,16,720]{2,1,0:T(8,128)} %copy-done.3, f32[4,16,720]{2,1,0:T(8,128)} %copy-done.4, ...), custom_call_target="tpu_custom_call" | custom-call | flops 5000000000 | tf_op jit(solution)/shard_map/partial_spectra/pallas_call | solution.py:423
  54.3 1.4 collective-permute-start.9
  55.7 2.7 %collective-permute-done.10 = f32[2,1600,128]{2,1,0:T(8,128)} collective-permute-done((f32[2,1600,128]{2,1,0:T(8,128)}, f32[2,1600,128]{2,1,0:T(8,128)}, u32[]{:S(2)}, u32[]{:S(2)}) %collective-permute-start.10) | collective-permute-done | bytes 1638432 | tf_op jit(solution)/shard_map/ppermute | solution.py:805
  59.2 2.4 %collective-permute-start.2 = (f32[4,16,128]{2,1,0:T(8,128)S(1)}, f32[4,16,128]{2,1,0:T(8,128)S(1)}, u32[]{:S(2)}, u32[]{:S(2)}) collective-permute-start(f32[4,16,128]{2,1,0:T(8,128)S(1)} %copy-done.13), channel_id=1, source_target_pairs={{4,5},{5,6},{6,7},{7,4},{8,9},{9,10},{10,11},{11,8},{12,13},{13,14... | collective-permute-start | bytes 98312 | tf_op jit(solution)/shard_map/ppermute | solution.py:923
  61.6 3.4 %collective-permute-start.3 = (f32[4,16,128]{2,1,0:T(8,128)S(1)}, f32[4,16,128]{2,1,0:T(8,128)S(1)}, u32[]{:S(2)}, u32[]{:S(2)}) collective-permute-start(f32[4,16,128]{2,1,0:T(8,128)S(1)} %copy-done.12), channel_id=1, source_target_pairs={{5,4},{6,5},{7,6},{4,7},{9,8},{10,9},{11,10},{8,11},{13,12},{14,13... | collective-permute-start | bytes 98312 | tf_op jit(solution)/shard_map/ppermute | solution.py:924
  65.4 2.9 %collective-permute-done.3.east = f32[4,16,128]{2,1,0:T(8,128)S(1)} collective-permute-done((f32[4,16,128]{2,1,0:T(8,128)S(1)}, f32[4,16,128]{2,1,0:T(8,128)S(1)}, u32[]{:S(2)}, u32[]{:S(2)}) %collective-permute-start.3) | collective-permute-done | bytes 32800 | tf_op jit(solution)/shard_map/ppermute | solution.py:924
  68.4 2.4 %fusion = f32[2496,128]{1,0:T(8,128)S(1)} fusion(f32[2,2496,128]{2,1,0:T(8,128)S(1)} %collective-permute-done.4, f32[2,2496,128]{2,1,0:T(8,128)} %get-tuple-element.27), kind=kLoop, calls=%fused_computation.1 | loop fusion | flops 319488 | bytes 3833856 | tf_op jit(solution)/shard_map/add | solution.py:834
  70.8 2.5 %collective-permute-start.5 = (f32[2496,128]{1,0:T(8,128)S(1)}, f32[2496,128]{1,0:T(8,128)S(1)}, u32[]{:S(2)}, u32[]{:S(2)}) collective-permute-start(f32[2496,128]{1,0:T(8,128)S(1)} %fusion), channel_id=1, source_target_pairs={{0,2},{1,3},{2,0},{3,1},{28,30},{29,31},{30,28},{31,29},{4,5},{5,4... | collective-permute-start | bytes 3833864 | tf_op jit(solution)/shard_map/ppermute | solution.py:796
  73.3 2.6 %collective-permute-done.9 = f32[2,1600,128]{2,1,0:T(8,128)S(1)} collective-permute-done((f32[2,1600,128]{2,1,0:T(8,128)}, f32[2,1600,128]{2,1,0:T(8,128)S(1)}, u32[]{:S(2)}, u32[]{:S(2)}) %collective-permute-start.9) | collective-permute-done | bytes 1638432 | tf_op jit(solution)/shard_map/ppermute | solution.py:805
  76.8 13.2 %collective-permute-done.5 = f32[2496,128]{1,0:T(8,128)S(1)} collective-permute-done((f32[2496,128]{1,0:T(8,128)S(1)}, f32[2496,128]{1,0:T(8,128)S(1)}, u32[]{:S(2)}, u32[]{:S(2)}) %collective-permute-start.5) | collective-permute-done | bytes 1277984 | tf_op jit(solution)/shard_map/ppermute | solution.py:796
  90.0 1.6 fusion.2.refs_8_
  91.6 2.6 %collective-permute-start.7 = (f32[2496,128]{1,0:T(8,128)S(1)}, f32[2496,128]{1,0:T(8,128)S(1)}, u32[]{:S(2)}, u32[]{:S(2)}) collective-permute-start(f32[2496,128]{1,0:T(8,128)S(1)} %fusion.2.refs_8_), channel_id=1, source_target_pairs={{0,2},{1,3},{2,0},{3,1},{28,30},{29,31},{30,28},{31,29},{4,5},{5,4... | collective-permute-start | bytes 3833864 | tf_op jit(solution)/shard_map/ppermute | solution.py:796
  94.4 1.6 collective-permute-start.13
  96.0 3.0 %collective-permute-start.6 = (f32[2496,128]{1,0:T(8,128)S(1)}, f32[2496,128]{1,0:T(8,128)}, u32[]{:S(2)}, u32[]{:S(2)}) collective-permute-start(f32[2496,128]{1,0:T(8,128)S(1)} %fusion.2.refs_8_), channel_id=1, source_target_pairs={{0,1},{1,0},{2,3},{3,2},{28,29},{29,28},{30,31},{31,30},{4,6},{5,7... | collective-permute-start | bytes 3833864 | tf_op jit(solution)/shard_map/ppermute | solution.py:796
  99.0 1.6 collective-permute-start.15
  100.6 1.5 collective-permute-start.18
  102.2 21.7 %collective-permute-done.7.refs_10_ = f32[2496,128]{1,0:T(8,128)S(1)} collective-permute-done((f32[2496,128]{1,0:T(8,128)S(1)}, f32[2496,128]{1,0:T(8,128)S(1)}, u32[]{:S(2)}, u32[]{:S(2)}) %collective-permute-start.7) | collective-permute-done | bytes 1277984 | tf_op jit(solution)/shard_map/ppermute | solution.py:796
  123.9 4.0 %collective-permute-start.8 = (f32[2496,128]{1,0:T(8,128)S(1)}, f32[2496,128]{1,0:T(8,128)}, u32[]{:S(2)}, u32[]{:S(2)}) collective-permute-start(f32[2496,128]{1,0:T(8,128)S(1)} %collective-permute-done.7.refs_10_), channel_id=1, source_target_pairs={{0,1},{1,0},{2,3},{3,2},{28,29},{29,28},{30,31},{31,30},{4,6},{5,7... | collective-permute-start | bytes 3833864 | tf_op jit(solution)/shard_map/ppermute | solution.py:796
  127.9 1.3 collective-permute-start.14
  129.2 1.3 collective-permute-start.17
  130.5 1.3 collective-permute-start.16
  131.9 1.3 collective-permute-start.19
  134.4 25.3 %collective-permute-done.16.refs_13_ = f32[1600,128]{1,0:T(8,128)S(1)} collective-permute-done((f32[1600,128]{1,0:T(8,128)}, f32[1600,128]{1,0:T(8,128)S(1)}, u32[]{:S(2)}, u32[]{:S(2)}) %collective-permute-start.16) | collective-permute-done | bytes 819232 | tf_op jit(solution)/shard_map/ppermute | solution.py:805
  159.7 8.9 %collective-permute-done.19.refs_15_ = f32[1600,128]{1,0:T(8,128)} collective-permute-done((f32[1600,128]{1,0:T(8,128)}, f32[1600,128]{1,0:T(8,128)}, u32[]{:S(2)}, u32[]{:S(2)}) %collective-permute-start.19) | collective-permute-done | bytes 819232 | tf_op jit(solution)/shard_map/ppermute | solution.py:805
  169.8 36.9 %inverse_and_substep.1 = (f32[2,90,16,720]{3,2,1,0:T(8,128)}, f32[90,16,720]{2,1,0:T(8,128)}, f32[90,16,720]{2,1,0:T(8,128)}) custom-call(s32[11]{0:T(128)} %stack.58._.scal, f32[540]{0:T(1024)} %concatenate.3.coef, f32[4,16,128]{2,1,0:T(8,128)} %copy-done.7, f32[4,16,128]{2,1,0:T(8,128)} %copy-done.8, f32[4,16,720]{2,1,0:T(8,128)} %copy-done.3, ...), custom_call_target="tpu_custom_call" | custom-call | flops 9286189056 | bytes 40000000 | tf_op jit(solution)/shard_map/inverse_and_substep/pallas_call | solution.py:762
  (62 shorter events, 8.3 us)
Async XLA Ops:
  2.4 17.1 %collective-permute-start = (f32[4,16,720]{2,1,0:T(8,128)S(1)}, f32[4,16,720]{2,1,0:T(8,128)S(1)}, u32[]{:S(2)}, u32[]{:S(2)}) collective-permute-start(f32[4,16,720]{2,1,0:T(8,128)S(1)} %pad_maximum_fusion), channel_id=1, source_target_pairs={{0,4},{1,5},{2,6},{3,7},{4,8},{5,9},{6,10},{7,11},{8,12},{9,13},{1... | collective-permute-start | bytes 552968 | tf_op jit(solution)/shard_map/ppermute | solution.py:895
  4.4 15.2 %collective-permute-start.1 = (f32[4,16,720]{2,1,0:T(8,128)S(1)}, f32[4,16,720]{2,1,0:T(8,128)S(1)}, u32[]{:S(2)}, u32[]{:S(2)}) collective-permute-start(f32[4,16,720]{2,1,0:T(8,128)S(1)} %pad_maximum_fusion.1), channel_id=1, source_target_pairs={{4,0},{5,1},{6,2},{7,3},{8,4},{9,5},{10,6},{11,7},{12,8},{13,9},{1... | collective-permute-start | bytes 552968 | tf_op jit(solution)/shard_map/ppermute | solution.py:896
  34.2 34.1 %collective-permute-start.4 = (f32[2,2496,128]{2,1,0:T(8,128)}, f32[2,2496,128]{2,1,0:T(8,128)S(1)}, u32[]{:S(2)}, u32[]{:S(2)}) collective-permute-start(f32[2,2496,128]{2,1,0:T(8,128)} %get-tuple-element.21), channel_id=1, source_target_pairs={{0,1},{1,0},{2,3},{3,2},{28,29},{29,28},{30,31},{31,30},{4,6},{5,7... | collective-permute-start | bytes 7667720 | tf_op jit(solution)/shard_map/ppermute | solution.py:796
  38.0 21.2 %copy-start.13 = (f32[4,16,128]{2,1,0:T(8,128)S(1)}, f32[4,16,128]{2,1,0:T(8,128)}, u32[]{:S(2)}) copy-start(f32[4,16,128]{2,1,0:T(8,128)} %get-tuple-element.24) | copy-start | bytes 98308
  38.0 23.6 %copy-start.12 = (f32[4,16,128]{2,1,0:T(8,128)S(1)}, f32[4,16,128]{2,1,0:T(8,128)}, u32[]{:S(2)}) copy-start(f32[4,16,128]{2,1,0:T(8,128)} %get-tuple-element.19) | copy-start | bytes 98308
  38.0 20.4 %collective-permute-start.10 = (f32[2,1600,128]{2,1,0:T(8,128)}, f32[2,1600,128]{2,1,0:T(8,128)}, u32[]{:S(2)}, u32[]{:S(2)}) collective-permute-start(f32[2,1600,128]{2,1,0:T(8,128)} %get-tuple-element.29), channel_id=1, source_target_pairs={{4,12},{5,13},{6,14},{7,15},{24,16},{25,17},{26,18},{27,19}} | collective-permute-start | bytes 4915208 | tf_op jit(solution)/shard_map/ppermute | solution.py:805
  54.3 21.6 %collective-permute-start.9 = (f32[2,1600,128]{2,1,0:T(8,128)}, f32[2,1600,128]{2,1,0:T(8,128)S(1)}, u32[]{:S(2)}, u32[]{:S(2)}) collective-permute-start(f32[2,1600,128]{2,1,0:T(8,128)} %get-tuple-element.28), channel_id=1, source_target_pairs={{4,12},{5,13},{6,14},{7,15},{24,16},{25,17},{26,18},{27,19}} | collective-permute-start | bytes 4915208 | tf_op jit(solution)/shard_map/ppermute | solution.py:805
  58.4 17.6 %collective-permute-start.11 = (f32[2,1600,128]{2,1,0:T(8,128)}, f32[2,1600,128]{2,1,0:T(8,128)S(1)}, u32[]{:S(2)}, u32[]{:S(2)}) collective-permute-start(f32[2,1600,128]{2,1,0:T(8,128)} %collective-permute-done.10), channel_id=1, source_target_pairs={{12,14},{13,15},{14,12},{15,13},{16,18},{17,19},{18,16},{19,17}} | collective-permute-start | bytes 4915208 | tf_op jit(solution)/shard_map/ppermute | solution.py:796
  59.2 6.2 %collective-permute-start.2 = (f32[4,16,128]{2,1,0:T(8,128)S(1)}, f32[4,16,128]{2,1,0:T(8,128)S(1)}, u32[]{:S(2)}, u32[]{:S(2)}) collective-permute-start(f32[4,16,128]{2,1,0:T(8,128)S(1)} %copy-done.13), channel_id=1, source_target_pairs={{4,5},{5,6},{6,7},{7,4},{8,9},{9,10},{10,11},{11,8},{12,13},{13,14... | collective-permute-start | bytes 98312 | tf_op jit(solution)/shard_map/ppermute | solution.py:923
  61.6 6.7 %collective-permute-start.3 = (f32[4,16,128]{2,1,0:T(8,128)S(1)}, f32[4,16,128]{2,1,0:T(8,128)S(1)}, u32[]{:S(2)}, u32[]{:S(2)}) collective-permute-start(f32[4,16,128]{2,1,0:T(8,128)S(1)} %copy-done.12), channel_id=1, source_target_pairs={{5,4},{6,5},{7,6},{4,7},{9,8},{10,9},{11,10},{8,11},{13,12},{14,13... | collective-permute-start | bytes 98312 | tf_op jit(solution)/shard_map/ppermute | solution.py:924
  65.4 5.4 %copy-start.7 = (f32[4,16,128]{2,1,0:T(8,128)}, f32[4,16,128]{2,1,0:T(8,128)S(1)}, u32[]{:S(2)}) copy-start(f32[4,16,128]{2,1,0:T(8,128)S(1)} %collective-permute-done.2.west) | copy-start | bytes 98308
  68.4 2.4 %copy-start.8 = (f32[4,16,128]{2,1,0:T(8,128)}, f32[4,16,128]{2,1,0:T(8,128)S(1)}, u32[]{:S(2)}) copy-start(f32[4,16,128]{2,1,0:T(8,128)S(1)} %collective-permute-done.3.east) | copy-start | bytes 98308
  68.4 2.4 %copy-start.1 = (f32[2,2496,128]{2,1,0:T(8,128)}, f32[2,2496,128]{2,1,0:T(8,128)S(1)}, u32[]{:S(2)}) copy-start(f32[2,2496,128]{2,1,0:T(8,128)S(1)} %collective-permute-done.4) | copy-start | bytes 7667716
  68.4 21.6 %copy-start.2 = (f32[2,2496,128]{2,1,0:T(8,128)S(1)}, f32[2,2496,128]{2,1,0:T(8,128)}, u32[]{:S(2)}) copy-start(f32[2,2496,128]{2,1,0:T(8,128)} %get-tuple-element.27) | copy-start | bytes 7667716
  70.8 19.1 %collective-permute-start.5 = (f32[2496,128]{1,0:T(8,128)S(1)}, f32[2496,128]{1,0:T(8,128)S(1)}, u32[]{:S(2)}, u32[]{:S(2)}) collective-permute-start(f32[2496,128]{1,0:T(8,128)S(1)} %fusion), channel_id=1, source_target_pairs={{0,2},{1,3},{2,0},{3,1},{28,30},{29,31},{30,28},{31,29},{4,5},{5,4... | collective-permute-start | bytes 3833864 | tf_op jit(solution)/shard_map/ppermute | solution.py:796
  76.1 18.2 %collective-permute-start.12 = (f32[1600,128]{1,0:T(8,128)S(1)}, f32[1600,128]{1,0:T(8,128)S(1)}, u32[]{:S(2)}, u32[]{:S(2)}) collective-permute-start(f32[1600,128]{1,0:T(8,128)S(1)} %fusion.3), channel_id=1, source_target_pairs={{12,13},{13,12},{14,15},{15,14},{16,17},{17,16},{18,19},{19,18}} | collective-permute-start | bytes 2457608 | tf_op jit(solution)/shard_map/ppermute | solution.py:796
  91.5 10.6 %copy-start = (f32[2496,128]{1,0:T(8,128)}, f32[2496,128]{1,0:T(8,128)S(1)}, u32[]{:S(2)}) copy-start(f32[2496,128]{1,0:T(8,128)S(1)} %fusion.2.refs_8_) | copy-start | bytes 3833860
  91.5 36.3 %copy-start.11 = (s32[2,2,92]{2,1,0:T(2,128)S(1)}, s32[2,2,92]{2,1,0:T(2,128)}, u32[]{:S(2)}) copy-start(s32[2,2,92]{2,1,0:T(2,128)} %constant.88.clone) | copy-start | bytes 4420
  91.6 36.4 %copy-start.10 = (s32[240]{0:T(256)S(1)}, s32[240]{0:T(256)}, u32[]{:S(2)}) copy-start(s32[240]{0:T(256)} %param.14) | copy-start | bytes 2884
  91.6 41.6 %copy-start.9 = (s32[240]{0:T(256)S(1)}, s32[240]{0:T(256)}, u32[]{:S(2)}) copy-start(s32[240]{0:T(256)} %param.13) | copy-start | bytes 2884
  91.6 32.3 %collective-permute-start.7 = (f32[2496,128]{1,0:T(8,128)S(1)}, f32[2496,128]{1,0:T(8,128)S(1)}, u32[]{:S(2)}, u32[]{:S(2)}) collective-permute-start(f32[2496,128]{1,0:T(8,128)S(1)} %fusion.2.refs_8_), channel_id=1, source_target_pairs={{0,2},{1,3},{2,0},{3,1},{28,30},{29,31},{30,28},{31,29},{4,5},{5,4... | collective-permute-start | bytes 3833864 | tf_op jit(solution)/shard_map/ppermute | solution.py:796
  94.4 6.3 %collective-permute-start.13 = (f32[1600,128]{1,0:T(8,128)S(1)}, f32[1600,128]{1,0:T(8,128)}, u32[]{:S(2)}, u32[]{:S(2)}) collective-permute-start(f32[1600,128]{1,0:T(8,128)S(1)} %fusion.5), channel_id=1, source_target_pairs={{12,13},{13,12},{14,15},{15,14},{16,17},{17,16},{18,19},{19,18}} | collective-permute-start | bytes 2457608 | tf_op jit(solution)/shard_map/ppermute | solution.py:796
  96.0 34.6 %collective-permute-start.6 = (f32[2496,128]{1,0:T(8,128)S(1)}, f32[2496,128]{1,0:T(8,128)}, u32[]{:S(2)}, u32[]{:S(2)}) collective-permute-start(f32[2496,128]{1,0:T(8,128)S(1)} %fusion.2.refs_8_), channel_id=1, source_target_pairs={{0,1},{1,0},{2,3},{3,2},{28,29},{29,28},{30,31},{31,30},{4,6},{5,7... | collective-permute-start | bytes 3833864 | tf_op jit(solution)/shard_map/ppermute | solution.py:796
  99.0 30.3 %collective-permute-start.15 = (f32[1600,128]{1,0:T(8,128)S(1)}, f32[1600,128]{1,0:T(8,128)}, u32[]{:S(2)}, u32[]{:S(2)}) collective-permute-start(f32[1600,128]{1,0:T(8,128)S(1)} %fusion.5), channel_id=1, source_target_pairs={{12,14},{13,15},{14,12},{15,13},{16,18},{17,19},{18,16},{19,17}} | collective-permute-start | bytes 2457608 | tf_op jit(solution)/shard_map/ppermute | solution.py:796
  100.6 31.2 %collective-permute-start.18 = (f32[1600,128]{1,0:T(8,128)}, f32[1600,128]{1,0:T(8,128)}, u32[]{:S(2)}, u32[]{:S(2)}) collective-permute-start(f32[1600,128]{1,0:T(8,128)} %collective-permute-done.13), channel_id=1, source_target_pairs={{12,14},{13,15},{14,12},{15,13},{16,18},{17,19},{18,16},{19,17}} | collective-permute-start | bytes 2457608 | tf_op jit(solution)/shard_map/ppermute | solution.py:796
  123.9 45.9 %copy-start.5 = (f32[2496,128]{1,0:T(8,128)}, f32[2496,128]{1,0:T(8,128)S(1)}, u32[]{:S(2)}) copy-start(f32[2496,128]{1,0:T(8,128)S(1)} %collective-permute-done.7.refs_10_) | copy-start | bytes 3833860
  123.9 35.8 %collective-permute-start.8 = (f32[2496,128]{1,0:T(8,128)S(1)}, f32[2496,128]{1,0:T(8,128)}, u32[]{:S(2)}, u32[]{:S(2)}) collective-permute-start(f32[2496,128]{1,0:T(8,128)S(1)} %collective-permute-done.7.refs_10_), channel_id=1, source_target_pairs={{0,1},{1,0},{2,3},{3,2},{28,29},{29,28},{30,31},{31,30},{4,6},{5,7... | collective-permute-start | bytes 3833864 | tf_op jit(solution)/shard_map/ppermute | solution.py:796
  127.9 31.8 %collective-permute-start.14 = (f32[1600,128]{1,0:T(8,128)S(1)}, f32[1600,128]{1,0:T(8,128)}, u32[]{:S(2)}, u32[]{:S(2)}) collective-permute-start(f32[1600,128]{1,0:T(8,128)S(1)} %fusion.5), channel_id=1, source_target_pairs={{12,4},{13,5},{14,6},{15,7},{16,24},{17,25},{18,26},{19,27}} | collective-permute-start | bytes 2457608 | tf_op jit(solution)/shard_map/ppermute | solution.py:805
  129.2 30.5 %collective-permute-start.17 = (f32[1600,128]{1,0:T(8,128)}, f32[1600,128]{1,0:T(8,128)}, u32[]{:S(2)}, u32[]{:S(2)}) collective-permute-start(f32[1600,128]{1,0:T(8,128)} %collective-permute-done.13), channel_id=1, source_target_pairs={{12,4},{13,5},{14,6},{15,7},{16,24},{17,25},{18,26},{19,27}} | collective-permute-start | bytes 2457608 | tf_op jit(solution)/shard_map/ppermute | solution.py:805
  130.5 29.2 %collective-permute-start.16 = (f32[1600,128]{1,0:T(8,128)}, f32[1600,128]{1,0:T(8,128)S(1)}, u32[]{:S(2)}, u32[]{:S(2)}) collective-permute-start(f32[1600,128]{1,0:T(8,128)} %collective-permute-done.15), channel_id=1, source_target_pairs={{12,4},{13,5},{14,6},{15,7},{16,24},{17,25},{18,26},{19,27}} | collective-permute-start | bytes 2457608 | tf_op jit(solution)/shard_map/ppermute | solution.py:805
  131.9 36.7 %collective-permute-start.19 = (f32[1600,128]{1,0:T(8,128)}, f32[1600,128]{1,0:T(8,128)}, u32[]{:S(2)}, u32[]{:S(2)}) collective-permute-start(f32[1600,128]{1,0:T(8,128)} %collective-permute-done.18), channel_id=1, source_target_pairs={{12,4},{13,5},{14,6},{15,7},{16,24},{17,25},{18,26},{19,27}} | collective-permute-start | bytes 2457608 | tf_op jit(solution)/shard_map/ppermute | solution.py:805
  159.7 10.1 %copy-start.6 = (f32[1600,128]{1,0:T(8,128)}, f32[1600,128]{1,0:T(8,128)S(1)}, u32[]{:S(2)}) copy-start(f32[1600,128]{1,0:T(8,128)S(1)} %collective-permute-done.16.refs_13_) | copy-start | bytes 2457604
  (2 other events, 1.4 us)

commit v3 on v2

--- a/solution.py
+++ b/solution.py
@@ -827,14 +827,15 @@
     return sent, kept
 
 
-def store_sums(plan, members, sent, kept):
+def store_sums(plan, members, sent, kept, before=None):
     near = [(blocks, bit) for blocks, bit in members]
     far = [(blocks, 1 - bit) for blocks, bit in members]
     moved = lon_swap(plan, sent, near)
     own = (kept[0] + moved[0]) + lon_swap(plan, kept[1] + moved[1], far)
     across = lon_swap(plan, own, far)
     beside = lon_swap(plan, own, near)
-    return own, beside, across, lon_swap(plan, across, near)
+    onward = across if before is None else lax.optimization_barrier((across, before))[0]
+    return own, beside, across, lon_swap(plan, onward, near)
 
 
 def split_sums(plan, place, at, sent, kept):
@@ -857,21 +858,29 @@
 
 
 def all_sums(plan, place, arrays):
-    result = []
-    for number, store in enumerate(plan.stores()):
-        first, second = arrays[number, 0], arrays[number, 1]
-        if plan.parts > 1:
-            result += split_sums(plan, place, store[0][0], first, second)
-        elif store[0][1] == 0:
-            result += store_sums(plan, [(plan.blocks(at), at % 2) for at, _ in store], first, second)
+    stores = plan.stores()
+    if plan.parts > 1:
+        return sum(
+            [
+                split_sums(plan, place, store[0][0], arrays[number, 0], arrays[number, 1])
+                for number, store in enumerate(stores)
+            ],
+            [],
+        )
+    back, results = None, {}
+    for number in reversed(range(len(stores))):
+        store, first, second = stores[number], arrays[number, 0], arrays[number, 1]
+        if store[0][1] == 0:
+            members = [(plan.blocks(at), at % 2) for at, _ in store]
+            results[number] = store_sums(plan, members, first, second, back)
         else:
             at = store[0][0]
             home, helpers = plan.blocks(at), plan.blocks(at + len(plan.roles))
             first, second = [lat_move(plan, array, home, helpers) for array in (first, second)]
-            own, near, far, both = store_sums(plan, [(helpers, at % 2)], first, second)
-            own, far = lax.optimization_barrier((own, far))
-            result += [lat_move(plan, array, helpers, home) for array in (own, near, far, both)]
-    return result
+            sums = store_sums(plan, [(helpers, at % 2)], first, second)
+            results[number] = [lat_move(plan, array, helpers, home) for array in sums]
+            back = results[number][0]
+    return [array for number in range(len(stores)) for array in results[number]]
 
 
 def body(winds, theta, thick, polar_rows, cutoffs):
@@ -917,15 +926,15 @@
     ]
     scal = jnp.stack([jnp.asarray(fact).astype(jnp.int32) for fact in facts])
 
-    first_edge, last_edge = edges(plan, scal, winds, theta, thick)
+    arrays = forward(plan, 0, scal, winds, theta, thick, top, bottom, t_tabs)
+
+    first_edge, last_edge = edges(plan, arrays[plan.arrays()[0][0]], winds, theta, thick)
     some = [b for b in range(lat) if (min(b, lat - 1 - b) + 1) * rows > plan.low]
     east_pairs = [(b * lon + i, b * lon + (i + 1) % lon) for b in some for i in range(lon)]
     west = lax.ppermute(last_edge, ("lat", "lon"), east_pairs)
     east = lax.ppermute(first_edge, ("lat", "lon"), [(to, at) for at, to in east_pairs])
 
     scal, _ = lax.optimization_barrier((scal, first_edge))
-    arrays = forward(plan, 0, scal, winds, theta, thick, top, bottom, t_tabs)
-    scal, _ = lax.optimization_barrier((scal, arrays[plan.arrays()[0][0]]))
     later = forward(plan, 1, scal, winds, theta, thick, top, bottom, t_tabs)
     added = {key: array for key, array in later.items() if plan.stores()[key[0]][0][1] == 0}
     added, west, east = lax.optimization_barrier((added, west, east))

time: 209 us -> 197 us (0.943)
  waiting for transfers between devices: 77.7 us -> 66 us
    ppermute x10, waiting for transfers between devices: 34.9 us -> 24.8 us  [lon_swap(): return lax.ppermute(value, ('lat', 'lon'), pairs)]
where the time goes in v3:
time: 197 us; the launch traced here: 196 us
  Pallas kernels  70.9 us (36%)
  waiting for transfers between devices  66 us (34%)
  starting transfers between devices  42.8 us (22%)
  other arithmetic  5.95 us (3%)
  local copies, waits for them, and re-layouts  5.83 us (3%)
  between operations  4.52 us (2%)
    ppermute x6, waiting for transfers between devices, lat_move(): return lax.ppermute(value, ('lat', 'lon'), pairs)  37.9 us
    pallas_call x1, Pallas kernels, substep(): pl.pallas_call(functools.partial(step_kernel, plan, step_rows), grid_spec...  37.6 us
    pallas_call x2, Pallas kernels, forward(): pl.pallas_call(functools.partial(forward_kernel, plan, call), grid_spec=p...  27.1 us
    ppermute x10, waiting for transfers between devices, lon_swap(): return lax.ppermute(value, ('lat', 'lon'), pairs)  24.8 us
    ppermute x10, starting transfers between devices, lon_swap(): return lax.ppermute(value, ('lat', 'lon'), pairs)  22.3 us
    ppermute x6, starting transfers between devices, lat_move(): return lax.ppermute(value, ('lat', 'lon'), pairs)  9.06 us
    pallas_call x1, Pallas kernels, edges(): pl.pallas_call(functools.partial(edge_kernel, plan, count), grid=(1,), in...  6.25 us
    add x4, other arithmetic, store_sums(): own = kept[0] + moved[0] + lon_swap(plan, kept[1] + moved[1], far)  4.18 us
  transfers between devices with their start and end apart: 20, of which 8 were waited for; matrix products, arithmetic and copies ran while one was open for 4% of the time, Pallas kernels for 10%

profile of v3, /device:TPU:26, one launch (start us, length us, event | category | flops | bytes accessed | tf_op | source)
XLA Modules:
  0.0 196.1 jit_solution(3092195649278654878)
XLA Ops:
  2.4 1.9 collective-permute-start
  4.4 3.6 %collective-permute-start.1 = (f32[4,16,720]{2,1,0:T(8,128)S(1)}, f32[4,16,720]{2,1,0:T(8,128)S(1)}, u32[]{:S(2)}, u32[]{:S(2)}) collective-permute-start(f32[4,16,720]{2,1,0:T(8,128)S(1)} %pad_maximum_fusion.1), channel_id=1, source_target_pairs={{4,0},{5,1},{6,2},{7,3},{8,4},{9,5},{10,6},{11,7},{12,8},{13,9},{1... | collective-permute-start | bytes 552968 | tf_op jit(solution)/shard_map/ppermute | solution.py:905
  8.1 1.3 fusion.6
  14.7 13.3 %partial_spectra.2 = (f32[2,2496,128]{2,1,0:T(8,128)}, f32[2,1600,128]{2,1,0:T(8,128)}) custom-call(s32[11]{0:T(128)} %stack.58.scal, f32[2,90,16,720]{3,2,1,0:T(8,128)} %bitcast.43, f32[90,16,720]{2,1,0:T(8,128)} %bitcast.62, f32[90,16,720]{2,1,0:T(8,128)} %bitcast.73, f32[4,16,720]{2,1,0:T(8,128)} %copy-done.3, f32[4,16,720]{2,1,0:T(8,128)} %copy-done.4, ...), custom_call_target="tpu_custom_call" | custom-call | flops 5000000000 | tf_op jit(solution)/shard_map/partial_spectra/pallas_call | solution.py:423
  28.0 3.8 %collective-permute-start.4 = (f32[2,2496,128]{2,1,0:T(8,128)}, f32[2,2496,128]{2,1,0:T(8,128)S(1)}, u32[]{:S(2)}, u32[]{:S(2)}) collective-permute-start(f32[2,2496,128]{2,1,0:T(8,128)} %get-tuple-element.17._), channel_id=1, source_target_pairs={{0,1},{1,0},{2,3},{3,2},{28,29},{29,28},{30,31},{31,30},{4,6},{5,7... | collective-permute-start | bytes 7667720 | tf_op jit(solution)/shard_map/ppermute | solution.py:796
  31.8 2.5 %collective-permute-start.9 = (f32[2,1600,128]{2,1,0:T(8,128)}, f32[2,1600,128]{2,1,0:T(8,128)}, u32[]{:S(2)}, u32[]{:S(2)}) collective-permute-start(f32[2,1600,128]{2,1,0:T(8,128)} %get-tuple-element.26), channel_id=1, source_target_pairs={{4,12},{5,13},{6,14},{7,15},{24,16},{25,17},{26,18},{27,19}} | collective-permute-start | bytes 4915208 | tf_op jit(solution)/shard_map/ppermute | solution.py:805
  34.3 6.2 %edge_columns.1 = (f32[4,16,128]{2,1,0:T(8,128)}, f32[4,16,128]{2,1,0:T(8,128)}) custom-call(f32[2,2496,128]{2,1,0:T(8,128)} %get-tuple-element.17._, f32[2,90,16,720]{3,2,1,0:T(8,128)} %bitcast.44, f32[2,90,16,720]{3,2,1,0:T(8,128)} %bitcast.45, f32[90,16,720]{2,1,0:T(8,128)} %bitcast.63, f32[90,16,720]{2,1,0:T(8,128)} %bitcast.74, ...), custom_call_target="tpu_custom_call" | custom-call | flops 5000000000 | tf_op jit(solution)/shard_map/edge_columns/pallas_call | solution.py:483
  40.5 13.8 %partial_spectra.3 = (f32[2,2496,128]{2,1,0:T(8,128)}, f32[2,1600,128]{2,1,0:T(8,128)}) custom-call(s32[11]{0:T(128)} %stack.58.scal, f32[2,90,16,720]{3,2,1,0:T(8,128)} %bitcast.56, f32[90,16,720]{2,1,0:T(8,128)} %bitcast.69, f32[90,16,720]{2,1,0:T(8,128)} %bitcast.80, f32[4,16,720]{2,1,0:T(8,128)} %copy-done.3, f32[4,16,720]{2,1,0:T(8,128)} %copy-done.4, ...), custom_call_target="tpu_custom_call" | custom-call | flops 5000000000 | tf_op jit(solution)/shard_map/partial_spectra/pallas_call | solution.py:423
  54.3 1.4 collective-permute-start.8
  56.5 2.5 %collective-permute-start.2 = (f32[4,16,128]{2,1,0:T(8,128)S(1)}, f32[4,16,128]{2,1,0:T(8,128)S(1)}, u32[]{:S(2)}, u32[]{:S(2)}) collective-permute-start(f32[4,16,128]{2,1,0:T(8,128)S(1)} %copy-done.13), channel_id=1, source_target_pairs={{4,5},{5,6},{6,7},{7,4},{8,9},{9,10},{10,11},{11,8},{12,13},{13,14... | collective-permute-start | bytes 98312 | tf_op jit(solution)/shard_map/ppermute | solution.py:934
  59.0 3.3 %collective-permute-start.3 = (f32[4,16,128]{2,1,0:T(8,128)S(1)}, f32[4,16,128]{2,1,0:T(8,128)S(1)}, u32[]{:S(2)}, u32[]{:S(2)}) collective-permute-start(f32[4,16,128]{2,1,0:T(8,128)S(1)} %copy-done.12), channel_id=1, source_target_pairs={{5,4},{6,5},{7,6},{4,7},{9,8},{10,9},{11,10},{8,11},{13,12},{14,13... | collective-permute-start | bytes 98312 | tf_op jit(solution)/shard_map/ppermute | solution.py:935
  62.4 3.3 %collective-permute-done.3.east = f32[4,16,128]{2,1,0:T(8,128)S(1)} collective-permute-done((f32[4,16,128]{2,1,0:T(8,128)S(1)}, f32[4,16,128]{2,1,0:T(8,128)S(1)}, u32[]{:S(2)}, u32[]{:S(2)}) %collective-permute-start.3) | collective-permute-done | bytes 32800 | tf_op jit(solution)/shard_map/ppermute | solution.py:935
  65.8 2.4 %fusion = f32[2496,128]{1,0:T(8,128)S(1)} fusion(f32[2,2496,128]{2,1,0:T(8,128)S(1)} %collective-permute-done.4, f32[2,2496,128]{2,1,0:T(8,128)} %get-tuple-element.24), kind=kLoop, calls=%fused_computation.1 | loop fusion | flops 319488 | bytes 3833856 | tf_op jit(solution)/shard_map/add | solution.py:834
  68.2 2.4 %collective-permute-start.5 = (f32[2496,128]{1,0:T(8,128)S(1)}, f32[2496,128]{1,0:T(8,128)S(1)}, u32[]{:S(2)}, u32[]{:S(2)}) collective-permute-start(f32[2496,128]{1,0:T(8,128)S(1)} %fusion), channel_id=1, source_target_pairs={{0,2},{1,3},{2,0},{3,1},{28,30},{29,31},{30,28},{31,29},{4,5},{5,4... | collective-permute-start | bytes 3833864 | tf_op jit(solution)/shard_map/ppermute | solution.py:796
  70.7 3.9 %collective-permute-done.8 = f32[2,1600,128]{2,1,0:T(8,128)S(1)} collective-permute-done((f32[2,1600,128]{2,1,0:T(8,128)}, f32[2,1600,128]{2,1,0:T(8,128)S(1)}, u32[]{:S(2)}, u32[]{:S(2)}) %collective-permute-start.8) | collective-permute-done | bytes 1638432 | tf_op jit(solution)/shard_map/ppermute | solution.py:805
  75.4 12.0 %collective-permute-done.5 = f32[2496,128]{1,0:T(8,128)S(1)} collective-permute-done((f32[2496,128]{1,0:T(8,128)S(1)}, f32[2496,128]{1,0:T(8,128)S(1)}, u32[]{:S(2)}, u32[]{:S(2)}) %collective-permute-start.5) | collective-permute-done | bytes 1277984 | tf_op jit(solution)/shard_map/ppermute | solution.py:796
  87.4 1.6 fusion.2.refs_8_
  89.0 2.6 %collective-permute-start.7 = (f32[2496,128]{1,0:T(8,128)S(1)}, f32[2496,128]{1,0:T(8,128)S(1)}, u32[]{:S(2)}, u32[]{:S(2)}) collective-permute-start(f32[2496,128]{1,0:T(8,128)S(1)} %fusion.2.refs_8_), channel_id=1, source_target_pairs={{0,2},{1,3},{2,0},{3,1},{28,30},{29,31},{30,28},{31,29},{4,5},{5,4... | collective-permute-start | bytes 3833864 | tf_op jit(solution)/shard_map/ppermute | solution.py:796
  91.7 1.6 collective-permute-start.16
  94.6 1.6 collective-permute-start.14
  96.2 1.6 collective-permute-start.18
  97.8 2.8 %collective-permute-start.6 = (f32[2496,128]{1,0:T(8,128)S(1)}, f32[2496,128]{1,0:T(8,128)}, u32[]{:S(2)}, u32[]{:S(2)}) collective-permute-start(f32[2496,128]{1,0:T(8,128)S(1)} %fusion.2.refs_8_), channel_id=1, source_target_pairs={{0,1},{1,0},{2,3},{3,2},{28,29},{29,28},{30,31},{31,30},{4,6},{5,7... | collective-permute-start | bytes 3833864 | tf_op jit(solution)/shard_map/ppermute | solution.py:796
  100.6 7.1 %collective-permute-done.12.refs_12_ = f32[1600,128]{1,0:T(8,128)} collective-permute-done((f32[1600,128]{1,0:T(8,128)S(1)}, f32[1600,128]{1,0:T(8,128)}, u32[]{:S(2)}, u32[]{:S(2)}) %collective-permute-start.12) | collective-permute-done | bytes 819232 | tf_op jit(solution)/shard_map/ppermute | solution.py:805
  107.7 12.8 %collective-permute-done.7.refs_10_ = f32[2496,128]{1,0:T(8,128)S(1)} collective-permute-done((f32[2496,128]{1,0:T(8,128)S(1)}, f32[2496,128]{1,0:T(8,128)S(1)}, u32[]{:S(2)}, u32[]{:S(2)}) %collective-permute-start.7) | collective-permute-done | bytes 1277984 | tf_op jit(solution)/shard_map/ppermute | solution.py:796
  120.5 4.5 %collective-permute-start.13 = (f32[2496,128]{1,0:T(8,128)S(1)}, f32[2496,128]{1,0:T(8,128)}, u32[]{:S(2)}, u32[]{:S(2)}) collective-permute-start(f32[2496,128]{1,0:T(8,128)S(1)} %collective-permute-done.7.refs_10_), channel_id=1, source_target_pairs={{0,1},{1,0},{2,3},{3,2},{28,29},{29,28},{30,31},{31,30},{4,6},{5,7... | collective-permute-start | bytes 3833864 | tf_op jit(solution)/shard_map/ppermute | solution.py:796
  125.0 1.3 collective-permute-start.17
  126.3 1.3 collective-permute-start.15
  127.6 1.3 collective-permute-start.19
  130.2 9.4 %collective-permute-done.17.refs_14_ = f32[1600,128]{1,0:T(8,128)} collective-permute-done((f32[1600,128]{1,0:T(8,128)}, f32[1600,128]{1,0:T(8,128)}, u32[]{:S(2)}, u32[]{:S(2)}) %collective-permute-start.17) | collective-permute-done | bytes 819232 | tf_op jit(solution)/shard_map/ppermute | solution.py:805
  139.6 8.7 %collective-permute-done.15.refs_13_ = f32[1600,128]{1,0:T(8,128)S(1)} collective-permute-done((f32[1600,128]{1,0:T(8,128)}, f32[1600,128]{1,0:T(8,128)S(1)}, u32[]{:S(2)}, u32[]{:S(2)}) %collective-permute-start.15) | collective-permute-done | bytes 819232 | tf_op jit(solution)/shard_map/ppermute | solution.py:805
  148.2 8.9 %collective-permute-done.19.refs_15_ = f32[1600,128]{1,0:T(8,128)} collective-permute-done((f32[1600,128]{1,0:T(8,128)}, f32[1600,128]{1,0:T(8,128)}, u32[]{:S(2)}, u32[]{:S(2)}) %collective-permute-start.19) | collective-permute-done | bytes 819232 | tf_op jit(solution)/shard_map/ppermute | solution.py:805
  158.3 37.6 %inverse_and_substep.1 = (f32[2,90,16,720]{3,2,1,0:T(8,128)}, f32[90,16,720]{2,1,0:T(8,128)}, f32[90,16,720]{2,1,0:T(8,128)}) custom-call(s32[11]{0:T(128)} %stack.58.scal, f32[540]{0:T(1024)} %concatenate.3.coef, f32[4,16,128]{2,1,0:T(8,128)} %copy-done.7, f32[4,16,128]{2,1,0:T(8,128)} %copy-done.8, f32[4,16,720]{2,1,0:T(8,128)} %copy-done.3, ...), custom_call_target="tpu_custom_call" | custom-call | flops 9286189056 | bytes 40000000 | tf_op jit(solution)/shard_map/inverse_and_substep/pallas_call | solution.py:762
  (62 shorter events, 9.3 us)
Async XLA Ops:
  2.4 10.9 %collective-permute-start = (f32[4,16,720]{2,1,0:T(8,128)S(1)}, f32[4,16,720]{2,1,0:T(8,128)S(1)}, u32[]{:S(2)}, u32[]{:S(2)}) collective-permute-start(f32[4,16,720]{2,1,0:T(8,128)S(1)} %pad_maximum_fusion), channel_id=1, source_target_pairs={{0,4},{1,5},{2,6},{3,7},{4,8},{5,9},{6,10},{7,11},{8,12},{9,13},{1... | collective-permute-start | bytes 552968 | tf_op jit(solution)/shard_map/ppermute | solution.py:904
  4.4 8.9 %collective-permute-start.1 = (f32[4,16,720]{2,1,0:T(8,128)S(1)}, f32[4,16,720]{2,1,0:T(8,128)S(1)}, u32[]{:S(2)}, u32[]{:S(2)}) collective-permute-start(f32[4,16,720]{2,1,0:T(8,128)S(1)} %pad_maximum_fusion.1), channel_id=1, source_target_pairs={{4,0},{5,1},{6,2},{7,3},{8,4},{9,5},{10,6},{11,7},{12,8},{13,9},{1... | collective-permute-start | bytes 552968 | tf_op jit(solution)/shard_map/ppermute | solution.py:905
  28.0 37.8 %collective-permute-start.4 = (f32[2,2496,128]{2,1,0:T(8,128)}, f32[2,2496,128]{2,1,0:T(8,128)S(1)}, u32[]{:S(2)}, u32[]{:S(2)}) collective-permute-start(f32[2,2496,128]{2,1,0:T(8,128)} %get-tuple-element.17._), channel_id=1, source_target_pairs={{0,1},{1,0},{2,3},{3,2},{28,29},{29,28},{30,31},{31,30},{4,6},{5,7... | collective-permute-start | bytes 7667720 | tf_op jit(solution)/shard_map/ppermute | solution.py:796
  31.8 24.0 %collective-permute-start.9 = (f32[2,1600,128]{2,1,0:T(8,128)}, f32[2,1600,128]{2,1,0:T(8,128)}, u32[]{:S(2)}, u32[]{:S(2)}) collective-permute-start(f32[2,1600,128]{2,1,0:T(8,128)} %get-tuple-element.26), channel_id=1, source_target_pairs={{4,12},{5,13},{6,14},{7,15},{24,16},{25,17},{26,18},{27,19}} | collective-permute-start | bytes 4915208 | tf_op jit(solution)/shard_map/ppermute | solution.py:805
  40.5 16.0 %copy-start.13 = (f32[4,16,128]{2,1,0:T(8,128)S(1)}, f32[4,16,128]{2,1,0:T(8,128)}, u32[]{:S(2)}) copy-start(f32[4,16,128]{2,1,0:T(8,128)} %get-tuple-element.21) | copy-start | bytes 98308
  40.5 18.5 %copy-start.12 = (f32[4,16,128]{2,1,0:T(8,128)S(1)}, f32[4,16,128]{2,1,0:T(8,128)}, u32[]{:S(2)}) copy-start(f32[4,16,128]{2,1,0:T(8,128)} %get-tuple-element.18) | copy-start | bytes 98308
  54.3 20.2 %collective-permute-start.8 = (f32[2,1600,128]{2,1,0:T(8,128)}, f32[2,1600,128]{2,1,0:T(8,128)S(1)}, u32[]{:S(2)}, u32[]{:S(2)}) collective-permute-start(f32[2,1600,128]{2,1,0:T(8,128)} %get-tuple-element.25), channel_id=1, source_target_pairs={{4,12},{5,13},{6,14},{7,15},{24,16},{25,17},{26,18},{27,19}} | collective-permute-start | bytes 4915208 | tf_op jit(solution)/shard_map/ppermute | solution.py:805
  55.7 18.8 %collective-permute-start.10 = (f32[2,1600,128]{2,1,0:T(8,128)}, f32[2,1600,128]{2,1,0:T(8,128)S(1)}, u32[]{:S(2)}, u32[]{:S(2)}) collective-permute-start(f32[2,1600,128]{2,1,0:T(8,128)} %collective-permute-done.9), channel_id=1, source_target_pairs={{12,14},{13,15},{14,12},{15,13},{16,18},{17,19},{18,16},{19,17}} | collective-permute-start | bytes 4915208 | tf_op jit(solution)/shard_map/ppermute | solution.py:796
  56.5 5.9 %collective-permute-start.2 = (f32[4,16,128]{2,1,0:T(8,128)S(1)}, f32[4,16,128]{2,1,0:T(8,128)S(1)}, u32[]{:S(2)}, u32[]{:S(2)}) collective-permute-start(f32[4,16,128]{2,1,0:T(8,128)S(1)} %copy-done.13), channel_id=1, source_target_pairs={{4,5},{5,6},{6,7},{7,4},{8,9},{9,10},{10,11},{11,8},{12,13},{13,14... | collective-permute-start | bytes 98312 | tf_op jit(solution)/shard_map/ppermute | solution.py:934
  59.0 6.7 %collective-permute-start.3 = (f32[4,16,128]{2,1,0:T(8,128)S(1)}, f32[4,16,128]{2,1,0:T(8,128)S(1)}, u32[]{:S(2)}, u32[]{:S(2)}) collective-permute-start(f32[4,16,128]{2,1,0:T(8,128)S(1)} %copy-done.12), channel_id=1, source_target_pairs={{5,4},{6,5},{7,6},{4,7},{9,8},{10,9},{11,10},{8,11},{13,12},{14,13... | collective-permute-start | bytes 98312 | tf_op jit(solution)/shard_map/ppermute | solution.py:935
  62.4 5.8 %copy-start.7 = (f32[4,16,128]{2,1,0:T(8,128)}, f32[4,16,128]{2,1,0:T(8,128)S(1)}, u32[]{:S(2)}) copy-start(f32[4,16,128]{2,1,0:T(8,128)S(1)} %collective-permute-done.2.west) | copy-start | bytes 98308
  65.8 2.4 %copy-start.8 = (f32[4,16,128]{2,1,0:T(8,128)}, f32[4,16,128]{2,1,0:T(8,128)S(1)}, u32[]{:S(2)}) copy-start(f32[4,16,128]{2,1,0:T(8,128)S(1)} %collective-permute-done.3.east) | copy-start | bytes 98308
  65.8 2.4 %copy-start.1 = (f32[2,2496,128]{2,1,0:T(8,128)}, f32[2,2496,128]{2,1,0:T(8,128)S(1)}, u32[]{:S(2)}) copy-start(f32[2,2496,128]{2,1,0:T(8,128)S(1)} %collective-permute-done.4) | copy-start | bytes 7667716
  65.8 21.6 %copy-start.2 = (f32[2,2496,128]{2,1,0:T(8,128)S(1)}, f32[2,2496,128]{2,1,0:T(8,128)}, u32[]{:S(2)}) copy-start(f32[2,2496,128]{2,1,0:T(8,128)} %get-tuple-element.24) | copy-start | bytes 7667716
  68.2 19.1 %collective-permute-start.5 = (f32[2496,128]{1,0:T(8,128)S(1)}, f32[2496,128]{1,0:T(8,128)S(1)}, u32[]{:S(2)}, u32[]{:S(2)}) collective-permute-start(f32[2496,128]{1,0:T(8,128)S(1)} %fusion), channel_id=1, source_target_pairs={{0,2},{1,3},{2,0},{3,1},{28,30},{29,31},{30,28},{31,29},{4,5},{5,4... | collective-permute-start | bytes 3833864 | tf_op jit(solution)/shard_map/ppermute | solution.py:796
  74.7 16.9 %collective-permute-start.11 = (f32[1600,128]{1,0:T(8,128)S(1)}, f32[1600,128]{1,0:T(8,128)S(1)}, u32[]{:S(2)}, u32[]{:S(2)}) collective-permute-start(f32[1600,128]{1,0:T(8,128)S(1)} %fusion.3), channel_id=1, source_target_pairs={{12,13},{13,12},{14,15},{15,14},{16,17},{17,16},{18,19},{19,18}} | collective-permute-start | bytes 2457608 | tf_op jit(solution)/shard_map/ppermute | solution.py:796
  88.9 8.9 %copy-start = (f32[2496,128]{1,0:T(8,128)}, f32[2496,128]{1,0:T(8,128)S(1)}, u32[]{:S(2)}) copy-start(f32[2496,128]{1,0:T(8,128)S(1)} %fusion.2.refs_8_) | copy-start | bytes 3833860
  88.9 36.0 %copy-start.11 = (s32[2,2,92]{2,1,0:T(2,128)S(1)}, s32[2,2,92]{2,1,0:T(2,128)}, u32[]{:S(2)}) copy-start(s32[2,2,92]{2,1,0:T(2,128)} %constant.88.clone) | copy-start | bytes 4420
  89.0 36.0 %copy-start.10 = (s32[240]{0:T(256)S(1)}, s32[240]{0:T(256)}, u32[]{:S(2)}) copy-start(s32[240]{0:T(256)} %param.14) | copy-start | bytes 2884
  89.0 40.0 %copy-start.9 = (s32[240]{0:T(256)S(1)}, s32[240]{0:T(256)}, u32[]{:S(2)}) copy-start(s32[240]{0:T(256)} %param.13) | copy-start | bytes 2884
  89.0 31.5 %collective-permute-start.7 = (f32[2496,128]{1,0:T(8,128)S(1)}, f32[2496,128]{1,0:T(8,128)S(1)}, u32[]{:S(2)}, u32[]{:S(2)}) collective-permute-start(f32[2496,128]{1,0:T(8,128)S(1)} %fusion.2.refs_8_), channel_id=1, source_target_pairs={{0,2},{1,3},{2,0},{3,1},{28,30},{29,31},{30,28},{31,29},{4,5},{5,4... | collective-permute-start | bytes 3833864 | tf_op jit(solution)/shard_map/ppermute | solution.py:796
  91.7 4.5 %collective-permute-start.16 = (f32[1600,128]{1,0:T(8,128)S(1)}, f32[1600,128]{1,0:T(8,128)}, u32[]{:S(2)}, u32[]{:S(2)}) collective-permute-start(f32[1600,128]{1,0:T(8,128)S(1)} %fusion.5), channel_id=1, source_target_pairs={{12,13},{13,12},{14,15},{15,14},{16,17},{17,16},{18,19},{19,18}} | collective-permute-start | bytes 2457608 | tf_op jit(solution)/shard_map/ppermute | solution.py:796
  93.4 14.3 %collective-permute-start.12 = (f32[1600,128]{1,0:T(8,128)S(1)}, f32[1600,128]{1,0:T(8,128)}, u32[]{:S(2)}, u32[]{:S(2)}) collective-permute-start(f32[1600,128]{1,0:T(8,128)S(1)} %fusion.5), channel_id=1, source_target_pairs={{12,4},{13,5},{14,6},{15,7},{16,24},{17,25},{18,26},{19,27}} | collective-permute-start | bytes 2457608 | tf_op jit(solution)/shard_map/ppermute | solution.py:805
  94.6 31.7 %collective-permute-start.14 = (f32[1600,128]{1,0:T(8,128)S(1)}, f32[1600,128]{1,0:T(8,128)}, u32[]{:S(2)}, u32[]{:S(2)}) collective-permute-start(f32[1600,128]{1,0:T(8,128)S(1)} %fusion.5), channel_id=1, source_target_pairs={{12,14},{13,15},{14,12},{15,13},{16,18},{17,19},{18,16},{19,17}} | collective-permute-start | bytes 2457608 | tf_op jit(solution)/shard_map/ppermute | solution.py:796
  96.2 31.4 %collective-permute-start.18 = (f32[1600,128]{1,0:T(8,128)}, f32[1600,128]{1,0:T(8,128)}, u32[]{:S(2)}, u32[]{:S(2)}) collective-permute-start(f32[1600,128]{1,0:T(8,128)} %collective-permute-done.16), channel_id=1, source_target_pairs={{12,14},{13,15},{14,12},{15,13},{16,18},{17,19},{18,16},{19,17}} | collective-permute-start | bytes 2457608 | tf_op jit(solution)/shard_map/ppermute | solution.py:796
  97.8 32.4 %collective-permute-start.6 = (f32[2496,128]{1,0:T(8,128)S(1)}, f32[2496,128]{1,0:T(8,128)}, u32[]{:S(2)}, u32[]{:S(2)}) collective-permute-start(f32[2496,128]{1,0:T(8,128)S(1)} %fusion.2.refs_8_), channel_id=1, source_target_pairs={{0,1},{1,0},{2,3},{3,2},{28,29},{29,28},{30,31},{31,30},{4,6},{5,7... | collective-permute-start | bytes 3833864 | tf_op jit(solution)/shard_map/ppermute | solution.py:796
  120.5 37.8 %copy-start.5 = (f32[2496,128]{1,0:T(8,128)}, f32[2496,128]{1,0:T(8,128)S(1)}, u32[]{:S(2)}) copy-start(f32[2496,128]{1,0:T(8,128)S(1)} %collective-permute-done.7.refs_10_) | copy-start | bytes 3833860
  120.5 27.8 %collective-permute-start.13 = (f32[2496,128]{1,0:T(8,128)S(1)}, f32[2496,128]{1,0:T(8,128)}, u32[]{:S(2)}, u32[]{:S(2)}) collective-permute-start(f32[2496,128]{1,0:T(8,128)S(1)} %collective-permute-done.7.refs_10_), channel_id=1, source_target_pairs={{0,1},{1,0},{2,3},{3,2},{28,29},{29,28},{30,31},{31,30},{4,6},{5,7... | collective-permute-start | bytes 3833864 | tf_op jit(solution)/shard_map/ppermute | solution.py:796
  125.0 14.6 %collective-permute-start.17 = (f32[1600,128]{1,0:T(8,128)}, f32[1600,128]{1,0:T(8,128)}, u32[]{:S(2)}, u32[]{:S(2)}) collective-permute-start(f32[1600,128]{1,0:T(8,128)} %collective-permute-done.16), channel_id=1, source_target_pairs={{12,4},{13,5},{14,6},{15,7},{16,24},{17,25},{18,26},{19,27}} | collective-permute-start | bytes 2457608 | tf_op jit(solution)/shard_map/ppermute | solution.py:805
  126.3 21.9 %collective-permute-start.15 = (f32[1600,128]{1,0:T(8,128)}, f32[1600,128]{1,0:T(8,128)S(1)}, u32[]{:S(2)}, u32[]{:S(2)}) collective-permute-start(f32[1600,128]{1,0:T(8,128)} %collective-permute-done.14), channel_id=1, source_target_pairs={{12,4},{13,5},{14,6},{15,7},{16,24},{17,25},{18,26},{19,27}} | collective-permute-start | bytes 2457608 | tf_op jit(solution)/shard_map/ppermute | solution.py:805
  127.6 29.5 %collective-permute-start.19 = (f32[1600,128]{1,0:T(8,128)}, f32[1600,128]{1,0:T(8,128)}, u32[]{:S(2)}, u32[]{:S(2)}) collective-permute-start(f32[1600,128]{1,0:T(8,128)} %collective-permute-done.18), channel_id=1, source_target_pairs={{12,4},{13,5},{14,6},{15,7},{16,24},{17,25},{18,26},{19,27}} | collective-permute-start | bytes 2457608 | tf_op jit(solution)/shard_map/ppermute | solution.py:805
  148.2 10.1 %copy-start.6 = (f32[1600,128]{1,0:T(8,128)}, f32[1600,128]{1,0:T(8,128)S(1)}, u32[]{:S(2)}) copy-start(f32[1600,128]{1,0:T(8,128)S(1)} %collective-permute-done.15.refs_13_) | copy-start | bytes 2457604
  (2 other events, 1.4 us)

commit v4 on v3

--- a/solution.py
+++ b/solution.py
@@ -879,7 +879,7 @@
             first, second = [lat_move(plan, array, home, helpers) for array in (first, second)]
             sums = store_sums(plan, [(helpers, at % 2)], first, second)
             results[number] = [lat_move(plan, array, helpers, home) for array in sums]
-            back = results[number][0]
+            back = (results[number][0], results[number][2])
     return [array for number in range(len(stores)) for array in results[number]]
 
 

time: 197 us -> 197 us (level)
  waiting for transfers between devices: 66 us -> 68.4 us
  starting transfers between devices: 42.8 us -> 40.5 us
    ppermute x10, waiting for transfers between devices: 24.8 us -> 28.2 us  [lon_swap(): return lax.ppermute(value, ('lat', 'lon'), pairs)]
    ppermute x10, starting transfers between devices: 22.3 us -> 20 us  [lon_swap(): return lax.ppermute(value, ('lat', 'lon'), pairs)]
  transfers between devices with their start and end apart: 20 -> 20, of which waited for: 8 -> 7; matrix products, arithmetic and copies ran while one was open for 4% -> 3% of each run, Pallas kernels for 10% -> 10%
where the time goes in v4:
time: 197 us; the launch traced here: 195 us
  Pallas kernels  71 us (36%)
  waiting for transfers between devices  68.4 us (35%)
  starting transfers between devices  40.5 us (21%)
  local copies, waits for them, and re-layouts  5.84 us (3%)
  between operations  4.56 us (2%)
  other arithmetic  4.55 us (2%)
    pallas_call x1, Pallas kernels, substep(): pl.pallas_call(functools.partial(step_kernel, plan, step_rows), grid_spec...  37.6 us
    ppermute x6, waiting for transfers between devices, lat_move(): return lax.ppermute(value, ('lat', 'lon'), pairs)  36.8 us
    ppermute x10, waiting for transfers between devices, lon_swap(): return lax.ppermute(value, ('lat', 'lon'), pairs)  28.2 us
    pallas_call x2, Pallas kernels, forward(): pl.pallas_call(functools.partial(forward_kernel, plan, call), grid_spec=p...  27.1 us
    ppermute x10, starting transfers between devices, lon_swap(): return lax.ppermute(value, ('lat', 'lon'), pairs)  20 us
    ppermute x6, starting transfers between devices, lat_move(): return lax.ppermute(value, ('lat', 'lon'), pairs)  9.06 us
    pallas_call x1, Pallas kernels, edges(): pl.pallas_call(functools.partial(edge_kernel, plan, count), grid=(1,), in...  6.27 us
  transfers between devices with their start and end apart: 20, of which 7 were waited for; matrix products, arithmetic and copies ran while one was open for 3% of the time, Pallas kernels for 10%

profile of v4, /device:TPU:26, one launch (start us, length us, event | category | flops | bytes accessed | tf_op | source)
XLA Modules:
  0.0 194.8 jit_solution(3174283477578183555)
XLA Ops:
  2.4 1.9 collective-permute-start
  4.4 3.6 %collective-permute-start.1 = (f32[4,16,720]{2,1,0:T(8,128)S(1)}, f32[4,16,720]{2,1,0:T(8,128)S(1)}, u32[]{:S(2)}, u32[]{:S(2)}) collective-permute-start(f32[4,16,720]{2,1,0:T(8,128)S(1)} %pad_maximum_fusion.1), channel_id=1, source_target_pairs={{4,0},{5,1},{6,2},{7,3},{8,4},{9,5},{10,6},{11,7},{12,8},{13,9},{1... | collective-permute-start | bytes 552968 | tf_op jit(solution)/shard_map/ppermute | solution.py:905
  8.1 1.3 fusion.6
  14.7 13.3 %partial_spectra.2 = (f32[2,2496,128]{2,1,0:T(8,128)}, f32[2,1600,128]{2,1,0:T(8,128)}) custom-call(s32[11]{0:T(128)} %stack.58.scal, f32[2,90,16,720]{3,2,1,0:T(8,128)} %bitcast.43, f32[90,16,720]{2,1,0:T(8,128)} %bitcast.62, f32[90,16,720]{2,1,0:T(8,128)} %bitcast.73, f32[4,16,720]{2,1,0:T(8,128)} %copy-done.4, f32[4,16,720]{2,1,0:T(8,128)} %copy-done.5, ...), custom_call_target="tpu_custom_call" | custom-call | flops 5000000000 | tf_op jit(solution)/shard_map/partial_spectra/pallas_call | solution.py:423
  28.0 2.5 %collective-permute-start.9 = (f32[2,1600,128]{2,1,0:T(8,128)}, f32[2,1600,128]{2,1,0:T(8,128)}, u32[]{:S(2)}, u32[]{:S(2)}) collective-permute-start(f32[2,1600,128]{2,1,0:T(8,128)} %get-tuple-element.26), channel_id=1, source_target_pairs={{4,12},{5,13},{6,14},{7,15},{24,16},{25,17},{26,18},{27,19}} | collective-permute-start | bytes 4915208 | tf_op jit(solution)/shard_map/ppermute | solution.py:805
  30.5 3.8 %collective-permute-start.4 = (f32[2,2496,128]{2,1,0:T(8,128)}, f32[2,2496,128]{2,1,0:T(8,128)S(1)}, u32[]{:S(2)}, u32[]{:S(2)}) collective-permute-start(f32[2,2496,128]{2,1,0:T(8,128)} %get-tuple-element.17._), channel_id=1, source_target_pairs={{0,1},{1,0},{2,3},{3,2},{28,29},{29,28},{30,31},{31,30},{4,6},{5,7... | collective-permute-start | bytes 7667720 | tf_op jit(solution)/shard_map/ppermute | solution.py:796
  34.3 6.3 %edge_columns.1 = (f32[4,16,128]{2,1,0:T(8,128)}, f32[4,16,128]{2,1,0:T(8,128)}) custom-call(f32[2,2496,128]{2,1,0:T(8,128)} %get-tuple-element.17._, f32[2,90,16,720]{3,2,1,0:T(8,128)} %bitcast.44, f32[2,90,16,720]{3,2,1,0:T(8,128)} %bitcast.45, f32[90,16,720]{2,1,0:T(8,128)} %bitcast.63, f32[90,16,720]{2,1,0:T(8,128)} %bitcast.74, ...), custom_call_target="tpu_custom_call" | custom-call | flops 5000000000 | tf_op jit(solution)/shard_map/edge_columns/pallas_call | solution.py:483
  40.5 13.8 %partial_spectra.3 = (f32[2,2496,128]{2,1,0:T(8,128)}, f32[2,1600,128]{2,1,0:T(8,128)}) custom-call(s32[11]{0:T(128)} %stack.58.scal, f32[2,90,16,720]{3,2,1,0:T(8,128)} %bitcast.56, f32[90,16,720]{2,1,0:T(8,128)} %bitcast.69, f32[90,16,720]{2,1,0:T(8,128)} %bitcast.80, f32[4,16,720]{2,1,0:T(8,128)} %copy-done.4, f32[4,16,720]{2,1,0:T(8,128)} %copy-done.5, ...), custom_call_target="tpu_custom_call" | custom-call | flops 5000000000 | tf_op jit(solution)/shard_map/partial_spectra/pallas_call | solution.py:423
  54.3 1.4 collective-permute-start.8
  56.5 2.5 %collective-permute-start.2 = (f32[4,16,128]{2,1,0:T(8,128)S(1)}, f32[4,16,128]{2,1,0:T(8,128)S(1)}, u32[]{:S(2)}, u32[]{:S(2)}) collective-permute-start(f32[4,16,128]{2,1,0:T(8,128)S(1)} %copy-done.14), channel_id=1, source_target_pairs={{4,5},{5,6},{6,7},{7,4},{8,9},{9,10},{10,11},{11,8},{12,13},{13,14... | collective-permute-start | bytes 98312 | tf_op jit(solution)/shard_map/ppermute | solution.py:934
  59.0 3.3 %collective-permute-start.3 = (f32[4,16,128]{2,1,0:T(8,128)S(1)}, f32[4,16,128]{2,1,0:T(8,128)S(1)}, u32[]{:S(2)}, u32[]{:S(2)}) collective-permute-start(f32[4,16,128]{2,1,0:T(8,128)S(1)} %copy-done.13), channel_id=1, source_target_pairs={{5,4},{6,5},{7,6},{4,7},{9,8},{10,9},{11,10},{8,11},{13,12},{14,13... | collective-permute-start | bytes 98312 | tf_op jit(solution)/shard_map/ppermute | solution.py:935
  62.4 3.3 %collective-permute-done.3.east = f32[4,16,128]{2,1,0:T(8,128)S(1)} collective-permute-done((f32[4,16,128]{2,1,0:T(8,128)S(1)}, f32[4,16,128]{2,1,0:T(8,128)S(1)}, u32[]{:S(2)}, u32[]{:S(2)}) %collective-permute-start.3) | collective-permute-done | bytes 32800 | tf_op jit(solution)/shard_map/ppermute | solution.py:935
  65.8 8.8 %collective-permute-done.8 = f32[2,1600,128]{2,1,0:T(8,128)S(1)} collective-permute-done((f32[2,1600,128]{2,1,0:T(8,128)}, f32[2,1600,128]{2,1,0:T(8,128)S(1)}, u32[]{:S(2)}, u32[]{:S(2)}) %collective-permute-start.8) | collective-permute-done | bytes 1638432 | tf_op jit(solution)/shard_map/ppermute | solution.py:805
  75.4 2.4 %fusion = f32[2496,128]{1,0:T(8,128)S(1)} fusion(f32[2,2496,128]{2,1,0:T(8,128)S(1)} %collective-permute-done.4, f32[2,2496,128]{2,1,0:T(8,128)} %get-tuple-element.24), kind=kLoop, calls=%fused_computation.1 | loop fusion | flops 319488 | bytes 3833856 | tf_op jit(solution)/shard_map/add | solution.py:834
  77.8 2.4 %collective-permute-start.5 = (f32[2496,128]{1,0:T(8,128)S(1)}, f32[2496,128]{1,0:T(8,128)S(1)}, u32[]{:S(2)}, u32[]{:S(2)}) collective-permute-start(f32[2496,128]{1,0:T(8,128)S(1)} %fusion), channel_id=1, source_target_pairs={{0,2},{1,3},{2,0},{3,1},{28,30},{29,31},{30,28},{31,29},{4,5},{5,4... | collective-permute-start | bytes 3833864 | tf_op jit(solution)/shard_map/ppermute | solution.py:796
  80.5 1.7 collective-permute-start.13
  82.2 15.2 %collective-permute-done.5 = f32[2496,128]{1,0:T(8,128)S(1)} collective-permute-done((f32[2496,128]{1,0:T(8,128)S(1)}, f32[2496,128]{1,0:T(8,128)S(1)}, u32[]{:S(2)}, u32[]{:S(2)}) %collective-permute-start.5) | collective-permute-done | bytes 1277984 | tf_op jit(solution)/shard_map/ppermute | solution.py:796
  97.6 2.7 %collective-permute-start.7 = (f32[2496,128]{1,0:T(8,128)S(1)}, f32[2496,128]{1,0:T(8,128)S(1)}, u32[]{:S(2)}, u32[]{:S(2)}) collective-permute-start(f32[2496,128]{1,0:T(8,128)S(1)} %fusion.2.refs_8_), channel_id=1, source_target_pairs={{0,2},{1,3},{2,0},{3,1},{28,30},{29,31},{30,28},{31,29},{4,5},{5,4... | collective-permute-start | bytes 3833864 | tf_op jit(solution)/shard_map/ppermute | solution.py:796
  100.3 1.3 collective-permute-start.12
  101.6 1.3 collective-permute-start.14
  102.9 1.6 collective-permute-start.16
  104.5 1.6 collective-permute-start.18
  106.1 8.5 %collective-permute-done.12.refs_12_ = f32[1600,128]{1,0:T(8,128)} collective-permute-done((f32[1600,128]{1,0:T(8,128)S(1)}, f32[1600,128]{1,0:T(8,128)}, u32[]{:S(2)}, u32[]{:S(2)}) %collective-permute-start.12) | collective-permute-done | bytes 819232 | tf_op jit(solution)/shard_map/ppermute | solution.py:805
  114.6 2.8 %collective-permute-start.6 = (f32[2496,128]{1,0:T(8,128)S(1)}, f32[2496,128]{1,0:T(8,128)}, u32[]{:S(2)}, u32[]{:S(2)}) collective-permute-start(f32[2496,128]{1,0:T(8,128)S(1)} %fusion.2.refs_8_), channel_id=1, source_target_pairs={{0,1},{1,0},{2,3},{3,2},{28,29},{29,28},{30,31},{31,30},{4,6},{5,7... | collective-permute-start | bytes 3833864 | tf_op jit(solution)/shard_map/ppermute | solution.py:796
  117.4 13.0 %collective-permute-done.7.refs_10_ = f32[2496,128]{1,0:T(8,128)S(1)} collective-permute-done((f32[2496,128]{1,0:T(8,128)S(1)}, f32[2496,128]{1,0:T(8,128)S(1)}, u32[]{:S(2)}, u32[]{:S(2)}) %collective-permute-start.7) | collective-permute-done | bytes 1277984 | tf_op jit(solution)/shard_map/ppermute | solution.py:796
  130.5 1.9 collective-permute-start.15
  132.5 1.3 collective-permute-start.17
  133.8 1.3 collective-permute-start.19
  136.3 10.6 %collective-permute-done.17.refs_13_ = f32[1600,128]{1,0:T(8,128)S(1)} collective-permute-done((f32[1600,128]{1,0:T(8,128)}, f32[1600,128]{1,0:T(8,128)S(1)}, u32[]{:S(2)}, u32[]{:S(2)}) %collective-permute-start.17) | collective-permute-done | bytes 819232 | tf_op jit(solution)/shard_map/ppermute | solution.py:805
  146.9 8.9 %collective-permute-done.19.refs_15_ = f32[1600,128]{1,0:T(8,128)} collective-permute-done((f32[1600,128]{1,0:T(8,128)}, f32[1600,128]{1,0:T(8,128)}, u32[]{:S(2)}, u32[]{:S(2)}) %collective-permute-start.19) | collective-permute-done | bytes 819232 | tf_op jit(solution)/shard_map/ppermute | solution.py:805
  155.8 1.2 broadcast_in_dim.35.cuts
  157.0 37.6 %inverse_and_substep.1 = (f32[2,90,16,720]{3,2,1,0:T(8,128)}, f32[90,16,720]{2,1,0:T(8,128)}, f32[90,16,720]{2,1,0:T(8,128)}) custom-call(s32[11]{0:T(128)} %stack.58.scal, f32[540]{0:T(1024)} %concatenate.3.coef, f32[4,16,128]{2,1,0:T(8,128)} %copy-done.8, f32[4,16,128]{2,1,0:T(8,128)} %copy-done.9, f32[4,16,720]{2,1,0:T(8,128)} %copy-done.4, ...), custom_call_target="tpu_custom_call" | custom-call | flops 9286189056 | bytes 40000000 | tf_op jit(solution)/shard_map/inverse_and_substep/pallas_call | solution.py:762
  (64 shorter events, 7.0 us)
Async XLA Ops:
  2.4 10.9 %collective-permute-start = (f32[4,16,720]{2,1,0:T(8,128)S(1)}, f32[4,16,720]{2,1,0:T(8,128)S(1)}, u32[]{:S(2)}, u32[]{:S(2)}) collective-permute-start(f32[4,16,720]{2,1,0:T(8,128)S(1)} %pad_maximum_fusion), channel_id=1, source_target_pairs={{0,4},{1,5},{2,6},{3,7},{4,8},{5,9},{6,10},{7,11},{8,12},{9,13},{1... | collective-permute-start | bytes 552968 | tf_op jit(solution)/shard_map/ppermute | solution.py:904
  4.4 8.9 %collective-permute-start.1 = (f32[4,16,720]{2,1,0:T(8,128)S(1)}, f32[4,16,720]{2,1,0:T(8,128)S(1)}, u32[]{:S(2)}, u32[]{:S(2)}) collective-permute-start(f32[4,16,720]{2,1,0:T(8,128)S(1)} %pad_maximum_fusion.1), channel_id=1, source_target_pairs={{4,0},{5,1},{6,2},{7,3},{8,4},{9,5},{10,6},{11,7},{12,8},{13,9},{1... | collective-permute-start | bytes 552968 | tf_op jit(solution)/shard_map/ppermute | solution.py:905
  28.0 27.7 %collective-permute-start.9 = (f32[2,1600,128]{2,1,0:T(8,128)}, f32[2,1600,128]{2,1,0:T(8,128)}, u32[]{:S(2)}, u32[]{:S(2)}) collective-permute-start(f32[2,1600,128]{2,1,0:T(8,128)} %get-tuple-element.26), channel_id=1, source_target_pairs={{4,12},{5,13},{6,14},{7,15},{24,16},{25,17},{26,18},{27,19}} | collective-permute-start | bytes 4915208 | tf_op jit(solution)/shard_map/ppermute | solution.py:805
  30.5 44.9 %collective-permute-start.4 = (f32[2,2496,128]{2,1,0:T(8,128)}, f32[2,2496,128]{2,1,0:T(8,128)S(1)}, u32[]{:S(2)}, u32[]{:S(2)}) collective-permute-start(f32[2,2496,128]{2,1,0:T(8,128)} %get-tuple-element.17._), channel_id=1, source_target_pairs={{0,1},{1,0},{2,3},{3,2},{28,29},{29,28},{30,31},{31,30},{4,6},{5,7... | collective-permute-start | bytes 7667720 | tf_op jit(solution)/shard_map/ppermute | solution.py:796
  40.5 16.0 %copy-start.14 = (f32[4,16,128]{2,1,0:T(8,128)S(1)}, f32[4,16,128]{2,1,0:T(8,128)}, u32[]{:S(2)}) copy-start(f32[4,16,128]{2,1,0:T(8,128)} %get-tuple-element.21) | copy-start | bytes 98308
  40.5 18.5 %copy-start.13 = (f32[4,16,128]{2,1,0:T(8,128)S(1)}, f32[4,16,128]{2,1,0:T(8,128)}, u32[]{:S(2)}) copy-start(f32[4,16,128]{2,1,0:T(8,128)} %get-tuple-element.18) | copy-start | bytes 98308
  54.3 20.2 %collective-permute-start.8 = (f32[2,1600,128]{2,1,0:T(8,128)}, f32[2,1600,128]{2,1,0:T(8,128)S(1)}, u32[]{:S(2)}, u32[]{:S(2)}) collective-permute-start(f32[2,1600,128]{2,1,0:T(8,128)} %get-tuple-element.25), channel_id=1, source_target_pairs={{4,12},{5,13},{6,14},{7,15},{24,16},{25,17},{26,18},{27,19}} | collective-permute-start | bytes 4915208 | tf_op jit(solution)/shard_map/ppermute | solution.py:805
  55.7 18.8 %collective-permute-start.10 = (f32[2,1600,128]{2,1,0:T(8,128)}, f32[2,1600,128]{2,1,0:T(8,128)S(1)}, u32[]{:S(2)}, u32[]{:S(2)}) collective-permute-start(f32[2,1600,128]{2,1,0:T(8,128)} %collective-permute-done.9), channel_id=1, source_target_pairs={{12,14},{13,15},{14,12},{15,13},{16,18},{17,19},{18,16},{19,17}} | collective-permute-start | bytes 4915208 | tf_op jit(solution)/shard_map/ppermute | solution.py:796
  56.5 5.9 %collective-permute-start.2 = (f32[4,16,128]{2,1,0:T(8,128)S(1)}, f32[4,16,128]{2,1,0:T(8,128)S(1)}, u32[]{:S(2)}, u32[]{:S(2)}) collective-permute-start(f32[4,16,128]{2,1,0:T(8,128)S(1)} %copy-done.14), channel_id=1, source_target_pairs={{4,5},{5,6},{6,7},{7,4},{8,9},{9,10},{10,11},{11,8},{12,13},{13,14... | collective-permute-start | bytes 98312 | tf_op jit(solution)/shard_map/ppermute | solution.py:934
  59.0 6.7 %collective-permute-start.3 = (f32[4,16,128]{2,1,0:T(8,128)S(1)}, f32[4,16,128]{2,1,0:T(8,128)S(1)}, u32[]{:S(2)}, u32[]{:S(2)}) collective-permute-start(f32[4,16,128]{2,1,0:T(8,128)S(1)} %copy-done.13), channel_id=1, source_target_pairs={{5,4},{6,5},{7,6},{4,7},{9,8},{10,9},{11,10},{8,11},{13,12},{14,13... | collective-permute-start | bytes 98312 | tf_op jit(solution)/shard_map/ppermute | solution.py:935
  62.4 15.4 %copy-start.8 = (f32[4,16,128]{2,1,0:T(8,128)}, f32[4,16,128]{2,1,0:T(8,128)S(1)}, u32[]{:S(2)}) copy-start(f32[4,16,128]{2,1,0:T(8,128)S(1)} %collective-permute-done.2.west) | copy-start | bytes 98308
  65.7 12.1 %copy-start.9 = (f32[4,16,128]{2,1,0:T(8,128)}, f32[4,16,128]{2,1,0:T(8,128)S(1)}, u32[]{:S(2)}) copy-start(f32[4,16,128]{2,1,0:T(8,128)S(1)} %collective-permute-done.3.east) | copy-start | bytes 98308
  74.7 5.7 %collective-permute-start.11 = (f32[1600,128]{1,0:T(8,128)S(1)}, f32[1600,128]{1,0:T(8,128)S(1)}, u32[]{:S(2)}, u32[]{:S(2)}) collective-permute-start(f32[1600,128]{1,0:T(8,128)S(1)} %fusion.3), channel_id=1, source_target_pairs={{12,13},{13,12},{14,15},{15,14},{16,17},{17,16},{18,19},{19,18}} | collective-permute-start | bytes 2457608 | tf_op jit(solution)/shard_map/ppermute | solution.py:796
  75.4 22.0 %copy-start.3 = (f32[2,2496,128]{2,1,0:T(8,128)S(1)}, f32[2,2496,128]{2,1,0:T(8,128)}, u32[]{:S(2)}) copy-start(f32[2,2496,128]{2,1,0:T(8,128)} %get-tuple-element.24) | copy-start | bytes 7667716
  77.8 19.5 %collective-permute-start.5 = (f32[2496,128]{1,0:T(8,128)S(1)}, f32[2496,128]{1,0:T(8,128)S(1)}, u32[]{:S(2)}, u32[]{:S(2)}) collective-permute-start(f32[2496,128]{1,0:T(8,128)S(1)} %fusion), channel_id=1, source_target_pairs={{0,2},{1,3},{2,0},{3,1},{28,30},{29,31},{30,28},{31,29},{4,5},{5,4... | collective-permute-start | bytes 3833864 | tf_op jit(solution)/shard_map/ppermute | solution.py:796
  80.3 17.1 %copy-start.2 = (f32[2,2496,128]{2,1,0:T(8,128)S(1)}, f32[2,2496,128]{2,1,0:T(8,128)}, u32[]{:S(2)}) copy-start(f32[2,2496,128]{2,1,0:T(8,128)} %copy-done.1) | copy-start | bytes 7667716
  80.4 52.0 %copy-start.12 = (s32[2,2,92]{2,1,0:T(2,128)S(1)}, s32[2,2,92]{2,1,0:T(2,128)}, u32[]{:S(2)}) copy-start(s32[2,2,92]{2,1,0:T(2,128)} %constant.88.clone) | copy-start | bytes 4420
  80.5 52.0 %copy-start.11 = (s32[240]{0:T(256)S(1)}, s32[240]{0:T(256)}, u32[]{:S(2)}) copy-start(s32[240]{0:T(256)} %param.14) | copy-start | bytes 2884
  80.5 54.6 %copy-start.10 = (s32[240]{0:T(256)S(1)}, s32[240]{0:T(256)}, u32[]{:S(2)}) copy-start(s32[240]{0:T(256)} %param.13) | copy-start | bytes 2884
  80.5 21.1 %collective-permute-start.13 = (f32[1600,128]{1,0:T(8,128)S(1)}, f32[1600,128]{1,0:T(8,128)}, u32[]{:S(2)}, u32[]{:S(2)}) collective-permute-start(f32[1600,128]{1,0:T(8,128)S(1)} %fusion.5), channel_id=1, source_target_pairs={{12,13},{13,12},{14,15},{15,14},{16,17},{17,16},{18,19},{19,18}} | collective-permute-start | bytes 2457608 | tf_op jit(solution)/shard_map/ppermute | solution.py:796
  97.6 59.4 %copy-start = (f32[2496,128]{1,0:T(8,128)}, f32[2496,128]{1,0:T(8,128)S(1)}, u32[]{:S(2)}) copy-start(f32[2496,128]{1,0:T(8,128)S(1)} %fusion.2.refs_8_) | copy-start | bytes 3833860
  97.6 32.9 %collective-permute-start.7 = (f32[2496,128]{1,0:T(8,128)S(1)}, f32[2496,128]{1,0:T(8,128)S(1)}, u32[]{:S(2)}, u32[]{:S(2)}) collective-permute-start(f32[2496,128]{1,0:T(8,128)S(1)} %fusion.2.refs_8_), channel_id=1, source_target_pairs={{0,2},{1,3},{2,0},{3,1},{28,30},{29,31},{30,28},{31,29},{4,5},{5,4... | collective-permute-start | bytes 3833864 | tf_op jit(solution)/shard_map/ppermute | solution.py:796
  100.3 14.3 %collective-permute-start.12 = (f32[1600,128]{1,0:T(8,128)S(1)}, f32[1600,128]{1,0:T(8,128)}, u32[]{:S(2)}, u32[]{:S(2)}) collective-permute-start(f32[1600,128]{1,0:T(8,128)S(1)} %fusion.5), channel_id=1, source_target_pairs={{12,4},{13,5},{14,6},{15,7},{16,24},{17,25},{18,26},{19,27}} | collective-permute-start | bytes 2457608 | tf_op jit(solution)/shard_map/ppermute | solution.py:805
  101.6 28.9 %collective-permute-start.14 = (f32[1600,128]{1,0:T(8,128)}, f32[1600,128]{1,0:T(8,128)}, u32[]{:S(2)}, u32[]{:S(2)}) collective-permute-start(f32[1600,128]{1,0:T(8,128)} %collective-permute-done.13), channel_id=1, source_target_pairs={{12,4},{13,5},{14,6},{15,7},{16,24},{17,25},{18,26},{19,27}} | collective-permute-start | bytes 2457608 | tf_op jit(solution)/shard_map/ppermute | solution.py:805
  102.9 29.6 %collective-permute-start.16 = (f32[1600,128]{1,0:T(8,128)S(1)}, f32[1600,128]{1,0:T(8,128)}, u32[]{:S(2)}, u32[]{:S(2)}) collective-permute-start(f32[1600,128]{1,0:T(8,128)S(1)} %fusion.5), channel_id=1, source_target_pairs={{12,14},{13,15},{14,12},{15,13},{16,18},{17,19},{18,16},{19,17}} | collective-permute-start | bytes 2457608 | tf_op jit(solution)/shard_map/ppermute | solution.py:796
  104.5 29.3 %collective-permute-start.18 = (f32[1600,128]{1,0:T(8,128)}, f32[1600,128]{1,0:T(8,128)}, u32[]{:S(2)}, u32[]{:S(2)}) collective-permute-start(f32[1600,128]{1,0:T(8,128)} %collective-permute-done.13), channel_id=1, source_target_pairs={{12,14},{13,15},{14,12},{15,13},{16,18},{17,19},{18,16},{19,17}} | collective-permute-start | bytes 2457608 | tf_op jit(solution)/shard_map/ppermute | solution.py:796
  114.6 21.7 %collective-permute-start.6 = (f32[2496,128]{1,0:T(8,128)S(1)}, f32[2496,128]{1,0:T(8,128)}, u32[]{:S(2)}, u32[]{:S(2)}) collective-permute-start(f32[2496,128]{1,0:T(8,128)S(1)} %fusion.2.refs_8_), channel_id=1, source_target_pairs={{0,1},{1,0},{2,3},{3,2},{28,29},{29,28},{30,31},{31,30},{4,6},{5,7... | collective-permute-start | bytes 3833864 | tf_op jit(solution)/shard_map/ppermute | solution.py:796
  130.5 26.5 %copy-start.6 = (f32[2496,128]{1,0:T(8,128)}, f32[2496,128]{1,0:T(8,128)S(1)}, u32[]{:S(2)}) copy-start(f32[2496,128]{1,0:T(8,128)S(1)} %collective-permute-done.7.refs_10_) | copy-start | bytes 3833860
  130.5 25.3 %collective-permute-start.15 = (f32[2496,128]{1,0:T(8,128)S(1)}, f32[2496,128]{1,0:T(8,128)}, u32[]{:S(2)}, u32[]{:S(2)}) collective-permute-start(f32[2496,128]{1,0:T(8,128)S(1)} %collective-permute-done.7.refs_10_), channel_id=1, source_target_pairs={{0,1},{1,0},{2,3},{3,2},{28,29},{29,28},{30,31},{31,30},{4,6},{5,7... | collective-permute-start | bytes 3833864 | tf_op jit(solution)/shard_map/ppermute | solution.py:796
  132.5 14.4 %collective-permute-start.17 = (f32[1600,128]{1,0:T(8,128)}, f32[1600,128]{1,0:T(8,128)S(1)}, u32[]{:S(2)}, u32[]{:S(2)}) collective-permute-start(f32[1600,128]{1,0:T(8,128)} %collective-permute-done.16), channel_id=1, source_target_pairs={{12,4},{13,5},{14,6},{15,7},{16,24},{17,25},{18,26},{19,27}} | collective-permute-start | bytes 2457608 | tf_op jit(solution)/shard_map/ppermute | solution.py:805
  133.8 22.0 %collective-permute-start.19 = (f32[1600,128]{1,0:T(8,128)}, f32[1600,128]{1,0:T(8,128)}, u32[]{:S(2)}, u32[]{:S(2)}) collective-permute-start(f32[1600,128]{1,0:T(8,128)} %collective-permute-done.18), channel_id=1, source_target_pairs={{12,4},{13,5},{14,6},{15,7},{16,24},{17,25},{18,26},{19,27}} | collective-permute-start | bytes 2457608 | tf_op jit(solution)/shard_map/ppermute | solution.py:805
  146.9 10.1 %copy-start.7 = (f32[1600,128]{1,0:T(8,128)}, f32[1600,128]{1,0:T(8,128)S(1)}, u32[]{:S(2)}) copy-start(f32[1600,128]{1,0:T(8,128)S(1)} %collective-permute-done.17.refs_13_) | copy-start | bytes 2457604
  (3 other events, 3.8 us)
